TPU v7x, 32 devices: a whole 2x2x4 slice. The times are simulated.
32 devices in a mesh: seq: 4 (over y, x), tok: 8 (over z, core).
Axes of the slice: x: 2, y: 2, z: 4, core: 2. Of those that a mesh axis runs over, the one named last changes fastest.
Arguments:
- tokens: bfloat16 [4, 2048, 2048], P('seq', 'tok'), may hold values from -6 to 6
- source_ids: int32 [4], P('seq'), may hold values from 0 to 7
- loss_weights: float32 [8], replicated, may hold values from 0.5 to 2
- grad_output: bfloat16 [4, 2048, 2048], P('seq', 'tok'), may hold values from -6 to 6
- first_gain: bfloat16 [2048], P(('seq', 'tok')), may hold values from 0.5 to 1.5
- input_weight: bfloat16 [2048, 2560], P(('seq', 'tok')), may hold values from -0.125 to 0.125
- gelu_weight: bfloat16 [2048, 2560], P(('seq', 'tok')), may hold values from -0.125 to 0.125
- conv_weight: bfloat16 [2560, 4], P(('seq', 'tok')), may hold values from -3 to 3
- conv_bias: bfloat16 [2560], P(('seq', 'tok')), may hold values from -3 to 3
- decay_gate: bfloat16 [2560, 256], P(('seq', 'tok')), may hold values from -0.375 to 0.375
- decay_bias: bfloat16 [2560], P(('seq', 'tok')), may hold values from -3 to 3
- input_gate: bfloat16 [2560, 256], P(('seq', 'tok')), may hold values from -0.375 to 0.375
- input_bias: bfloat16 [2560], P(('seq', 'tok')), may hold values from -3 to 3
- decay_param: bfloat16 [2560], P(('seq', 'tok')), may hold values from -13 to -4
- output_weight: bfloat16 [2560, 2048], P(('seq', 'tok')), may hold values from -0.3125 to 0.3125
- second_gain: bfloat16 [2048], P(('seq', 'tok')), may hold values from 0.5 to 1.5
- gate_weight: bfloat16 [2048, 6144], P(('seq', 'tok')), may hold values from -0.125 to 0.125
- up_weight: bfloat16 [2048, 6144], P(('seq', 'tok')), may hold values from -0.125 to 0.125
- down_weight: bfloat16 [6144, 2048], P(('seq', 'tok')), may hold values from -0.15625 to 0.15625
Outputs:
- block_out: bfloat16 [4, 2048, 2048], P('seq', 'tok')
- grad_tokens: float32 [4, 2048, 2048], P('seq', 'tok')
- grad_first_gain: float32 [2048], P(('seq', 'tok'))
- grad_input_weight: float32 [2048, 2560], P(('seq', 'tok'))
- grad_gelu_weight: float32 [2048, 2560], P(('seq', 'tok'))
- grad_conv_weight: float32 [2560, 4], P(('seq', 'tok'))
- grad_conv_bias: float32 [2560], P(('seq', 'tok'))
- grad_decay_gate: float32 [2560, 256], P(('seq', 'tok'))
- grad_decay_bias: float32 [2560], P(('seq', 'tok'))
- grad_input_gate: float32 [2560, 256], P(('seq', 'tok'))
- grad_input_bias: float32 [2560], P(('seq', 'tok'))
- grad_decay_param: float32 [2560], P(('seq', 'tok'))
- grad_output_weight: float32 [2560, 2048], P(('seq', 'tok'))
- grad_second_gain: float32 [2048], P(('seq', 'tok'))
- grad_gate_weight: float32 [2048, 6144], P(('seq', 'tok'))
- grad_up_weight: float32 [2048, 6144], P(('seq', 'tok'))
- grad_down_weight: float32 [6144, 2048], P(('seq', 'tok'))
Inputs may be any that keep to these rules, and one draw needn't show every extreme that they name: `source_ids`: each sequence's source, which selects its entry of loss_weights.
All inputs are finite; a program needn't handle non-finite values.
Results may differ from a plain program's by a relative error of at most 0.0094.
Values may be sent and summed in bfloat16 or wider, within the bound.
A program may use at most 448 MiB of HBM per device.

v0:
```python
import jax
import jax.numpy as jnp
from jax import lax
from jax.sharding import PartitionSpec as P

R = 2560
BW = 256
CONV = 4
HEADS = 10


eps = 1e-06


def from_behind(block, axis, distance):
    devices = range(lax.axis_size(axis))
    route = [(i - distance, i) for i in devices if i - distance in devices]
    return lax.ppermute(block, axis, route)


def entering(value, axis, join, neutral, backward):
    count, mine = (lax.axis_size(axis), lax.axis_index(axis))
    pieces = jax.tree.map(lambda part: lax.all_gather(part, axis), value)
    if backward:
        pieces = jax.tree.map(lambda part: part[::-1], pieces)
        mine = count - 1 - mine
    total = jax.tree.map(
        lambda part, zero: jnp.full_like(part, 0) + jnp.asarray(zero, part.dtype), value, neutral
    )

    def turn(position, total):
        longer = join(total, jax.tree.map(lambda part: part[position], pieces))
        return jax.tree.map(lambda new, old: jnp.where(position < mine, new, old), longer, total)

    return lax.fori_loop(0, count - 1, turn, total)


def gelu(value):
    return jax.nn.gelu(value, approximate=True)


def rms_scale(value, gain):
    return value * lax.rsqrt(jnp.mean(value * value, axis=-1, keepdims=True) + eps) * gain


def combine(earlier, later):
    return (earlier[0] * later[0], later[0] * earlier[1] + later[1])


def gelu_product(gate_val, up_val):
    return gelu(gate_val) * up_val


def recur_inputs(gate_pre, input_pre, conv_vals, decay_param):
    decay_log = -8.0 * jax.nn.sigmoid(gate_pre) * jax.nn.softplus(decay_param)
    inject = jnp.sqrt(-jnp.expm1(2.0 * decay_log)) * jax.nn.sigmoid(input_pre) * conv_vals
    return (jnp.exp(decay_log), inject)


def forward_product(left, weight):
    return jnp.dot(left, weight, preferred_element_type=jnp.float32)


def back_product(grad, weight):
    return lax.dot_general(
        grad, weight, (((2,), (1,)), ((), ())), preferred_element_type=jnp.float32
    )


def token_product(left, grad):
    return lax.dot_general(
        left, grad, (((0, 1), (0, 1)), ((), ())), preferred_element_type=jnp.float32
    )


def block_gate(conv_low, weights, bias):
    seqs, length = (conv_low.shape[0], conv_low.shape[1])
    shaped = conv_low.reshape(seqs, length, HEADS, BW)
    result = jnp.einsum(
        "sthi,hij->sthj", shaped, weights.reshape(HEADS, BW, BW), preferred_element_type=jnp.float32
    )
    return result.reshape(seqs, length, R) + bias.astype(jnp.float32)


def block_gate_back(grad_low, weights):
    seqs, length = (grad_low.shape[0], grad_low.shape[1])
    shaped = grad_low.reshape(seqs, length, HEADS, BW)
    result = jnp.einsum(
        "sthj,hij->sthi", shaped, weights.reshape(HEADS, BW, BW), preferred_element_type=jnp.float32
    )
    return result.reshape(seqs, length, R)


def block_gate_weight(conv_low, grad_low):
    seqs, length = (conv_low.shape[0], conv_low.shape[1])
    result = jnp.einsum(
        "sthi,sthj->hij",
        conv_low.reshape(seqs, length, HEADS, BW),
        grad_low.reshape(seqs, length, HEADS, BW),
        preferred_element_type=jnp.float32,
    )
    return result.reshape(R, BW)


def feed_back(normed_rows, cot_rows, gate_val, up_val, hidden, weight_gate, weight_up, weight_down):
    grad_down = token_product(hidden, cot_rows)
    grad_hidden = back_product(cot_rows, weight_down)
    _, hidden_pull = jax.vjp(gelu_product, gate_val, up_val)
    grad_gate_val, grad_up_val = hidden_pull(grad_hidden)
    grad_gate_low = grad_gate_val.astype(jnp.bfloat16)
    grad_up_low = grad_up_val.astype(jnp.bfloat16)
    grad_gate_w = token_product(normed_rows, grad_gate_low)
    grad_up_w = token_product(normed_rows, grad_up_low)
    grad_second = back_product(grad_gate_low, weight_gate) + back_product(grad_up_low, weight_up)
    return (grad_gate_w, grad_up_w, grad_down, grad_second)


def body(
    tokens,
    source_ids,
    loss_weights,
    grad_output,
    first_gain,
    input_weight,
    gelu_weight,
    conv_weight,
    conv_bias,
    decay_gate,
    decay_bias,
    input_gate,
    input_bias,
    decay_param,
    output_weight,
    second_gain,
    gate_weight,
    up_weight,
    down_weight,
):
    seqs, length = (tokens.shape[0], tokens.shape[1])
    (
        gain_one,
        weight_in,
        weight_gelu,
        weight_conv,
        bias_conv,
        weight_decay,
        bias_decay,
        weight_input,
        bias_input,
        param_decay,
        weight_out,
        gain_two,
    ) = (
        lax.all_gather(first_gain, ("seq", "tok"), axis=0, tiled=True),
        lax.all_gather(input_weight, ("seq", "tok"), axis=0, tiled=True),
        lax.all_gather(gelu_weight, ("seq", "tok"), axis=0, tiled=True),
        lax.all_gather(conv_weight, ("seq", "tok"), axis=0, tiled=True),
        lax.all_gather(conv_bias, ("seq", "tok"), axis=0, tiled=True),
        lax.all_gather(decay_gate, ("seq", "tok"), axis=0, tiled=True),
        lax.all_gather(decay_bias, ("seq", "tok"), axis=0, tiled=True),
        lax.all_gather(input_gate, ("seq", "tok"), axis=0, tiled=True),
        lax.all_gather(input_bias, ("seq", "tok"), axis=0, tiled=True),
        lax.all_gather(decay_param, ("seq", "tok"), axis=0, tiled=True),
        lax.all_gather(output_weight, ("seq", "tok"), axis=0, tiled=True),
        lax.all_gather(second_gain, ("seq", "tok"), axis=0, tiled=True),
    )
    inputs = tokens.astype(jnp.float32)
    normed = rms_scale(inputs, gain_one.astype(jnp.float32)).astype(jnp.bfloat16)
    branch_x = forward_product(normed, weight_in).astype(jnp.bfloat16)
    branch_y = forward_product(normed, weight_gelu)
    previous = from_behind(branch_x[:, length - (CONV - 1) :, :], "tok", 1)
    extended = jnp.concatenate([previous, branch_x], axis=1)
    conv_float = weight_conv.astype(jnp.float32)
    conv_out = bias_conv.astype(jnp.float32) + jnp.zeros(branch_x.shape, jnp.float32)
    for offset in range(CONV):
        conv_out = (
            conv_out
            + extended[:, offset : offset + length, :].astype(jnp.float32) * conv_float[:, offset]
        )
    conv_low = conv_out.astype(jnp.bfloat16)
    conv_vals = conv_low.astype(jnp.float32)
    gate_pre = block_gate(conv_low, weight_decay, bias_decay)
    input_pre = block_gate(conv_low, weight_input, bias_input)
    param_float = param_decay.astype(jnp.float32)
    decays, inject = recur_inputs(gate_pre, input_pre, conv_vals, param_float)
    cum_decay, local_state = lax.associative_scan(combine, (decays, inject), axis=1)
    incoming = entering(
        (cum_decay[:, -1, :], local_state[:, -1, :]),
        "tok",
        combine,
        (jnp.ones((seqs, R), jnp.float32), jnp.zeros((seqs, R), jnp.float32)),
        False,
    )[1]
    states = local_state + cum_decay * incoming[:, None, :]
    gated = gelu(branch_y)
    mixed = (states * gated).astype(jnp.bfloat16)
    resid = inputs + forward_product(mixed, weight_out)
    gain_float = gain_two.astype(jnp.float32)
    second_normed = rms_scale(resid, gain_float).astype(jnp.bfloat16)
    sources = lax.broadcasted_iota(jnp.int32, (seqs, loss_weights.shape[0]), 1)
    picked = jnp.sum(jnp.where(source_ids[:, None] == sources, loss_weights[None, :], 0.0), axis=1)
    cotangent = grad_output.astype(jnp.float32) * picked[:, None, None]
    cot_low = cotangent.astype(jnp.bfloat16)
    weight_gate, weight_up, weight_down = (
        lax.all_gather(gate_weight, ("seq", "tok"), axis=0, tiled=True),
        lax.all_gather(up_weight, ("seq", "tok"), axis=0, tiled=True),
        lax.all_gather(down_weight, ("seq", "tok"), axis=0, tiled=True),
    )
    gate_val = forward_product(second_normed, weight_gate)
    up_val = forward_product(second_normed, weight_up)
    hidden = gelu_product(gate_val, up_val).astype(jnp.bfloat16)
    block_out = (resid + forward_product(hidden, weight_down)).astype(jnp.bfloat16)
    weight_gate, weight_up, weight_down = (
        lax.all_gather(gate_weight, ("seq", "tok"), axis=0, tiled=True),
        lax.all_gather(up_weight, ("seq", "tok"), axis=0, tiled=True),
        lax.all_gather(down_weight, ("seq", "tok"), axis=0, tiled=True),
    )
    grad_gate_w, grad_up_w, grad_down, grad_second = feed_back(
        second_normed, cot_low, gate_val, up_val, hidden, weight_gate, weight_up, weight_down
    )
    grad_gate_out, grad_up_out, grad_down_out = (
        lax.psum_scatter(grad_gate_w, ("seq", "tok"), scatter_dimension=0, tiled=True),
        lax.psum_scatter(grad_up_w, ("seq", "tok"), scatter_dimension=0, tiled=True),
        lax.psum_scatter(grad_down, ("seq", "tok"), scatter_dimension=0, tiled=True),
    )
    _, second_pull = jax.vjp(rms_scale, resid, gain_float)
    grad_resid_norm, grad_gain_two = second_pull(grad_second)
    grad_resid = cotangent + grad_resid_norm
    (
        gain_one,
        weight_in,
        weight_gelu,
        weight_conv,
        bias_conv,
        weight_decay,
        bias_decay,
        weight_input,
        bias_input,
        param_decay,
        weight_out,
        gain_two,
    ) = (
        lax.all_gather(first_gain, ("seq", "tok"), axis=0, tiled=True),
        lax.all_gather(input_weight, ("seq", "tok"), axis=0, tiled=True),
        lax.all_gather(gelu_weight, ("seq", "tok"), axis=0, tiled=True),
        lax.all_gather(conv_weight, ("seq", "tok"), axis=0, tiled=True),
        lax.all_gather(conv_bias, ("seq", "tok"), axis=0, tiled=True),
        lax.all_gather(decay_gate, ("seq", "tok"), axis=0, tiled=True),
        lax.all_gather(decay_bias, ("seq", "tok"), axis=0, tiled=True),
        lax.all_gather(input_gate, ("seq", "tok"), axis=0, tiled=True),
        lax.all_gather(input_bias, ("seq", "tok"), axis=0, tiled=True),
        lax.all_gather(decay_param, ("seq", "tok"), axis=0, tiled=True),
        lax.all_gather(output_weight, ("seq", "tok"), axis=0, tiled=True),
        lax.all_gather(second_gain, ("seq", "tok"), axis=0, tiled=True),
    )
    conv_float = weight_conv.astype(jnp.float32)
    param_float = param_decay.astype(jnp.float32)
    resid_low = grad_resid.astype(jnp.bfloat16)
    grad_out_w = token_product(mixed, resid_low)
    grad_mixed = back_product(resid_low, weight_out)
    grad_local = grad_mixed * gated
    _, gelu_pull = jax.vjp(gelu, branch_y)
    grad_y_low = gelu_pull(grad_mixed * states)[0].astype(jnp.bfloat16)
    next_decay = jnp.concatenate([decays[:, 1:, :], jnp.ones((seqs, 1, R), jnp.float32)], axis=1)
    reach, local_adjoint = lax.associative_scan(
        combine, (next_decay, grad_local), axis=1, reverse=True
    )
    first_adjoint = decays[:, 0, :] * local_adjoint[:, 0, :]
    carry_in = entering(
        (cum_decay[:, -1, :], first_adjoint),
        "tok",
        combine,
        (jnp.ones((seqs, R), jnp.float32), jnp.zeros((seqs, R), jnp.float32)),
        True,
    )[1]
    grad_states = local_adjoint + reach * carry_in[:, None, :]
    prev_states = jnp.concatenate([incoming[:, None, :], states[:, :-1, :]], axis=1)
    _, recur_pull = jax.vjp(recur_inputs, gate_pre, input_pre, conv_vals, param_float)
    grad_gate_pre, grad_input_pre, grad_conv, grad_param = recur_pull(
        (grad_states * prev_states, grad_states)
    )
    gate_low = grad_gate_pre.astype(jnp.bfloat16)
    input_low = grad_input_pre.astype(jnp.bfloat16)
    grad_decay_b = jnp.sum(gate_low.astype(jnp.float32), axis=(0, 1))
    grad_input_b = jnp.sum(input_low.astype(jnp.float32), axis=(0, 1))
    grad_decay_w = block_gate_weight(conv_low, gate_low)
    grad_input_w = block_gate_weight(conv_low, input_low)
    grad_conv = (
        grad_conv
        + block_gate_back(gate_low, weight_decay)
        + block_gate_back(input_low, weight_input)
    )
    grad_conv_b = jnp.sum(grad_conv, axis=(0, 1))
    tap_grads = []
    grad_extended = jnp.zeros((seqs, length + CONV - 1, R), jnp.float32)
    for offset in range(CONV):
        window = extended[:, offset : offset + length, :].astype(jnp.float32)
        tap_grads.append(jnp.sum(grad_conv * window, axis=(0, 1)))
        grad_extended = grad_extended + jnp.pad(
            grad_conv * conv_float[:, offset], ((0, 0), (offset, CONV - 1 - offset), (0, 0))
        )
    grad_conv_w = jnp.stack(tap_grads, axis=1)
    returned_rim = from_behind(grad_extended[:, : CONV - 1, :], "tok", -1)
    grad_branch_x = grad_extended[:, CONV - 1 :, :] + jnp.pad(
        returned_rim, ((0, 0), (length - (CONV - 1), 0), (0, 0))
    )
    grad_x_low = grad_branch_x.astype(jnp.bfloat16)
    grad_in_w = token_product(normed, grad_x_low)
    grad_gelu_w = token_product(normed, grad_y_low)
    grad_normed = back_product(grad_x_low, weight_in) + back_product(grad_y_low, weight_gelu)
    _, first_pull = jax.vjp(rms_scale, inputs, gain_one.astype(jnp.float32))
    grad_inputs_norm, grad_gain_one = first_pull(grad_normed)
    grad_tokens = grad_resid + grad_inputs_norm
    recur_scattered = (
        lax.psum_scatter(grad_gain_one, ("seq", "tok"), scatter_dimension=0, tiled=True),
        lax.psum_scatter(grad_in_w, ("seq", "tok"), scatter_dimension=0, tiled=True),
        lax.psum_scatter(grad_gelu_w, ("seq", "tok"), scatter_dimension=0, tiled=True),
        lax.psum_scatter(grad_conv_w, ("seq", "tok"), scatter_dimension=0, tiled=True),
        lax.psum_scatter(grad_conv_b, ("seq", "tok"), scatter_dimension=0, tiled=True),
        lax.psum_scatter(grad_decay_w, ("seq", "tok"), scatter_dimension=0, tiled=True),
        lax.psum_scatter(grad_decay_b, ("seq", "tok"), scatter_dimension=0, tiled=True),
        lax.psum_scatter(grad_input_w, ("seq", "tok"), scatter_dimension=0, tiled=True),
        lax.psum_scatter(grad_input_b, ("seq", "tok"), scatter_dimension=0, tiled=True),
        lax.psum_scatter(grad_param, ("seq", "tok"), scatter_dimension=0, tiled=True),
        lax.psum_scatter(grad_out_w, ("seq", "tok"), scatter_dimension=0, tiled=True),
        lax.psum_scatter(grad_gain_two, ("seq", "tok"), scatter_dimension=0, tiled=True),
    )
    return (
        block_out,
        grad_tokens,
        recur_scattered[0],
        recur_scattered[1],
        recur_scattered[2],
        recur_scattered[3],
        recur_scattered[4],
        recur_scattered[5],
        recur_scattered[6],
        recur_scattered[7],
        recur_scattered[8],
        recur_scattered[9],
        recur_scattered[10],
        recur_scattered[11],
        grad_gate_out,
        grad_up_out,
        grad_down_out,
    )


def solution(mesh):
    placed = (
        P("seq", "tok", None),
        P("seq"),
        P(),
        P("seq", "tok", None),
        P(("seq", "tok")),
        P(("seq", "tok"), None),
        P(("seq", "tok"), None),
        P(("seq", "tok"), None),
        P(("seq", "tok")),
        P(("seq", "tok"), None),
        P(("seq", "tok")),
        P(("seq", "tok"), None),
        P(("seq", "tok")),
        P(("seq", "tok")),
        P(("seq", "tok"), None),
        P(("seq", "tok")),
        P(("seq", "tok"), None),
        P(("seq", "tok"), None),
        P(("seq", "tok"), None),
    )
    return jax.shard_map(
        body,
        mesh=mesh,
        in_specs=placed,
        out_specs=(
            P("seq", "tok", None),
            P("seq", "tok", None),
            P(("seq", "tok")),
            P(("seq", "tok"), None),
            P(("seq", "tok"), None),
            P(("seq", "tok"), None),
            P(("seq", "tok")),
            P(("seq", "tok"), None),
            P(("seq", "tok")),
            P(("seq", "tok"), None),
            P(("seq", "tok")),
            P(("seq", "tok")),
            P(("seq", "tok"), None),
            P(("seq", "tok")),
            P(("seq", "tok"), None),
            P(("seq", "tok"), None),
            P(("seq", "tok"), None),
        ),
        check_vma=False,
    )
```

profile of v0, /device:TPU:0, one launch (start us, length us, event | category | flops | bytes accessed | tf_op | source)
XLA Modules:
  0.0 3637.5 jit_solution(10469083971203439702)
XLA Ops:
  14.4 43.2 %all-reduce.84 = (bf16[2560]{0:T(1024)(128)(2,1)S(1)}, bf16[2048]{0:T(1024)(128)(2,1)S(1)}, bf16[2560]{0:T(1024)(128)(2,1)S(1)}, bf16[2560]{0:T(1024)(128)(2,1)S...) all-reduce(bf16[2560]{0:T(1024)(128)(2,1)S(1)} %dynamic-update-slic, ...), channel_id=1, replica_groups=mesh['seq'=4,'tok'=8] {'seq','tok'}, use_global_device_ids=true, to_apply=%add.74 | all-reduce | flops 14336 | bytes 57344
  57.6 40.6 %all-gather = bf16[32,80,4]{1,2,0:T(4,128)(2,1)S(1)} all-gather(bf16[1,80,4]{1,2,0:T(4,128)(2,1)S(1)} %bitcast.237), channel_id=1, replica_groups=mesh['seq'=4,'tok'=8] {'seq','tok'}, dimensions={0}, use_global_device_ids=true | all-gather | bytes 21120 | tf_op jit(solution)/shard_map/all_gather | solution.py:157
  110.1 79.1 %all-gather.16.cloned.1.call-done = bf16[2048,2560]{1,0:T(8,128)(2,1)} async-done(((bf16[64,2560]{1,0:T(8,128)(2,1)}), bf16[2048,2560]{1,0:T(8,128)(2,1)}) %all-gather.16.cloned.1.call-update) | async-done | bytes 10485776 | tf_op jit(solution)/shard_map/all_gather | solution.py:156
  199.8 45.2 %all-gather.12.cloned.1.call-done = bf16[2560,256]{1,0:T(8,128)(2,1)} async-done(((bf16[80,256]{1,0:T(8,128)(2,1)}), bf16[2560,256]{1,0:T(8,128)(2,1)}) %all-gather.12.cloned.1.call-update) | async-done | bytes 1310736 | tf_op jit(solution)/shard_map/all_gather | solution.py:159
  250.5 50.6 %all-gather.14.cloned.1.call-done = bf16[2560,256]{1,0:T(8,128)(2,1)} async-done(((bf16[80,256]{1,0:T(8,128)(2,1)}), bf16[2560,256]{1,0:T(8,128)(2,1)}) %all-gather.14.cloned.1.call-update) | async-done | bytes 1310736 | tf_op jit(solution)/shard_map/all_gather | solution.py:161
  465.1 9.6 pad.233
  477.3 9.1 pad.248
  486.4 9.1 pad.249
  495.5 10.8 slice.622
  506.3 10.8 slice.629
  517.1 10.9 slice.620
  528.9 14.1 all_gather.76
  544.6 14.0 all_gather.77
  578.1 14.2 fusion.127
  592.2 110.0 %all-gather.22.cloned.1.call-done = bf16[2048,6144]{1,0:T(8,128)(2,1)} async-done(((bf16[64,6144]{1,0:T(8,128)(2,1)}), bf16[2048,6144]{1,0:T(8,128)(2,1)}) %all-gather.22.cloned.1.call-update) | async-done | bytes 25165840 | tf_op jit(solution)/shard_map/all_gather | solution.py:206
  702.2 13.5 fusion.128
  715.8 142.3 %all-gather.24.cloned.1.call-done = bf16[6144,2048]{1,0:T(8,128)(2,1)} async-done(((bf16[192,2048]{1,0:T(8,128)(2,1)}), bf16[6144,2048]{1,0:T(8,128)(2,1)}) %all-gather.24.cloned.1.call-update) | async-done | bytes 25165840 | tf_op jit(solution)/shard_map/all_gather | solution.py:207
  858.1 22.4 multiply_convert_fusion
  880.6 13.4 fusion.129
  894.0 15.9 fusion.47
  913.9 10.1 fusion.25
  930.7 10.7 slice.624
  941.4 10.7 slice.626
  1051.5 9.1 pad.265
  1071.3 10.8 slice.682
  1089.6 9.4 pad.264
  1103.4 14.1 all_gather.84
  1123.0 9.1 pad.281
  1140.3 13.2 rev.15
  1153.5 21.0 rev.14
  1207.1 9.9 fusion.112
  1226.2 10.3 fusion.64
  1238.1 8.8 fusion.57
  1254.9 8.9 fusion.78
  1265.0 21.4 fusion.132
  1286.4 21.4 fusion.133
  1309.0 22.2 fusion.68
  1337.1 13.1 fusion.38
  1350.2 8.7 fusion.42
  1358.9 41.7 %all-reduce.83 = (f32[2048]{0:T(1024)S(1)}, f32[2560]{0:T(1024)S(1)}, f32[2560]{0:T(1024)S(1)}, f32[2560]{0:T(1024)S(1)}, f32[2560]{0:T(1024)S(1)}, /*index=5*/f32[2048]{0:T(1024)S(1)}) all-reduce(f32[2048]{0:T(1024)S(1)} %get-tuple-element.248, f32[2560]{0:T(1024)S(1)} %copy-done.86, ...), channel_id=2, replica_groups=mesh['seq'=4,'tok'=8] {'seq','tok'}, use_global_device_ids=true, to_apply=%region_10.11.clone | all-reduce | flops 14336 | bytes 114688
  1409.0 81.0 %reduce-scatter.16.cloned.1.call-done = f32[80,256]{1,0:T(8,128)} async-done(((f32[2560,256]{1,0:T(8,128)}), f32[80,256]{1,0:T(8,128)}) %reduce-scatter.16.cloned.1.call-update) | async-done | bytes 81936 | tf_op jit(solution)/shard_map/reduce_scatter | solution.py:320
  1490.0 137.9 %reduce-scatter.18.cloned.1.call-done = f32[80,256]{1,0:T(8,128)} async-done(((f32[2560,256]{1,0:T(8,128)}), f32[80,256]{1,0:T(8,128)}) %reduce-scatter.18.cloned.1.call-update) | async-done | bytes 81936 | tf_op jit(solution)/shard_map/reduce_scatter | solution.py:322
  1627.9 229.9 %reduce-scatter.20.cloned.1.call-done = f32[80,2048]{1,0:T(8,128)} async-done(((f32[2560,2048]{1,0:T(8,128)}), f32[80,2048]{1,0:T(8,128)}) %reduce-scatter.20.cloned.1.call-update) | async-done | bytes 655376 | tf_op jit(solution)/shard_map/reduce_scatter | solution.py:325
  1857.8 229.8 %reduce-scatter.14.cloned.1.call-done = f32[64,2560]{1,0:T(8,128)} async-done(((f32[2048,2560]{1,0:T(8,128)}), f32[64,2560]{1,0:T(8,128)}) %reduce-scatter.14.cloned.1.call-update) | async-done | bytes 655376 | tf_op jit(solution)/shard_map/reduce_scatter | solution.py:317
  2087.6 229.7 %reduce-scatter.12.cloned.1.call-done = f32[64,2560]{1,0:T(8,128)} async-done(((f32[2048,2560]{1,0:T(8,128)}), f32[64,2560]{1,0:T(8,128)}) %reduce-scatter.12.cloned.1.call-update) | async-done | bytes 655376 | tf_op jit(solution)/shard_map/reduce_scatter | solution.py:316
  2317.3 436.3 %reduce-scatter.22.cloned.1.call-done = f32[64,6144]{1,0:T(8,128)} async-done(((f32[2048,6144]{1,0:T(8,128)}), f32[64,6144]{1,0:T(8,128)}) %reduce-scatter.22.cloned.1.call-update) | async-done | bytes 1572880 | tf_op jit(solution)/shard_map/reduce_scatter | solution.py:222
  2753.6 438.7 %reduce-scatter.24.cloned.1.call-done = f32[64,6144]{1,0:T(8,128)} async-done(((f32[2048,6144]{1,0:T(8,128)}), f32[64,6144]{1,0:T(8,128)}) %reduce-scatter.24.cloned.1.call-update) | async-done | bytes 1572880 | tf_op jit(solution)/shard_map/reduce_scatter | solution.py:223
  3192.3 438.5 %reduce-scatter.26.cloned.1.call-done = f32[192,2048]{1,0:T(8,128)} async-done(((f32[6144,2048]{1,0:T(8,128)}), f32[192,2048]{1,0:T(8,128)}) %reduce-scatter.26.cloned.1.call-update) | async-done | bytes 1572880 | tf_op jit(solution)/shard_map/reduce_scatter | solution.py:224
  (625 shorter events, 440.8 us)
Async XLA Ops:
  7.3 50.3 %copy-start.115 = (bf16[80,4]{0,1:T(4,128)(2,1)S(1)}, bf16[80,4]{0,1:T(4,128)(2,1)}, u32[]{:S(2)}) copy-start(bf16[80,4]{0,1:T(4,128)(2,1)} %param.30) | copy-start | bytes 1924
  7.3 92.3 %copy-start.122 = (f32[8]{0:T(128)S(1)}, f32[8]{0:T(128)}, u32[]{:S(2)}) copy-start(f32[8]{0:T(128)} %param.25) | copy-start | bytes 100
  7.3 93.1 %copy-start.12 = (bf16[1,256,2048]{2,1,0:T(8,128)(2,1)S(1)}, bf16[1,256,2048]{2,1,0:T(8,128)(2,1)}, u32[]{:S(2)}) copy-start(bf16[1,256,2048]{2,1,0:T(8,128)(2,1)} %param.23) | copy-start | bytes 3145732
  7.3 93.5 %all-gather.10.cloned.1.call-start = ((), (), s32[]{:S(2)}) async-start(), calls=%async_computation.9 | async-start | bytes 10813440 | tf_op jit(solution)/shard_map/all_gather | solution.py:155
  8.0 181.2 %all-gather.16.cloned.1.call-start = ((), (), s32[]{:S(2)}) async-start(), calls=%async_computation.12 | async-start | bytes 10813440 | tf_op jit(solution)/shard_map/all_gather | solution.py:156
  8.8 236.2 %all-gather.12.cloned.1.call-start = ((), (), s32[]{:S(2)}) async-start(), calls=%async_computation.10 | async-start | bytes 1351680 | tf_op jit(solution)/shard_map/all_gather | solution.py:159
  9.5 291.6 %all-gather.14.cloned.1.call-start = ((), (), s32[]{:S(2)}) async-start(), calls=%async_computation.11 | async-start | bytes 1351680 | tf_op jit(solution)/shard_map/all_gather | solution.py:161
  10.1 556.8 %all-gather.18.cloned.1.call-start = ((), (), s32[]{:S(2)}) async-start(), calls=%async_computation.13 | async-start | bytes 10813440 | tf_op jit(solution)/shard_map/all_gather | solution.py:164
  10.7 567.4 %all-gather.20.cloned.1.call-start = ((), (), s32[]{:S(2)}) async-start(), calls=%async_computation.14 | async-start | bytes 25952256 | tf_op jit(solution)/shard_map/all_gather | solution.py:205
  11.2 691.0 %all-gather.22.cloned.1.call-start = ((), (), s32[]{:S(2)}) async-start(), calls=%async_computation.15 | async-start | bytes 25952256 | tf_op jit(solution)/shard_map/all_gather | solution.py:206
  12.0 846.1 %all-gather.24.cloned.1.call-start = ((), (), s32[]{:S(2)}) async-start(), calls=%async_computation.16 | async-start | bytes 25952256 | tf_op jit(solution)/shard_map/all_gather | solution.py:207
  12.7 1394.9 %reduce-scatter.28.cloned.1.call-start = ((), (), s32[]{:S(2)}) async-start(), calls=%async_computation.25 | async-start | bytes 1351680
  57.5 50.1 %copy-start.110 = (bf16[2560]{0:T(1024)(128)(2,1)}, bf16[2560]{0:T(1024)(128)(2,1)S(1)}, u32[]{:S(2)}) copy-start(bf16[2560]{0:T(1024)(128)(2,1)S(1)} %get-tuple-element.285) | copy-start | bytes 15364
  57.6 131.6 %copy-start.59 = (f32[2048]{0:T(1024)}, f32[2048]{0:T(1024)S(1)}, u32[]{:S(2)}) copy-start(f32[2048]{0:T(1024)S(1)} %convert_element_type.121) | copy-start | bytes 24580
  98.3 209.8 %copy-start.53 = (f32[2560]{0:T(1024)}, f32[2560]{0:T(1024)S(1)}, u32[]{:S(2)}) copy-start(f32[2560]{0:T(1024)S(1)} %convert_element_type.131) | copy-start | bytes 30724
  98.3 209.8 %copy-start.55 = (f32[2560]{0:T(1024)}, f32[2560]{0:T(1024)S(1)}, u32[]{:S(2)}) copy-start(f32[2560]{0:T(1024)S(1)} %convert_element_type.133) | copy-start | bytes 30724
  100.3 97.3 %copy-start.67 = (f32[2560]{0:T(1024)}, f32[2560]{0:T(1024)S(1)}, u32[]{:S(2)}) copy-start(f32[2560]{0:T(1024)S(1)} %get-tuple-element.255) | copy-start | bytes 30724
  100.3 97.3 %copy-start.69 = (f32[2560]{0:T(1024)}, f32[2560]{0:T(1024)S(1)}, u32[]{:S(2)}) copy-start(f32[2560]{0:T(1024)S(1)} %get-tuple-element.256) | copy-start | bytes 30724
  100.4 97.3 %copy-start.71 = (f32[2560]{0:T(1024)}, f32[2560]{0:T(1024)S(1)}, u32[]{:S(2)}) copy-start(f32[2560]{0:T(1024)S(1)} %get-tuple-element.257) | copy-start | bytes 30724
  100.4 97.3 %copy-start.73 = (f32[2560]{0:T(1024)}, f32[2560]{0:T(1024)S(1)}, u32[]{:S(2)}) copy-start(f32[2560]{0:T(1024)S(1)} %get-tuple-element.258) | copy-start | bytes 30724
  100.7 88.5 %copy-start.82 = (f32[256]{0:T(256)}, f32[256]{0:T(256)S(1)}, u32[]{:S(2)}) copy-start(f32[256]{0:T(256)S(1)} %fusion.102) | copy-start | bytes 3076
  100.7 207.4 %copy-start.57 = (f32[2560]{0:T(1024)}, f32[2560]{0:T(1024)S(1)}, u32[]{:S(2)}) copy-start(f32[2560]{0:T(1024)S(1)} %broadcast_multiply_fusion.4) | copy-start | bytes 30724
  107.7 90.0 %copy-start.11 = (bf16[256,2560]{1,0:T(8,128)(2,1)}, bf16[256,2560]{1,0:T(8,128)(2,1)S(1)}, u32[]{:S(2)}) copy-start(bf16[256,2560]{1,0:T(8,128)(2,1)S(1)} %convolution_convert_fusion) | copy-start | bytes 3932164
  107.7 89.9 %collective-permute-start = (bf16[1,3,2560]{2,1,0:T(4,128)(2,1)S(1)}, bf16[1,3,2560]{2,1,0:T(4,128)(2,1)S(1)}, u32[]{:S(2)}, u32[]{:S(2)}) collective-permute-start(bf16[1,3,2560]{2,1,0:T(4,128)(2,1)S(1)} %slice.701), channel_id=1, source_target_pairs={{0,1},{1,2},{2,3},{3,4},{4,5},{5,6},{6,7},{8,9},{9,10},{10,11},{11... | collective-permute-start | bytes 46088 | tf_op jit(solution)/shard_map/ppermute | solution.py:18
  199.2 49.2 %copy-start.5 = (bf16[1,256,2560]{2,1,0:T(8,128)(2,1)}, bf16[1,256,2560]{2,1,0:T(8,128)(2,1)S(1)}, u32[]{:S(2)}) copy-start(bf16[1,256,2560]{2,1,0:T(8,128)(2,1)S(1)} %fusion.11) | copy-start | bytes 3932164
  199.8 48.5 %copy-start.3 = (bf16[1,256,2560]{1,2,0:T(8,128)(2,1)}, bf16[1,256,2560]{1,2,0:T(8,128)(2,1)S(1)}, u32[]{:S(2)}) copy-start(bf16[1,256,2560]{1,2,0:T(8,128)(2,1)S(1)} %copy.83) | copy-start | bytes 3932164
  250.5 57.6 %copy-start = (f32[1,256,2560]{2,1,0:T(8,128)}, f32[1,256,2560]{2,1,0:T(8,128)S(1)}, u32[]{:S(2)}) copy-start(f32[1,256,2560]{2,1,0:T(8,128)S(1)} %copy.86) | copy-start | bytes 7864324
  465.1 78.6 %copy-start.24 = (f32[1,256,2560]{2,1,0:T(8,128)}, f32[1,256,2560]{2,1,0:T(8,128)S(1)}, u32[]{:S(2)}) copy-start(f32[1,256,2560]{2,1,0:T(8,128)S(1)} %pad.232) | copy-start | bytes 7864324
  566.9 347.0 %copy-start.8 = (f32[1,256,2560]{2,1,0:T(8,128)}, f32[1,256,2560]{2,1,0:T(8,128)S(1)}, u32[]{:S(2)}) copy-start(f32[1,256,2560]{2,1,0:T(8,128)S(1)} %get-tuple-element.299) | copy-start | bytes 7864324
  1026.7 13.2 copy-start.65
  1099.9 17.6 copy-start.50
  1103.4 28.7 copy-start.34
  1153.4 21.1 copy-start.1
  1153.4 21.1 copy-start.47
  1153.4 21.1 copy-start.54
  1153.4 21.1 copy-start.56
  1153.5 21.1 copy-start.58
  1218.7 271.4 %reduce-scatter.16.cloned.1.call-start = ((), (), s32[]{:S(2)}) async-start(), calls=%async_computation.19 | async-start | bytes 2703360 | tf_op jit(solution)/shard_map/reduce_scatter | solution.py:320
  1221.3 406.6 %reduce-scatter.18.cloned.1.call-start = ((), (), s32[]{:S(2)}) async-start(), calls=%async_computation.20 | async-start | bytes 2703360 | tf_op jit(solution)/shard_map/reduce_scatter | solution.py:322
  1224.6 633.2 %reduce-scatter.20.cloned.1.call-start = ((), (), s32[]{:S(2)}) async-start(), calls=%async_computation.21 | async-start | bytes 21626880 | tf_op jit(solution)/shard_map/reduce_scatter | solution.py:325
  1236.5 851.1 %reduce-scatter.14.cloned.1.call-start = ((), (), s32[]{:S(2)}) async-start(), calls=%async_computation.18 | async-start | bytes 21626880 | tf_op jit(solution)/shard_map/reduce_scatter | solution.py:317
  1247.0 1070.4 %reduce-scatter.12.cloned.1.call-start = ((), (), s32[]{:S(2)}) async-start(), calls=%async_computation.17 | async-start | bytes 21626880 | tf_op jit(solution)/shard_map/reduce_scatter | solution.py:316
  1251.0 3.1 collective-permute-start.1
  1263.8 1489.8 %reduce-scatter.22.cloned.1.call-start = ((), (), s32[]{:S(2)}) async-start(), calls=%async_computation.22 | async-start | bytes 51904512 | tf_op jit(solution)/shard_map/reduce_scatter | solution.py:222
  1286.4 1905.9 %reduce-scatter.24.cloned.1.call-start = ((), (), s32[]{:S(2)}) async-start(), calls=%async_computation.23 | async-start | bytes 51904512 | tf_op jit(solution)/shard_map/reduce_scatter | solution.py:223
  1307.8 2322.9 %reduce-scatter.26.cloned.1.call-start = ((), (), s32[]{:S(2)}) async-start(), calls=%async_computation.24 | async-start | bytes 51904512 | tf_op jit(solution)/shard_map/reduce_scatter | solution.py:224
  1350.2 53.9 %copy-start.113 = (f32[256]{0:T(256)S(1)}, f32[256]{0:T(256)}, u32[]{:S(2)}) copy-start(f32[256]{0:T(256)} %copy-done.112) | copy-start | bytes 3076
  1350.2 53.9 %copy-start.16 = (f32[1,256,2048]{2,1,0:T(8,128)S(1)}, f32[1,256,2048]{2,1,0:T(8,128)}, u32[]{:S(2)}) copy-start(f32[1,256,2048]{2,1,0:T(8,128)} %copy-done.14) | copy-start | bytes 6291460
  (94 other events, 443.8 us)
Sparse Core Ops, SparseCore 0:
  11.0 89.7 all-gather.9
  103.6 85.5 all-gather.15
  192.0 52.9 all-gather.11
  247.7 53.3 all-gather.13
  303.8 85.7 all-gather.17
  392.5 153.7 all-gather.19
  549.4 152.8 all-gather.21
  705.3 152.8 all-gather.23
  1218.8 133.3 reduce-scatter.27
  1355.0 135.0 reduce-scatter.15
  1493.0 134.8 reduce-scatter.17
  1630.7 227.0 reduce-scatter.19
  1860.8 226.8 reduce-scatter.13
  2090.5 226.8 reduce-scatter.11
  2325.3 428.2 reduce-scatter.21
  2761.6 430.6 reduce-scatter.23
  3200.2 430.4 reduce-scatter.25
where the time goes:
time: 3660 us; the launch traced here: 3640 us
  waiting for transfers between devices  2650 us (72%)
  local copies, waits for them, and re-layouts  412 us (11%)
  matrix products  252 us (7%)
  blocking collectives  168 us (5%)
  other arithmetic  128 us (3%)
    reduce_scatter x1, waiting for transfers between devices, body(): lax.psum_scatter(grad_up_w, ('seq', 'tok'), scatter_dimension=0, tiled=True)  439 us
    reduce_scatter x1, waiting for transfers between devices, body(): lax.psum_scatter(grad_down, ('seq', 'tok'), scatter_dimension=0, tiled=True)  438 us
    reduce_scatter x1, waiting for transfers between devices, body(): lax.psum_scatter(grad_gate_w, ('seq', 'tok'), scatter_dimension=0, tiled=...  436 us
    reduce_scatter x1, waiting for transfers between devices, body(): lax.psum_scatter(grad_out_w, ('seq', 'tok'), scatter_dimension=0, tiled=T...  230 us
    reduce_scatter x1, waiting for transfers between devices, body(): lax.psum_scatter(grad_gelu_w, ('seq', 'tok'), scatter_dimension=0, tiled=...  230 us
    reduce_scatter x1, waiting for transfers between devices, body(): lax.psum_scatter(grad_in_w, ('seq', 'tok'), scatter_dimension=0, tiled=True)  230 us
    slice x57, local copies, waits for them, and re-layouts, body(): lax.associative_scan(combine, (next_decay, grad_local), axis=1, reverse=T...  150 us
    all_gather x1, waiting for transfers between devices, body(): lax.all_gather(down_weight, ('seq', 'tok'), axis=0, tiled=True)  142 us
  transfers between devices with their start and end apart: 19, of which 14 were waited for; matrix products, arithmetic and copies ran while one was open for 12% of the time, Pallas kernels for 0%

commit v1 on v0

v1 whole, which is shorter than its diff:
```python
import jax
import jax.numpy as jnp
from jax import lax
from jax.sharding import PartitionSpec as P

BW = 256
CONV = 4
SMALL = 128
BF = jnp.bfloat16
F32 = jnp.float32
eps = 1e-06


def from_behind(block, axis, distance):
    devices = range(lax.axis_size(axis))
    route = [(i - distance, i) for i in devices if i - distance in devices]
    return lax.ppermute(block, axis, route)


def entering(value, axis, join, neutral, backward):
    count, mine = (lax.axis_size(axis), lax.axis_index(axis))
    pieces = jax.tree.map(lambda part: lax.all_gather(part, axis), value)
    if backward:
        pieces = jax.tree.map(lambda part: part[::-1], pieces)
        mine = count - 1 - mine
    total = jax.tree.map(
        lambda part, zero: jnp.full_like(part, 0) + jnp.asarray(zero, part.dtype), value, neutral
    )

    def turn(position, total):
        longer = join(total, jax.tree.map(lambda part: part[position], pieces))
        return jax.tree.map(lambda new, old: jnp.where(position < mine, new, old), longer, total)

    return lax.fori_loop(0, count - 1, turn, total)


def gelu(value):
    return jax.nn.gelu(value, approximate=True)


def rms_scale(value, gain):
    return value * lax.rsqrt(jnp.mean(value * value, axis=-1, keepdims=True) + eps) * gain


def combine(earlier, later):
    return (earlier[0] * later[0], later[0] * earlier[1] + later[1])


def gelu_product(gate_val, up_val):
    return gelu(gate_val) * up_val


def recur_inputs(gate_pre, input_pre, conv_vals, decay_param):
    decay_log = -8.0 * jax.nn.sigmoid(gate_pre) * jax.nn.softplus(decay_param)
    inject = jnp.sqrt(-jnp.expm1(2.0 * decay_log)) * jax.nn.sigmoid(input_pre) * conv_vals
    return (jnp.exp(decay_log), inject)


def forward_product(left, weight):
    return jnp.dot(left, weight, preferred_element_type=F32)


def back_product(grad, weight):
    return lax.dot_general(grad, weight, (((2,), (1,)), ((), ())), preferred_element_type=F32)


def token_product(left, grad):
    return lax.dot_general(left, grad, (((0, 1), (0, 1)), ((), ())), preferred_element_type=F32)


def split_blocks(value):
    return value.reshape(value.shape[:-1] + (value.shape[-1] // BW, BW))


def block_gate(conv_low, weights, bias):
    result = jnp.einsum(
        "sthi,hij->sthj", split_blocks(conv_low), weights.reshape(-1, BW, BW), preferred_element_type=F32
    )
    return result.reshape(conv_low.shape) + bias


def block_gate_back(grad_low, weights):
    result = jnp.einsum(
        "sthj,hij->sthi", split_blocks(grad_low), weights.reshape(-1, BW, BW), preferred_element_type=F32
    )
    return result.reshape(grad_low.shape)


def block_gate_weight(conv_low, grad_low):
    result = jnp.einsum(
        "sthi,sthj->hij", split_blocks(conv_low), split_blocks(grad_low), preferred_element_type=F32
    )
    return result.reshape(-1, BW)


def to_seq(parts):
    return lax.all_to_all(parts, "seq", split_axis=0, concat_axis=0, tiled=True)


def gather(value, axis):
    return lax.all_gather(value, axis, axis=0, tiled=True)


def scatter(value, axis):
    return lax.psum_scatter(value.astype(BF), axis, scatter_dimension=0, tiled=True)


def body(
    tokens,
    source_ids,
    loss_weights,
    grad_output,
    first_gain,
    input_weight,
    gelu_weight,
    conv_weight,
    conv_bias,
    decay_gate,
    decay_bias,
    input_gate,
    input_bias,
    decay_param,
    output_weight,
    second_gain,
    gate_weight,
    up_weight,
    down_weight,
):
    S, T = lax.axis_size("seq"), lax.axis_size("tok")
    me = lax.axis_index("seq")
    length, D = tokens.shape[1:]
    ds, R = input_weight.shape
    rs = output_weight.shape[0]
    F = gate_weight.shape[1]
    FQ = F // S
    heads = R // BW
    starts = [-(-i * heads // S) for i in range(S + 1)]
    C = max(starts[i + 1] - starts[i] for i in range(S)) * BW
    quarter = R // S
    offs = [starts[i] * BW - i * quarter for i in range(S)] + [0]
    most = max(offs)
    off = sum(jnp.where(me == i, offs[i], 0) for i in range(S))
    own = sum(jnp.where(me == i, (starts[i + 1] - starts[i]) * BW, 0) for i in range(S))

    def cols_for(w):
        parts = [w[:, starts[i] * BW : starts[i + 1] * BW] for i in range(S)]
        return jnp.stack([jnp.pad(p, ((0, 0), (0, C - p.shape[1]))) for p in parts])

    def d_rows(w):
        w = gather(w[None], "tok")
        return jnp.swapaxes(w, 0, 1).reshape((D, w.shape[-1]))

    gains = jnp.pad(jnp.stack([first_gain, second_gain], axis=1), ((0, 0), (0, SMALL - 2)))
    pack_in = jnp.concatenate(
        [cols_for(input_weight), cols_for(gelu_weight), jnp.broadcast_to(gains, (S,) + gains.shape)], axis=2
    )
    pack_in = d_rows(to_seq(pack_in))
    weight_in, weight_gelu = pack_in[:, :C], pack_in[:, C : 2 * C]
    gain_one, gain_two = pack_in[:, 2 * C].astype(F32), pack_in[:, 2 * C + 1].astype(F32)
    small = jnp.concatenate(
        [conv_weight, jnp.stack([conv_bias, decay_bias, input_bias, decay_param], axis=1)], axis=1
    )
    small = jnp.pad(small, ((0, 0), (0, SMALL - small.shape[1])))
    pack_r = gather(jnp.concatenate([output_weight, decay_gate, input_gate, small], axis=1), "tok")
    lent = from_behind(pack_r[:most], "seq", -1)
    pack_r = jnp.concatenate([pack_r, lent, jnp.zeros_like(lent)], axis=0)
    pack_r = lax.dynamic_slice_in_dim(pack_r, off, C, axis=0)
    pack_r = jnp.where(lax.broadcasted_iota(jnp.int32, pack_r.shape, 0) < own, pack_r, 0)
    weight_out = pack_r[:, :D]
    weight_decay, weight_input = pack_r[:, D : D + BW], pack_r[:, D + BW : D + 2 * BW]
    rows = pack_r[:, D + 2 * BW :].T.astype(F32)
    conv_float, bias_conv, bias_decay, bias_input, param = rows[:CONV], rows[4], rows[5], rows[6], rows[7]

    pack_f = jnp.stack([w.reshape(ds, S, FQ).swapaxes(0, 1) for w in (gate_weight, up_weight)])
    pack_f = lax.all_to_all(pack_f, "seq", split_axis=1, concat_axis=1, tiled=True)
    pack_f = gather(pack_f[None], "tok")
    pack_f = pack_f.transpose(1, 2, 0, 3, 4).reshape(2, D, FQ)
    weight_gate, weight_up = pack_f[0], pack_f[1]
    weight_down = gather(down_weight, "tok")

    inputs = tokens.astype(F32)
    everyone = gather(tokens, "seq").astype(F32)
    normed = rms_scale(everyone, gain_one).astype(BF)
    branch_x = forward_product(normed, weight_in).astype(BF)
    branch_y = forward_product(normed, weight_gelu)
    previous = from_behind(branch_x[:, length - (CONV - 1) :, :], "tok", 1)
    extended = jnp.concatenate([previous, branch_x], axis=1)
    conv_out = bias_conv + jnp.zeros(branch_x.shape, F32)
    for k in range(CONV):
        conv_out = conv_out + extended[:, k : k + length, :].astype(F32) * conv_float[k]
    conv_low = conv_out.astype(BF)
    conv_vals = conv_low.astype(F32)
    gate_pre = block_gate(conv_low, weight_decay, bias_decay)
    input_pre = block_gate(conv_low, weight_input, bias_input)
    decays, inject = recur_inputs(gate_pre, input_pre, conv_vals, param)
    cum_decay, local_state = lax.associative_scan(combine, (decays, inject), axis=1)
    ones, zeros = jnp.ones((S, C), F32), jnp.zeros((S, C), F32)
    incoming = entering(
        (cum_decay[:, -1, :], local_state[:, -1, :]), "tok", combine, (ones, zeros), False
    )[1]
    states = local_state + cum_decay * incoming[:, None, :]
    gated = gelu(branch_y)
    mixed = (states * gated).astype(BF)
    resid = inputs + scatter(forward_product(mixed, weight_out), "seq").astype(F32)
    second_own = rms_scale(resid, gain_two).astype(BF)
    second_normed = gather(second_own, "seq")
    sources = lax.broadcasted_iota(jnp.int32, (1, loss_weights.shape[0]), 1)
    picked = jnp.sum(jnp.where(source_ids[:, None] == sources, loss_weights[None, :], 0.0), axis=1)
    cotangent = grad_output.astype(F32) * picked[:, None, None]
    cot_low = gather(cotangent.astype(BF), "seq")

    gate_val = forward_product(second_normed, weight_gate)
    up_val = forward_product(second_normed, weight_up)
    hidden = gelu_product(gate_val, up_val).astype(BF)
    block_out = (resid + scatter(forward_product(hidden, weight_down), "seq").astype(F32)).astype(BF)

    grad_hidden = back_product(cot_low, weight_down)
    _, hidden_pull = jax.vjp(gelu_product, gate_val, up_val)
    grad_gate_val, grad_up_val = hidden_pull(grad_hidden)
    grad_gate_low, grad_up_low = grad_gate_val.astype(BF), grad_up_val.astype(BF)
    grad_second = back_product(grad_gate_low, weight_gate) + back_product(grad_up_low, weight_up)
    grad_second = scatter(grad_second, "seq").astype(F32)
    grad_down = scatter(token_product(hidden, cot_low), "tok").astype(F32)

    def d_scatter(g):
        cols = g.shape[-1]
        g = g.reshape((S, T, ds, cols)).swapaxes(0, 1).astype(BF).reshape(D, cols)
        return to_seq(scatter(g, "tok").reshape(S, ds, cols))

    def whole_rows(parts):
        return parts.swapaxes(0, 1).reshape(ds, F).astype(F32)

    grad_gate_w = whole_rows(d_scatter(token_product(second_normed, grad_gate_low)))
    grad_up_w = whole_rows(d_scatter(token_product(second_normed, grad_up_low)))

    _, second_pull = jax.vjp(rms_scale, resid, gain_two)
    grad_resid_norm, grad_gain_two = second_pull(grad_second)
    grad_resid = cotangent + grad_resid_norm
    resid_low = gather(grad_resid.astype(BF), "seq")

    grad_out_w = token_product(mixed, resid_low)
    grad_mixed = back_product(resid_low, weight_out)
    grad_local = grad_mixed * gated
    _, gelu_pull = jax.vjp(gelu, branch_y)
    grad_y_low = gelu_pull(grad_mixed * states)[0].astype(BF)
    next_decay = jnp.concatenate([decays[:, 1:, :], jnp.ones((S, 1, C), F32)], axis=1)
    reach, local_adjoint = lax.associative_scan(combine, (next_decay, grad_local), axis=1, reverse=True)
    first_adjoint = decays[:, 0, :] * local_adjoint[:, 0, :]
    carry_in = entering((cum_decay[:, -1, :], first_adjoint), "tok", combine, (ones, zeros), True)[1]
    grad_states = local_adjoint + reach * carry_in[:, None, :]
    prev_states = jnp.concatenate([incoming[:, None, :], states[:, :-1, :]], axis=1)
    _, recur_pull = jax.vjp(recur_inputs, gate_pre, input_pre, conv_vals, param)
    grad_gate_pre, grad_input_pre, grad_conv, grad_param = recur_pull((grad_states * prev_states, grad_states))
    gate_low, input_low = grad_gate_pre.astype(BF), grad_input_pre.astype(BF)
    grad_decay_b = jnp.sum(gate_low.astype(F32), axis=(0, 1))
    grad_input_b = jnp.sum(input_low.astype(F32), axis=(0, 1))
    grad_decay_w = block_gate_weight(conv_low, gate_low)
    grad_input_w = block_gate_weight(conv_low, input_low)
    grad_conv = grad_conv + block_gate_back(gate_low, weight_decay) + block_gate_back(input_low, weight_input)
    grad_conv_b = jnp.sum(grad_conv, axis=(0, 1))
    taps = []
    grad_extended = jnp.zeros((S, length + CONV - 1, C), F32)
    for k in range(CONV):
        taps.append(jnp.sum(grad_conv * extended[:, k : k + length, :].astype(F32), axis=(0, 1)))
        grad_extended = grad_extended + jnp.pad(
            grad_conv * conv_float[k], ((0, 0), (k, CONV - 1 - k), (0, 0))
        )
    rim = from_behind(grad_extended[:, : CONV - 1, :], "tok", -1)
    grad_branch_x = grad_extended[:, CONV - 1 :, :] + jnp.pad(rim, ((0, 0), (length - (CONV - 1), 0), (0, 0)))
    grad_x_low = grad_branch_x.astype(BF)
    grad_in_w = token_product(normed, grad_x_low)
    grad_gelu_w = token_product(normed, grad_y_low)
    grad_normed = back_product(grad_x_low, weight_in) + back_product(grad_y_low, weight_gelu)
    grad_normed = scatter(grad_normed, "seq").astype(F32)
    _, first_pull = jax.vjp(rms_scale, inputs, gain_one)
    grad_inputs_norm, grad_gain_one = first_pull(grad_normed)
    grad_tokens = grad_resid + grad_inputs_norm

    smalls = jnp.stack(taps + [grad_conv_b, grad_decay_b, grad_input_b, grad_param], axis=1)
    smalls = jnp.pad(smalls, ((0, 0), (0, SMALL - smalls.shape[1])))
    grad_r = jnp.concatenate([grad_out_w, grad_decay_w, grad_input_w, smalls], axis=1).astype(BF)
    grad_r = lax.dynamic_update_slice_in_dim(
        jnp.zeros((quarter + 2 * most, grad_r.shape[1]), BF), grad_r, off, axis=0
    )
    back = from_behind(grad_r[quarter : quarter + most], "seq", 1)
    keep = lax.broadcasted_iota(jnp.int32, (quarter, 1), 0) < off
    grad_r = jnp.where(keep, jnp.pad(back, ((0, quarter - most), (0, 0))), grad_r[:quarter])
    grad_r = scatter(grad_r, "tok").astype(F32)
    gain_grads = jnp.pad(jnp.stack([grad_gain_one, grad_gain_two], axis=1), ((0, 0), (0, SMALL - 2)))
    grad_i = d_scatter(jnp.concatenate([grad_in_w, grad_gelu_w, gain_grads], axis=1)).astype(F32)
    gain_grads = jnp.sum(grad_i[:, :, 2 * C :], axis=0)

    def columns(at):
        return jnp.concatenate(
            [grad_i[i, :, at : at + (starts[i + 1] - starts[i]) * BW] for i in range(S)], axis=1
        )

    smalls = grad_r[:, D + 2 * BW :]
    return (
        block_out,
        grad_tokens,
        gain_grads[:, 0],
        columns(0),
        columns(C),
        smalls[:, :CONV],
        smalls[:, 4],
        grad_r[:, D : D + BW],
        smalls[:, 5],
        grad_r[:, D + BW : D + 2 * BW],
        smalls[:, 6],
        smalls[:, 7],
        grad_r[:, :D],
        gain_grads[:, 1],
        grad_gate_w,
        grad_up_w,
        grad_down,
    )


def solution(mesh):
    one, two = P(("seq", "tok")), P(("seq", "tok"), None)
    data = P("seq", "tok", None)
    return jax.shard_map(
        body,
        mesh=mesh,
        in_specs=(data, P("seq"), P(), data, one, two, two, two, one, two, one, two, one, one, two, one, two, two, two),
        out_specs=(data, data, one, two, two, two, one, two, one, two, one, one, two, one, two, two, two),
        check_vma=False,
    )
```

time: 3660 us -> 1820 us (0.50)
  waiting for transfers between devices: 2650 us -> 789 us
  local copies, waits for them, and re-layouts: 412 us -> 522 us
  matrix products: 252 us -> 177 us
  blocking collectives: 168 us -> 100 us
  other arithmetic: 128 us -> 173 us
    reduce_scatter x8 -> x5, waiting for transfers between devices: 2220 us -> 243 us  [scatter(): lax.psum_scatter(value.astype(BF), axis, scatter_dimension=0, tiled=True)]
    unnamed x18 -> x21, waiting for transfers between devices: 5.18 us -> 130 us
    unnamed x2 -> x0, blocking collectives: 84.8 us -> none
    all_to_all x0 -> x2, blocking collectives: none -> 57.8 us  [the longest x1 40.5 us: body(): lax.all_to_all(pack_f, 'seq', split_axis=1, concat_axis=1, tiled=True)]
    dot_general x6, matrix products: 92.9 us -> 46.9 us  [token_product(): lax.dot_general(left, grad, (((0, 1), (0, 1)), ((), ())), preferred_eleme...]
    all_gather x1 -> x0, blocking collectives: 40.6 us -> none  [body(): lax.all_gather(conv_weight, ('seq', 'tok'), axis=0, tiled=True)]
  transfers between devices with their start and end apart: 19 -> 24, of which waited for: 14 -> 18; matrix products, arithmetic and copies ran while one was open for 12% -> 13% of each run, Pallas kernels for 0% -> 0%
where the time goes in v1:
time: 1820 us; the launch traced here: 1800 us
  waiting for transfers between devices  789 us (43%)
  local copies, waits for them, and re-layouts  522 us (29%)
  matrix products  177 us (10%)
  other arithmetic  173 us (10%)
  blocking collectives  100 us (5%)
  starting transfers between devices  20.8 us (1%)
    all_gather x8, waiting for transfers between devices, gather(): return lax.all_gather(value, axis, axis=0, tiled=True)  400 us
    reduce_scatter x5, waiting for transfers between devices, scatter(): lax.psum_scatter(value.astype(BF), axis, scatter_dimension=0, tiled=True)  243 us
    slice x57, local copies, waits for them, and re-layouts, body(): lax.associative_scan(combine, (next_decay, grad_local), axis=1, reverse=T...  171 us
    unnamed x21, waiting for transfers between devices  130 us
    slice x52, local copies, waits for them, and re-layouts, body(): lax.associative_scan(combine, (decays, inject), axis=1)  124 us
    dot_general x6, matrix products, back_product(): lax.dot_general(grad, weight, (((2,), (1,)), ((), ())), preferred_element...  65.8 us
    dot_general x6, matrix products, forward_product(): return jnp.dot(left, weight, preferred_element_type=F32)  53.9 us
    rev x2, local copies, waits for them, and re-layouts, body(): lax.associative_scan(combine, (next_decay, grad_local), axis=1, reverse=T...  49.5 us
  transfers between devices with their start and end apart: 24, of which 18 were waited for; matrix products, arithmetic and copies ran while one was open for 13% of the time, Pallas kernels for 0%

profile of v1, /device:TPU:0, one launch (start us, length us, event | category | flops | bytes accessed | tf_op | source)
XLA Modules:
  0.0 1798.7 jit_solution(10549583955441443971)
XLA Ops:
  13.6 17.3 all_to_all.25
  31.1 22.6 %all-gather.14.cloned.1.call-done = bf16[640,2688]{1,0:T(8,128)(2,1)} async-done(((bf16[80,2688]{1,0:T(8,128)(2,1)}), bf16[640,2688]{1,0:T(8,128)(2,1)}) %all-gather.14.cloned.1.call-update) | async-done | bytes 3440656 | tf_op jit(solution)/shard_map/all_gather | solution.py:101
  57.2 59.1 %all-gather.16.cloned.1.call-done = bf16[4,256,2048]{2,1,0:T(8,128)(2,1)} async-done(((bf16[1,256,2048]{2,1,0:T(8,128)(2,1)}), bf16[4,256,2048]{2,1,0:T(8,128)(2,1)}) %all-gather.16.cloned.1.call-update) | async-done | bytes 4194320 | tf_op jit(solution)/shard_map/all_gather | solution.py:101
  125.2 61.8 %all-gather.26.cloned.1.call-done = bf16[32,64,1664]{2,1,0:T(8,128)(2,1)} async-done(((bf16[4,64,1664]{2,1,0:T(8,128)(2,1)}), bf16[32,64,1664]{2,1,0:T(8,128)(2,1)}) %all-gather.26.cloned.1.call-update) | async-done | bytes 6815760 | tf_op jit(solution)/shard_map/all_gather | solution.py:101
  223.8 9.7 slice.707
  233.5 9.5 slice.708
  355.7 9.6 slice.762
  412.1 14.7 all-gather.2
  436.1 13.9 all-gather.1
  450.7 13.9 multiply_convert_fusion.2
  474.5 40.5 %all_to_all.26 = bf16[2,4,64,1536]{3,2,0,1:T(8,128)(2,1)S(1)} all-to-all(bf16[2,4,64,1536]{3,2,0,1:T(8,128)(2,1)S(1)} %copy.215), channel_id=1, replica_groups=mesh['seq'=4,'tok'=8] {'seq'}, dimensions={1} | all-to-all | bytes 3145728 | tf_op jit(solution)/shard_map/all_to_all | solution.py:175
  516.7 23.6 %reduce-scatter.28.cloned.1.call-done = bf16[1,256,2048]{2,1,0:T(8,128)(2,1)} async-done(((bf16[4,256,2048]{2,1,0:T(8,128)(2,1)}), bf16[1,256,2048]{2,1,0:T(8,128)(2,1)}) %reduce-scatter.28.cloned.1.call-update) | async-done | bytes 1048592
  548.6 110.7 %all-gather.28.cloned.1.call-done = bf16[16,4,64,1536]{3,2,1,0:T(8,128)(2,1)} async-done(((bf16[2,4,64,1536]{3,2,1,0:T(8,128)(2,1)}), bf16[16,4,64,1536]{3,2,1,0:T(8,128)(2,1)}) %all-gather.28.cloned.1.call-update) | async-done | bytes 12582928 | tf_op jit(solution)/shard_map/all_gather | solution.py:101
  671.6 41.0 %all-gather.18.cloned.1.call-done = bf16[4,256,2048]{2,1,0:T(8,128)(2,1)} async-done(((bf16[1,256,2048]{2,1,0:T(8,128)(2,1)}), bf16[4,256,2048]{2,1,0:T(8,128)(2,1)}) %all-gather.18.cloned.1.call-update) | async-done | bytes 4194320 | tf_op jit(solution)/shard_map/all_gather | solution.py:101
  712.7 11.8 fusion.132
  724.5 8.6 fusion.133
  733.1 34.9 %all-gather.22.cloned.1.call-done = bf16[4,256,2048]{2,1,0:T(8,128)(2,1)} async-done(((bf16[1,256,2048]{2,1,0:T(8,128)(2,1)}), bf16[4,256,2048]{2,1,0:T(8,128)(2,1)}) %all-gather.22.cloned.1.call-update) | async-done | bytes 4194320 | tf_op jit(solution)/shard_map/all_gather | solution.py:101
  767.9 66.5 %all-gather.20.cloned.1.call-done = bf16[1536,2048]{1,0:T(8,128)(2,1)} async-done(((bf16[192,2048]{1,0:T(8,128)(2,1)}), bf16[1536,2048]{1,0:T(8,128)(2,1)}) %all-gather.20.cloned.1.call-update) | async-done | bytes 6291472 | tf_op jit(solution)/shard_map/all_gather | solution.py:101
  834.5 18.0 multiply_convert_fusion
  852.5 11.1 fusion.134
  863.5 11.1 add_convert_fusion.1
  874.8 51.5 %reduce-scatter.30.cloned.1.call-done = bf16[1,256,2048]{2,1,0:T(8,128)(2,1)} async-done(((bf16[4,256,2048]{2,1,0:T(8,128)(2,1)}), bf16[1,256,2048]{2,1,0:T(8,128)(2,1)}) %reduce-scatter.30.cloned.1.call-update) | async-done | bytes 1048592
  953.2 12.9 slice.790
  966.1 7.9 slice.797
  974.0 7.8 slice.788
  985.4 11.5 fusion.71
  1008.4 12.8 slice.792
  1021.2 12.8 slice.794
  1115.8 9.5 slice.849
  1157.5 13.2 slice.850
  1190.0 14.0 all-gather.4
  1224.4 24.6 %rev.15 = f32[4,256,768]{2,1,0:T(8,128)} reverse(f32[4,256,768]{2,1,0:T(8,128)} %add.693), dimensions={1} | reverse | bytes 6291456 | tf_op jit(solution)/shard_map/rev | solution.py:247
  1249.0 24.8 %rev.14 = f32[4,256,768]{2,1,0:T(8,128)} reverse(f32[4,256,768]{2,1,0:T(8,128)} %add.685), dimensions={1} | reverse | bytes 6291456 | tf_op jit(solution)/shard_map/rev | solution.py:247
  1273.9 8.9 multiply_reduce_fusion
  1309.1 9.9 fusion.32
  1330.1 8.3 add_convert_fusion
  1340.3 9.4 bitcast_convert_fusion.2
  1354.8 9.6 bitcast_convert_fusion.1
  1369.7 10.8 bitcast_convert_fusion
  1393.8 15.2 collective-permute-done.3
  1412.9 7.9 bitcast_convert_fusion.4
  1434.8 9.8 copy.229
  1451.1 11.1 fusion.22
  1467.7 67.0 %reduce-scatter.24.cloned.1.call-done = bf16[256,1536]{1,0:T(8,128)(2,1)} async-done(((bf16[2048,1536]{1,0:T(8,128)(2,1)}), bf16[256,1536]{1,0:T(8,128)(2,1)}) %reduce-scatter.24.cloned.1.call-update) | async-done | bytes 786448 | tf_op jit(solution)/shard_map/reduce_scatter | solution.py:105
  1538.3 66.8 %reduce-scatter.26.cloned.1.call-done = bf16[192,2048]{1,0:T(8,128)(2,1)} async-done(((bf16[1536,2048]{1,0:T(8,128)(2,1)}), bf16[192,2048]{1,0:T(8,128)(2,1)}) %reduce-scatter.26.cloned.1.call-update) | async-done | bytes 786448 | tf_op jit(solution)/shard_map/reduce_scatter | solution.py:105
  1610.6 38.4 %reduce-scatter.20.cloned.1.call-done = bf16[80,2688]{1,0:T(8,128)(2,1)} async-done(((bf16[640,2688]{1,0:T(8,128)(2,1)}), bf16[80,2688]{1,0:T(8,128)(2,1)}) %reduce-scatter.20.cloned.1.call-update) | async-done | bytes 430096 | tf_op jit(solution)/shard_map/reduce_scatter | solution.py:105
  1655.5 69.0 %reduce-scatter.18.cloned.1.call-done = bf16[256,1664]{1,0:T(8,128)(2,1)} async-done(((bf16[2048,1664]{1,0:T(8,128)(2,1)}), bf16[256,1664]{1,0:T(8,128)(2,1)}) %reduce-scatter.18.cloned.1.call-update) | async-done | bytes 851984 | tf_op jit(solution)/shard_map/reduce_scatter | solution.py:105
  1728.8 53.3 %reduce-scatter.32.cloned.1.call-done = bf16[1,256,2048]{2,1,0:T(8,128)(2,1)} async-done(((bf16[4,256,2048]{2,1,0:T(8,128)(2,1)}), bf16[1,256,2048]{2,1,0:T(8,128)(2,1)}) %reduce-scatter.32.cloned.1.call-update) | async-done | bytes 1048592
  (725 shorter events, 577.8 us)
Async XLA Ops:
  7.2 46.5 %all-gather.14.cloned.1.call-start = ((), (), s32[]{:S(2)}) async-start(), calls=%async_computation.14 | async-start | bytes 3870720 | tf_op jit(solution)/shard_map/all_gather | solution.py:101
  10.0 106.3 %all-gather.16.cloned.1.call-start = ((), (), s32[]{:S(2)}) async-start(), calls=%async_computation.15 | async-start | bytes 5242880 | tf_op jit(solution)/shard_map/all_gather | solution.py:101
  10.8 176.3 %all-gather.26.cloned.1.call-start = ((), (), s32[]{:S(2)}) async-start(), calls=%async_computation.25 | async-start | bytes 7667712 | tf_op jit(solution)/shard_map/all_gather | solution.py:101
  30.9 509.5 %reduce-scatter.28.cloned.1.call-start = ((), (), s32[]{:S(2)}) async-start(), calls=%async_computation.27 | async-start | bytes 5242880
  53.7 66.2 %copy-start.37 = (bf16[640,2688]{1,0:T(8,128)(2,1)S(1)}, bf16[640,2688]{1,0:T(8,128)(2,1)}, u32[]{:S(2)}) copy-start(bf16[640,2688]{1,0:T(8,128)(2,1)} %all-gather.14.cloned.1.call-done) | copy-start | bytes 10321924
  55.9 64.1 %collective-permute-start = (bf16[128,2688]{1,0:T(8,128)(2,1)}, bf16[128,2688]{1,0:T(8,128)(2,1)}, u32[]{:S(2)}, u32[]{:S(2)}) collective-permute-start(bf16[128,2688]{1,0:T(8,128)(2,1)} %slice.890), channel_id=1, source_target_pairs={{8,0},{16,8},{24,16},{9,1},{17,9},{25,17},{10,2},{18,10},{26,18},{... | collective-permute-start | bytes 2064392 | tf_op jit(solution)/shard_map/ppermute | solution.py:17
  124.4 73.4 %copy-start.115 = (f32[768]{0:T(1024)}, f32[768]{0:T(1024)S(1)}, u32[]{:S(2)}) copy-start(f32[768]{0:T(1024)S(1)} %get-tuple-element.345) | copy-start | bytes 9220
  124.4 74.2 %copy-start.107 = (f32[768]{0:T(1024)}, f32[768]{0:T(1024)S(1)}, u32[]{:S(2)}) copy-start(f32[768]{0:T(1024)S(1)} %get-tuple-element.347) | copy-start | bytes 9220
  124.4 74.2 %copy-start.109 = (f32[768]{0:T(1024)}, f32[768]{0:T(1024)S(1)}, u32[]{:S(2)}) copy-start(f32[768]{0:T(1024)S(1)} %get-tuple-element.348) | copy-start | bytes 9220
  124.4 74.2 %copy-start.111 = (f32[768]{0:T(1024)}, f32[768]{0:T(1024)S(1)}, u32[]{:S(2)}) copy-start(f32[768]{0:T(1024)S(1)} %get-tuple-element.349) | copy-start | bytes 9220
  124.4 74.2 %copy-start.113 = (f32[768]{0:T(1024)}, f32[768]{0:T(1024)S(1)}, u32[]{:S(2)}) copy-start(f32[768]{0:T(1024)S(1)} %get-tuple-element.350) | copy-start | bytes 9220
  124.4 92.5 %copy-start.67 = (f32[768]{0:T(1024)}, f32[768]{0:T(1024)S(1)}, u32[]{:S(2)}) copy-start(f32[768]{0:T(1024)S(1)} %get-tuple-element.344) | copy-start | bytes 9220
  125.2 83.0 %copy-start.40 = (bf16[768,256]{1,0:T(8,128)(2,1)}, bf16[768,256]{1,0:T(8,128)(2,1)S(1)}, u32[]{:S(2)}) copy-start(bf16[768,256]{1,0:T(8,128)(2,1)S(1)} %get-tuple-element.391) | copy-start | bytes 1179652
  195.6 3.0 collective-permute-start.1
  470.8 188.5 %all-gather.28.cloned.1.call-start = ((), (), s32[]{:S(2)}) async-start(), calls=%async_computation.26 | async-start | bytes 14155776 | tf_op jit(solution)/shard_map/all_gather | solution.py:101
  515.0 25.4 %copy-start.3 = (bf16[1,256,2048]{2,1,0:T(8,128)(2,1)S(1)}, bf16[1,256,2048]{2,1,0:T(8,128)(2,1)}, u32[]{:S(2)}) copy-start(bf16[1,256,2048]{2,1,0:T(8,128)(2,1)} %param.23) | copy-start | bytes 3145732
  515.0 27.0 %copy-start.63 = (f32[2048]{0:T(1024)S(1)}, f32[2048]{0:T(1024)}, u32[]{:S(2)}) copy-start(f32[2048]{0:T(1024)} %get-tuple-element.328) | copy-start | bytes 24580
  516.2 29.1 %copy-start.130 = (f32[8]{0:T(128)S(1)}, f32[8]{0:T(128)}, u32[]{:S(2)}) copy-start(f32[8]{0:T(128)} %param.25) | copy-start | bytes 100
  516.3 29.7 %copy-start.18 = (bf16[1,256,2048]{2,1,0:T(8,128)(2,1)S(1)}, bf16[1,256,2048]{2,1,0:T(8,128)(2,1)}, u32[]{:S(2)}) copy-start(bf16[1,256,2048]{2,1,0:T(8,128)(2,1)} %param.26) | copy-start | bytes 3145732
  516.3 196.4 %all-gather.18.cloned.1.call-start = ((), (), s32[]{:S(2)}) async-start(), calls=%async_computation.16 | async-start | bytes 5242880 | tf_op jit(solution)/shard_map/all_gather | solution.py:101
  542.0 387.3 %copy-start.117 = (f32[256]{0:T(256)}, f32[256]{0:T(256)S(1)}, u32[]{:S(2)}) copy-start(f32[256]{0:T(256)S(1)} %fusion.106) | copy-start | bytes 3076
  544.6 223.3 %all-gather.22.cloned.1.call-start = ((), (), s32[]{:S(2)}) async-start(), calls=%async_computation.18 | async-start | bytes 5242880 | tf_op jit(solution)/shard_map/all_gather | solution.py:101
  547.8 286.7 %all-gather.20.cloned.1.call-start = ((), (), s32[]{:S(2)}) async-start(), calls=%async_computation.17 | async-start | bytes 7077888 | tf_op jit(solution)/shard_map/all_gather | solution.py:101
  548.5 377.7 %reduce-scatter.30.cloned.1.call-start = ((), (), s32[]{:S(2)}) async-start(), calls=%async_computation.28 | async-start | bytes 5242880
  874.7 51.5 %copy-start.9 = (bf16[1,256,2048]{2,1,0:T(8,128)(2,1)S(1)}, bf16[1,256,2048]{2,1,0:T(8,128)(2,1)}, u32[]{:S(2)}) copy-start(bf16[1,256,2048]{2,1,0:T(8,128)(2,1)} %reduce-scatter.28.cloned.1.call-done) | copy-start | bytes 3145732
  874.7 110.7 %all-gather.24.cloned.1.call-start = ((), (), s32[]{:S(2)}) async-start(), calls=%async_computation.19 | async-start | bytes 5242880 | tf_op jit(solution)/shard_map/all_gather | solution.py:101
  932.5 493.8 %reduce-scatter.34.cloned.1.call-start = ((), (), s32[]{:S(2)}) async-start(), calls=%async_computation.30 | async-start | bytes 5242880
  1249.0 24.9 %copy-start.1 = (f32[4,256,768]{2,1,0:T(8,128)S(1)}, f32[4,256,768]{2,1,0:T(8,128)}, u32[]{:S(2)}) copy-start(f32[4,256,768]{2,1,0:T(8,128)} %copy-done) | copy-start | bytes 9437188
  1249.0 24.9 %copy-start.68 = (f32[768]{0:T(1024)S(1)}, f32[768]{0:T(1024)}, u32[]{:S(2)}) copy-start(f32[768]{0:T(1024)} %copy-done.67) | copy-start | bytes 9220
  1249.0 24.9 %copy-start.70 = (f32[768]{0:T(1024)S(1)}, f32[768]{0:T(1024)}, u32[]{:S(2)}) copy-start(f32[768]{0:T(1024)} %get-tuple-element.346) | copy-start | bytes 9220
  1249.0 24.9 %copy-start.73 = (f32[768]{0:T(1024)S(1)}, f32[768]{0:T(1024)}, u32[]{:S(2)}) copy-start(f32[768]{0:T(1024)} %get-tuple-element.490) | copy-start | bytes 9220
  1249.0 24.9 %copy-start.82 = (f32[4,1,768]{2,1,0:T(1,128)S(1)}, f32[4,1,768]{2,1,0:T(1,128)}, u32[]{:S(2)}) copy-start(f32[4,1,768]{2,1,0:T(1,128)} %broadcast_in_dim.69) | copy-start | bytes 36868
  1320.3 9.8 collective-permute-start.2
  1338.4 125.7 %reduce-scatter.22.cloned.1.call-start = ((), (), s32[]{:S(2)}) async-start(), calls=%async_computation.22 | async-start | bytes 7077888 | tf_op jit(solution)/shard_map/reduce_scatter | solution.py:105
  1353.0 181.7 %reduce-scatter.24.cloned.1.call-start = ((), (), s32[]{:S(2)}) async-start(), calls=%async_computation.23 | async-start | bytes 7077888 | tf_op jit(solution)/shard_map/reduce_scatter | solution.py:105
  1367.8 237.4 %reduce-scatter.26.cloned.1.call-start = ((), (), s32[]{:S(2)}) async-start(), calls=%async_computation.24 | async-start | bytes 7077888 | tf_op jit(solution)/shard_map/reduce_scatter | solution.py:105
  1380.6 268.4 %reduce-scatter.20.cloned.1.call-start = ((), (), s32[]{:S(2)}) async-start(), calls=%async_computation.21 | async-start | bytes 3870720 | tf_op jit(solution)/shard_map/reduce_scatter | solution.py:105
  1390.4 18.6 %collective-permute-start.3 = (bf16[128,2688]{1,0:T(8,128)(2,1)S(1)}, bf16[128,2688]{1,0:T(8,128)(2,1)S(1)}, u32[]{:S(2)}, u32[]{:S(2)}) collective-permute-start(bf16[128,2688]{1,0:T(8,128)(2,1)S(1)} %slice.1028), channel_id=1, source_target_pairs={{0,8},{8,16},{16,24},{1,9},{9,17},{17,25},{2,10},{10,18},{18,26},{... | collective-permute-start | bytes 2064392 | tf_op jit(solution)/shard_map/ppermute | solution.py:17
  1411.5 313.0 %reduce-scatter.18.cloned.1.call-start = ((), (), s32[]{:S(2)}) async-start(), calls=%async_computation.20 | async-start | bytes 7667712 | tf_op jit(solution)/shard_map/reduce_scatter | solution.py:105
  1451.0 331.0 %reduce-scatter.32.cloned.1.call-start = ((), (), s32[]{:S(2)}) async-start(), calls=%async_computation.29 | async-start | bytes 5242880
  1464.1 70.6 %all-to-all-start.3 = ((bf16[4,64,1536]{2,1,0:T(8,128)(2,1)}), bf16[4,64,1536]{2,1,0:T(8,128)(2,1)S(1)}, u32[]{:S(2)}, u32[]{:S(2)}) async-start(bf16[4,64,1536]{2,1,0:T(8,128)(2,1)} %bitcast.286), calls=%async_computation.6 | async-start | bytes 1572864 | tf_op jit(solution)/shard_map/all_to_all | solution.py:97
  1534.7 74.4 %all-to-all-start.4 = ((bf16[4,64,1536]{2,1,0:T(8,128)(2,1)}), bf16[4,64,1536]{2,1,0:T(8,128)(2,1)S(1)}, u32[]{:S(2)}, u32[]{:S(2)}) async-start(bf16[4,64,1536]{2,1,0:T(8,128)(2,1)} %bitcast.285), calls=%async_computation.8 | async-start | bytes 1572864 | tf_op jit(solution)/shard_map/all_to_all | solution.py:97
  1610.6 171.5 %copy-start.10 = (bf16[1,256,2048]{2,1,0:T(8,128)(2,1)S(1)}, bf16[1,256,2048]{2,1,0:T(8,128)(2,1)}, u32[]{:S(2)}) copy-start(bf16[1,256,2048]{2,1,0:T(8,128)(2,1)} %reduce-scatter.28.cloned.1.call-done) | copy-start | bytes 3145732
  1610.6 171.5 %copy-start.19 = (bf16[1,256,2048]{2,1,0:T(8,128)(2,1)S(1)}, bf16[1,256,2048]{2,1,0:T(8,128)(2,1)}, u32[]{:S(2)}) copy-start(bf16[1,256,2048]{2,1,0:T(8,128)(2,1)} %param.26) | copy-start | bytes 3145732
  1610.6 171.5 %copy-start.64 = (f32[2048]{0:T(1024)S(1)}, f32[2048]{0:T(1024)}, u32[]{:S(2)}) copy-start(f32[2048]{0:T(1024)} %get-tuple-element.328) | copy-start | bytes 24580
  1610.6 171.5 %copy-start.118 = (f32[256]{0:T(256)S(1)}, f32[256]{0:T(256)}, u32[]{:S(2)}) copy-start(f32[256]{0:T(256)} %copy-done.117) | copy-start | bytes 3076
  1610.6 171.5 %copy-start.124 = (f32[256]{0:T(256)S(1)}, f32[256]{0:T(256)}, u32[]{:S(2)}) copy-start(f32[256]{0:T(256)} %copy-done.123) | copy-start | bytes 3076
  1724.5 63.4 %all-to-all-start.2 = ((bf16[4,64,1664]{2,1,0:T(8,128)(2,1)}), bf16[4,64,1664]{2,1,0:T(8,128)(2,1)}, u32[]{:S(2)}, u32[]{:S(2)}) async-start(bf16[4,64,1664]{2,1,0:T(8,128)(2,1)} %bitcast.284), calls=%async_computation.3 | async-start | bytes 1703936 | tf_op jit(solution)/shard_map/all_to_all | solution.py:97
  (118 other events, 729.4 us)
Sparse Core Ops, SparseCore 0:
  10.3 43.4 all-gather.13
  55.6 60.6 all-gather.15
  117.9 69.0 all-gather.25
  470.9 69.3 reduce-scatter.27
  542.5 116.7 all-gather.27
  661.7 50.9 all-gather.17
  715.2 52.6 all-gather.21
  769.7 64.7 all-gather.19
  874.8 51.3 reduce-scatter.29
  932.7 52.6 all-gather.23
  1338.6 53.3 reduce-scatter.33
  1394.3 69.7 reduce-scatter.21
  1466.5 68.1 reduce-scatter.23
  1537.0 68.1 reduce-scatter.25
  1607.5 41.4 reduce-scatter.19
  1651.2 73.3 reduce-scatter.17
  1727.3 54.6 reduce-scatter.31

commit v2 on v1

v2 whole, which is shorter than its diff:
```python
import functools

import jax
import jax.numpy as jnp
from jax import lax
from jax.experimental import pallas as pl
from jax.experimental.pallas import tpu as pltpu
from jax.sharding import PartitionSpec as P

BW = 256
CONV = 4
SMALL = 128
BF = jnp.bfloat16
F32 = jnp.float32
eps = 1e-06


def from_behind(block, axis, distance):
    devices = range(lax.axis_size(axis))
    route = [(i - distance, i) for i in devices if i - distance in devices]
    return lax.ppermute(block, axis, route)


def gelu(value):
    return jax.nn.gelu(value, approximate=True)


def rms_scale(value, gain):
    return value * lax.rsqrt(jnp.mean(value * value, axis=-1, keepdims=True) + eps) * gain


def gelu_product(gate_val, up_val):
    return gelu(gate_val) * up_val


def forward_product(left, weight):
    return jnp.dot(left, weight, preferred_element_type=F32)


def back_product(grad, weight):
    return lax.dot_general(grad, weight, (((2,), (1,)), ((), ())), preferred_element_type=F32)


def token_product(left, grad):
    return lax.dot_general(left, grad, (((0, 1), (0, 1)), ((), ())), preferred_element_type=F32)


def to_seq(parts):
    return lax.all_to_all(parts, "seq", split_axis=0, concat_axis=0, tiled=True)


def gather(value, axis):
    return lax.all_gather(value, axis, axis=0, tiled=True)


def scatter(value, axis):
    return lax.psum_scatter(value.astype(BF), axis, scatter_dimension=0, tiled=True)


MESH = pl.DeviceIdType.MESH
TILE = 128
LAP = 16


def greet(axis, count, mine):
    barrier = pltpu.get_barrier_semaphore()
    for d in range(1, count):
        pl.semaphore_signal(
            barrier, inc=1, device_id={axis: lax.rem(mine + d, count)}, device_id_type=MESH
        )
    pl.semaphore_wait(barrier, count - 1)


def remote(src, dst, send, recv, axis, to):
    return pltpu.make_async_remote_copy(
        src_ref=src, dst_ref=dst, send_sem=send, recv_sem=recv, device_id={axis: to}, device_id_type=MESH
    )


def minus_expm1(x, whole):
    series = 1.0 + x * (1.0 / 7)
    for n in (6, 5, 4, 3, 2):
        series = 1.0 + x * (1.0 / n) * series
    return jnp.where(x > -0.5, -x * series, 1.0 - whole)


def gelu_parts(v):
    inner = 0.7978845608028654 * (v + 0.044715 * (v * v * v))
    th = jnp.tanh(inner)
    value = 0.5 * v * (1.0 + th)
    slope = 0.5 * (1.0 + th) + 0.5 * v * (1.0 - th * th) * 0.7978845608028654 * (
        1.0 + 3 * 0.044715 * (v * v)
    )
    return value, slope


def dot(a, b, dims=((1,), (0,))):
    return lax.dot_general(a, b, (dims, ((), ())), preferred_element_type=F32)


LANE = 128


def wide(ref, rows, col):
    return jnp.concatenate([ref[c, rows, :] for c in range(col // LANE, (col + BW) // LANE)], axis=1)


def put_wide(ref, rows, col, value):
    for c in range(BW // LANE):
        ref[col // LANE + c, rows, :] = value[:, c * LANE : (c + 1) * LANE]


def over_tiles(S, L, C, step):
    per = L // TILE

    @pl.loop(0, S * per)
    def _(i):
        for col in range(0, C, BW):
            step(i // per, pl.multiple_of(lax.rem(i, per) * TILE, TILE), col)


def recur_forward(
    T, S, L, C, xy_ref, rows_ref, wd_ref, wi_ref,
    mixed_ref, states_ref, conv_ref, x_ref, halo_ref, inc_ref,
    a_s, b_s, ext_s, fin_s, got_s, halo_send, halo_recv, send_sem, recv_sem,
):
    t = lax.axis_index("tok")
    SL = S * L // 8
    half = 8 // S
    greet("tok", T, t)
    for q in range(S):
        x_ref[q, L - LAP : L, :] = xy_ref[q, L - LAP : L, 0:C].astype(BF)
    lap = remote(x_ref.at[:, pl.ds(L - LAP, LAP), :], halo_ref, halo_send, halo_recv, "tok", lax.rem(t + 1, T))

    @pl.when(t < T - 1)
    def _():
        lap.start()

    @pl.when(t > 0)
    def _():
        lap.wait_recv()

    @pl.when(t == 0)
    def _():
        halo_ref[...] = jnp.zeros_like(halo_ref)

    def make(q, r0, col):
        cs = pl.ds(col, BW)

        @pl.when(r0 == 0)
        def _():
            ext_s[0:8, cs] = halo_ref[q, :, cs].astype(F32)[8:16]

        @pl.when(r0 > 0)
        def _():
            ext_s[0:8, cs] = ext_s[TILE : TILE + 8, cs]

        low_x = xy_ref[q, pl.ds(r0, TILE), cs].astype(BF)

        @pl.when(r0 < L - TILE)
        def _():
            x_ref[q, pl.ds(r0, TILE), cs] = low_x

        @pl.when(r0 == L - TILE)
        def _():
            x_ref[q, L - TILE : L - LAP, cs] = low_x[: TILE - LAP]

        ext_s[8 : 8 + TILE, cs] = low_x.astype(F32)
        conv = rows_ref[4:5, cs] + jnp.zeros((TILE, BW), F32)
        for k in range(CONV):
            conv = conv + ext_s[5 + k : 5 + k + TILE, cs] * rows_ref[k : k + 1, cs]
        low = conv.astype(BF)
        conv_ref[q, pl.ds(r0, TILE), cs] = low
        vals = low.astype(F32)
        gate = dot(low, wd_ref[cs, :]) + rows_ref[5:6, cs]
        inp = dot(low, wi_ref[cs, :]) + rows_ref[6:7, cs]
        log = -jax.nn.sigmoid(gate) * rows_ref[8:9, cs]
        a = jnp.exp(log)
        b = jnp.sqrt(minus_expm1(2.0 * log, a * a)) * jax.nn.sigmoid(inp) * vals
        here = pl.ds(pl.multiple_of(q * L + r0, TILE), TILE)
        put_wide(a_s, here, col, a)
        put_wide(b_s, here, col, b)

    over_tiles(S, L, C, make)

    NC = C // LANE

    def walk(i, carry):
        at = pl.ds(i, 8, stride=SL)
        out = []
        for c, (h, p) in enumerate(carry):
            a = a_s[c, at, :]
            h = a * h + b_s[c, at, :]
            p = a * p
            a_s[c, at, :] = p
            b_s[c, at, :] = h
            out.append((h, p))
        return tuple(out)

    start = tuple((jnp.zeros((8, LANE), F32), jnp.ones((8, LANE), F32)) for _ in range(NC))
    for c, (h, p) in enumerate(lax.fori_loop(0, SL, walk, start, unroll=4)):
        fin_s[c, 0:8, :] = p
        fin_s[c, 8:16, :] = h

    def ship(j, _):
        remote(fin_s, got_s.at[t], send_sem.at[j], recv_sem.at[t], "tok", j).start()
        return 0

    lax.fori_loop(t + 1, T, ship, 0)

    def fold(j, incs):
        remote(fin_s, got_s.at[j], send_sem.at[j], recv_sem.at[j], "tok", t).wait_recv()
        out = []
        for c, inc in enumerate(incs):
            for k in range(half):
                pj = got_s[j, c, pl.ds(k, S, stride=half), :]
                hj = got_s[j, c, pl.ds(8 + k, S, stride=half), :]
                inc = pj * inc + hj
            out.append(inc)
        return tuple(out)

    for c, inc in enumerate(lax.fori_loop(0, t, fold, tuple(jnp.zeros((S, LANE), F32) for _ in range(NC)))):
        for k in range(half):
            inc_ref[c, pl.ds(k, S, stride=half), :] = inc
            if k < half - 1:
                inc = fin_s[c, pl.ds(k, S, stride=half), :] * inc + fin_s[c, pl.ds(8 + k, S, stride=half), :]

    def finish(q, r0, col):
        cs = pl.ds(col, BW)
        row = q * L + r0
        here = pl.ds(pl.multiple_of(row, TILE), TILE)
        st = wide(b_s, here, col) + wide(a_s, here, col) * wide(inc_ref, pl.ds(row // SL, 1), col)
        states_ref[here, cs] = st
        value, _ = gelu_parts(xy_ref[q, pl.ds(r0, TILE), pl.ds(C + col, BW)])
        mixed_ref[here, cs] = (st * value).astype(BF)

    over_tiles(S, L, C, finish)

    def drain(j, _):
        remote(fin_s, got_s.at[t], send_sem.at[j], recv_sem.at[t], "tok", j).wait_send()
        return 0

    lax.fori_loop(t + 1, T, drain, 0)

    @pl.when(t < T - 1)
    def _():
        lap.wait_send()


def recur_backward(
    T, S, L, C, gm_ref, xy_ref, st_ref, conv_ref, x_ref, halo_ref, inc_ref, rows_ref, wd_ref, wi_ref,
    gxy_ref, gwd_ref, gwi_ref, small_ref,
    a_s, g_s, r_s, sg_s, si_s, gc_s, ext_s, pst_s, fin_s, got_s, car_s, lap_send, lap_recv, send_sem, recv_sem,
):
    t = lax.axis_index("tok")
    SL = S * L // 8
    half = 8 // S
    greet("tok", T, t)

    def prepare(q, r0, col):
        cs = pl.ds(col, BW)
        here = pl.ds(pl.multiple_of(q * L + r0, TILE), TILE)
        low = conv_ref[q, pl.ds(r0, TILE), cs]
        sg = jax.nn.sigmoid(dot(low, wd_ref[cs, :]) + rows_ref[5:6, cs])
        sg_s[here, cs] = sg
        si_s[here, cs] = jax.nn.sigmoid(dot(low, wi_ref[cs, :]) + rows_ref[6:7, cs])
        put_wide(a_s, here, col, jnp.exp(-sg * rows_ref[8:9, cs]))
        value, slope = gelu_parts(xy_ref[q, pl.ds(r0, TILE), pl.ds(C + col, BW)])
        gm = gm_ref[here, cs]
        put_wide(g_s, here, col, gm * value)
        gxy_ref[q, pl.ds(r0, TILE), pl.ds(C + col, BW)] = (gm * st_ref[here, cs] * slope).astype(BF)

    over_tiles(S, L, C, prepare)

    NC = C // LANE

    def walk(i, carry):
        at = pl.ds(SL - 1 - i, 8, stride=SL)
        out = []
        for c, (e, r) in enumerate(carry):
            a = a_s[c, at, :]
            adj = g_s[c, at, :] + e
            g_s[c, at, :] = adj
            r_s[c, at, :] = r
            out.append((a * adj, a * r))
        return tuple(out)

    start = tuple((jnp.zeros((8, LANE), F32), jnp.ones((8, LANE), F32)) for _ in range(NC))
    for c, (e, r) in enumerate(lax.fori_loop(0, SL, walk, start, unroll=4)):
        fin_s[c, 0:8, :] = r
        fin_s[c, 8:16, :] = e

    def ship(j, _):
        remote(fin_s, got_s.at[t], send_sem.at[j], recv_sem.at[t], "tok", j).start()
        return 0

    lax.fori_loop(0, t, ship, 0)

    def fold(i, cars):
        j = T - 1 - i
        remote(fin_s, got_s.at[j], send_sem.at[j], recv_sem.at[j], "tok", t).wait_recv()
        out = []
        for c, car in enumerate(cars):
            for k in reversed(range(half)):
                rj = got_s[j, c, pl.ds(k, S, stride=half), :]
                ej = got_s[j, c, pl.ds(8 + k, S, stride=half), :]
                car = rj * car + ej
            out.append(car)
        return tuple(out)

    for c, car in enumerate(lax.fori_loop(0, T - 1 - t, fold, tuple(jnp.zeros((S, LANE), F32) for _ in range(NC)))):
        for k in reversed(range(half)):
            car_s[c, pl.ds(k, S, stride=half), :] = car
            if k > 0:
                car = fin_s[c, pl.ds(k, S, stride=half), :] * car + fin_s[c, pl.ds(8 + k, S, stride=half), :]

    small_ref[...] = jnp.zeros_like(small_ref)
    gwd_ref[...] = jnp.zeros_like(gwd_ref)
    gwi_ref[...] = jnp.zeros_like(gwi_ref)

    def add_row(k, cs, value):
        small_ref[k : k + 1, cs] += jnp.sum(value, axis=0, keepdims=True)

    def chain(q, r0, col):
        cs = pl.ds(col, BW)
        row = q * L + r0
        here = pl.ds(pl.multiple_of(row, TILE), TILE)

        @pl.when(r0 == 0)
        def _():
            pst_s[0:8, cs] = wide(inc_ref, pl.ds(q * half, 1), col) + jnp.zeros((8, BW), F32)

        @pl.when(r0 > 0)
        def _():
            pst_s[0:8, cs] = pst_s[TILE : TILE + 8, cs]

        pst_s[8 : 8 + TILE, cs] = st_ref[here, cs]
        adj = wide(g_s, here, col) + wide(r_s, here, col) * wide(car_s, pl.ds(row // SL, 1), col)
        sg, si, a = sg_s[here, cs], si_s[here, cs], wide(a_s, here, col)
        low = conv_ref[q, pl.ds(r0, TILE), cs]
        vals = low.astype(F32)
        sp = rows_ref[8:9, cs]
        square = a * a
        scale = jnp.sqrt(minus_expm1(-2.0 * sg * sp, square))
        grad_log = adj * pst_s[7 : 7 + TILE, cs] * a - adj * si * vals * square / scale
        grad_gate = (-grad_log * sp * sg * (1.0 - sg)).astype(BF)
        add_row(7, cs, -grad_log * sg)
        grad_inp = (adj * scale * vals * si * (1.0 - si)).astype(BF)
        add_row(5, cs, grad_gate.astype(F32))
        add_row(6, cs, grad_inp.astype(F32))
        gc = (
            adj * scale * si
            + dot(grad_gate, wd_ref[cs, :], ((1,), (1,)))
            + dot(grad_inp, wi_ref[cs, :], ((1,), (1,)))
        )
        gc_s[q, pl.ds(r0, TILE), cs] = gc
        add_row(4, cs, gc)
        gwd_ref[cs, :] += dot(low, grad_gate, ((0,), (0,)))
        gwi_ref[cs, :] += dot(low, grad_inp, ((0,), (0,)))

    over_tiles(S, L, C, chain)
    small_ref[7:8, :] *= 8.0 * rows_ref[9:10, :]

    lap = remote(gc_s.at[:, pl.ds(0, 8), :], gc_s.at[:, pl.ds(L, 8), :], lap_send, lap_recv, "tok", lax.rem(t + T - 1, T))

    @pl.when(t > 0)
    def _():
        lap.start()

    @pl.when(t < T - 1)
    def _():
        lap.wait_recv()

    @pl.when(t == T - 1)
    def _():
        gc_s[:, pl.ds(L, 8), :] = jnp.zeros((S, 8, C), F32)

    def taps(q, r0, col):
        cs = pl.ds(col, BW)

        @pl.when(r0 == 0)
        def _():
            ext_s[0:8, cs] = halo_ref[q, :, cs].astype(F32)[8:16]

        @pl.when(r0 > 0)
        def _():
            ext_s[0:8, cs] = ext_s[TILE : TILE + 8, cs]

        ext_s[8 : 8 + TILE, cs] = x_ref[q, pl.ds(r0, TILE), cs].astype(F32)
        pst_s[0 : TILE + 8, cs] = gc_s[q, pl.ds(r0, TILE + 8), cs]
        gc = pst_s[0:TILE, cs]
        gx = jnp.zeros((TILE, BW), F32)
        for k in range(CONV):
            add_row(k, cs, gc * ext_s[5 + k : 5 + k + TILE, cs])
            gx = gx + pst_s[3 - k : 3 - k + TILE, cs] * rows_ref[k : k + 1, cs]
        gxy_ref[q, pl.ds(r0, TILE), cs] = gx.astype(BF)

    over_tiles(S, L, C, taps)

    def drain(j, _):
        remote(fin_s, got_s.at[t], send_sem.at[j], recv_sem.at[t], "tok", j).wait_send()
        return 0

    lax.fori_loop(0, t, drain, 0)

    @pl.when(t > 0)
    def _():
        lap.wait_send()


VM = pl.BlockSpec(memory_space=pltpu.VMEM)


def shape(dims, kind=F32):
    return jax.ShapeDtypeStruct(dims, kind)


def params(collective_id, mib=58):
    return pltpu.CompilerParams(
        collective_id=collective_id, has_side_effects=True, vmem_limit_bytes=mib * 1024 * 1024
    )


def run_forward(T, branches, rows, wd, wi):
    S, L, C = branches.shape
    C //= 2
    M = S * L
    dma = pltpu.SemaphoreType.DMA
    split = pltpu.VMEM((C // LANE, M, LANE), F32)
    return pl.pallas_call(
        functools.partial(recur_forward, T, S, L, C),
        out_shape=(
            shape((M, C), BF),
            shape((M, C)),
            shape((S, L, C), BF),
            shape((S, L, C), BF),
            shape((S, LAP, C), BF),
            shape((C // LANE, 8, LANE)),
        ),
        in_specs=[VM] * 4,
        out_specs=(VM,) * 6,
        scratch_shapes=[
            split,
            split,
            pltpu.VMEM((TILE + 8, C), F32),
            pltpu.VMEM((C // LANE, 16, LANE), F32),
            pltpu.VMEM((T, C // LANE, 16, LANE), F32),
            dma,
            dma,
            dma((T,)),
            dma((T,)),
        ],
        compiler_params=params(0),
        cost_estimate=pl.CostEstimate(flops=4 * M * C * BW, bytes_accessed=100000000, transcendentals=6 * M * C),
    )(branches, rows, wd, wi)


def run_backward(T, grad_mixed, branches, states, conv, branch_x, halo, inc, rows, wd, wi):
    S, L, C = branch_x.shape
    M = S * L
    dma = pltpu.SemaphoreType.DMA
    big = pltpu.VMEM((M, C), F32)
    split = pltpu.VMEM((C // LANE, M, LANE), F32)
    return pl.pallas_call(
        functools.partial(recur_backward, T, S, L, C),
        out_shape=(shape((S, L, 2 * C), BF), shape((C, BW)), shape((C, BW)), shape((8, C))),
        in_specs=[VM] * 10,
        out_specs=(VM,) * 4,
        scratch_shapes=[split] * 3
        + [big] * 2
        + [
            pltpu.VMEM((S, L + 8, C), F32),
            pltpu.VMEM((TILE + 8, C), F32),
            pltpu.VMEM((TILE + 8, C), F32),
            pltpu.VMEM((C // LANE, 16, LANE), F32),
            pltpu.VMEM((T, C // LANE, 16, LANE), F32),
            pltpu.VMEM((C // LANE, 8, LANE), F32),
            dma,
            dma,
            dma((T,)),
            dma((T,)),
        ],
        compiler_params=params(1),
        cost_estimate=pl.CostEstimate(flops=12 * M * C * BW, bytes_accessed=180000000, transcendentals=6 * M * C),
    )(grad_mixed, branches, states, conv, branch_x, halo, inc, rows, wd, wi)


CHUNKS = 4


def root_scale(v):
    return lax.rsqrt(jnp.mean(v * v, axis=-1, keepdims=True) + eps)


def rms_back(v, gain, grad):
    scale = root_scale(v)
    hat = v * scale
    inner = grad * gain
    return scale * (inner - hat * jnp.mean(inner * hat, axis=-1, keepdims=True)), grad * hat


def flip(me, bit):
    return me + bit - 2 * bit * lax.rem(me // bit, 2)


def plane_sum(kind, L, D, *refs):
    shares = kind in ("first", "second")
    part = refs[0]
    if kind == "first":
        tokens, gain, keep, everyone = refs[1:5]
        rest = refs[5:]
    elif kind == "second":
        resid, gain, cot, weight, keep, gain_grad, everyone = refs[1:8]
        rest = refs[8:]
    elif kind == "third":
        tokens, gain, before, keep = refs[1:5]
        rest = refs[5:]
    else:
        resid, keep = refs[1:3]
        rest = refs[3:]
    one_s, two_s, two_out, one_send, one_recv, two_send, two_recv = rest[:7]
    if shares:
        own_s, all_send, all_recv, own_sem = rest[7:]
    me = lax.axis_index("seq")
    H = L // CHUNKS
    px, py = flip(me, 1), flip(me, 2)
    pd = 3 - me
    barrier = pltpu.get_barrier_semaphore()
    for peer in (px, py):
        pl.semaphore_signal(barrier, inc=1, device_id={"seq": peer}, device_id_type=MESH)
    pl.semaphore_wait(barrier, 2)

    def peers(c):
        return (px, py) if c % 2 == 0 else (py, px)

    def rows(c):
        return pl.ds(c * H, H)

    def one(c, k):
        f, _ = peers(c)
        src = (f, pd)[k]
        return remote(part.at[src, rows(c), :], one_s.at[c, k], one_send.at[c, k], one_recv.at[c, k], "seq", f)

    def two(c):
        return remote(two_out.at[c], two_s.at[c], two_send.at[c], two_recv.at[c], "seq", peers(c)[1])

    def share(c, k):
        f, g = peers(c)
        if k == 2:
            place = everyone.at[f, rows(c), :]
            return remote(place, place, all_send.at[c, k], all_recv.at[c, k], "seq", g)
        place = everyone.at[me, rows(c), :]
        return remote(own_s.at[rows(c), :], place, all_send.at[c, k], all_recv.at[c, k], "seq", (f, g)[k])

    def own(c):
        return pltpu.make_async_copy(own_s.at[rows(c), :], everyone.at[me, rows(c), :], own_sem.at[c])

    def middle(c):
        one(c, 1).wait_recv()
        two_out[c] = (part[peers(c)[1], rows(c), :].astype(F32) + one_s[c, 1].astype(F32)).astype(BF)
        two(c).start()

    def finish(c):
        one(c, 0).wait_recv()
        two(c).wait_recv()
        total = part[me, rows(c), :].astype(F32) + one_s[c, 0].astype(F32) + two_s[c].astype(F32)
        r = rows(c)
        if kind == "first":
            total = tokens[r, :].astype(F32) + total
            keep[r, :] = total
            own_s[r, :] = (total * root_scale(total) * gain[0:1, :]).astype(BF)
        elif kind == "second":
            back, gg = rms_back(resid[r, :], gain[0:1, :], total)
            gg = jnp.sum(gg, axis=0, keepdims=True)
            gain_grad[0:1, :] = gg if c == 0 else gain_grad[0:1, :] + gg
            total = cot[r, :].astype(F32) * weight[0:1, 0:1] + back
            keep[r, :] = total
            own_s[r, :] = total.astype(BF)
        elif kind == "third":
            back, _ = rms_back(tokens[r, :].astype(F32), gain[0:1, :], total)
            keep[r, :] = before[r, :] + back
        else:
            keep[r, :] = (resid[r, :] + total).astype(BF)
        if shares:
            share(c, 0).start()
            share(c, 1).start()
            own(c).start()

    def forward(c):
        share(c, 0).wait_recv()
        share(c, 2).start()

    if kind == "second":
        gain_grad[...] = jnp.zeros_like(gain_grad)
    for c in range(CHUNKS):
        for k in (1, 0):
            one(c, k).start()
    for c in range(CHUNKS):
        middle(c)
        if c > 0:
            finish(c - 1)
        if shares and c > 1:
            forward(c - 2)
    finish(CHUNKS - 1)
    if shares:
        forward(CHUNKS - 2)
        forward(CHUNKS - 1)
    for c in range(CHUNKS):
        for k in (0, 1):
            one(c, k).wait_send()
        two(c).wait_send()
        if shares:
            for k in (1, 2):
                share(c, k).wait_recv()
            for k in (0, 1, 2):
                share(c, k).wait_send()
            own(c).wait()


def run_plane(kind, collective_id, part, *ins):
    S, L, D = part.shape
    H = L // CHUNKS
    dma = pltpu.SemaphoreType.DMA
    shares = kind in ("first", "second")
    outs = [shape((L, D), BF if kind == "out" else F32)]
    specs = [VM]
    if kind == "second":
        outs.append(shape((8, D)))
        specs.append(VM)
    if shares:
        outs.append(shape((S, L, D), BF))
        specs.append(pl.BlockSpec(memory_space=pl.ANY))
    scratch = [
        pltpu.VMEM((CHUNKS, 2, H, D), BF),
        pltpu.VMEM((CHUNKS, H, D), BF),
        pltpu.VMEM((CHUNKS, H, D), BF),
        dma((CHUNKS, 2)),
        dma((CHUNKS, 2)),
        dma((CHUNKS,)),
        dma((CHUNKS,)),
    ]
    if shares:
        scratch += [pltpu.VMEM((L, D), BF), dma((CHUNKS, 3)), dma((CHUNKS, 3)), dma((CHUNKS,))]
    return pl.pallas_call(
        functools.partial(plane_sum, kind, L, D),
        out_shape=tuple(outs),
        in_specs=[VM] * (1 + len(ins)),
        out_specs=tuple(specs),
        scratch_shapes=scratch,
        compiler_params=params(collective_id, 40),
        cost_estimate=pl.CostEstimate(
            flops=40 * L * D, bytes_accessed=(240 if shares else 120) * 1000000, transcendentals=L
        ),
    )(part, *ins)


def plane_swap(modes, *refs):
    n = len(modes)
    ins, outs = refs[:n], refs[n : 2 * n]
    send, recv, own_sem = refs[2 * n :]
    me = lax.axis_index("seq")
    S = lax.axis_size("seq")
    greet("seq", S, me)

    def copy(i, d):
        to = lax.rem(me + d, S)
        src = ins[i] if modes[i] == "all" else ins[i].at[to]
        return remote(src, outs[i].at[me], send.at[i, d], recv.at[i, d], "seq", to)

    def own(i):
        src = ins[i] if modes[i] == "all" else ins[i].at[me]
        return pltpu.make_async_copy(src, outs[i].at[me], own_sem.at[i])

    for i in range(n):
        for d in range(1, S):
            copy(i, d).start()
        own(i).start()
    for i in range(n):
        for d in range(1, S):
            copy(i, d).wait()
        own(i).wait()


def run_swap(S, modes, collective_id, *ins):
    n = len(modes)
    dma = pltpu.SemaphoreType.DMA
    outs = tuple(shape(((S,) if m == "all" else ()) + x.shape, x.dtype) for m, x in zip(modes, ins))
    size = sum(3 * x.size * x.dtype.itemsize // (1 if m == "all" else S) for m, x in zip(modes, ins))
    hbm = pl.BlockSpec(memory_space=pl.ANY)
    return pl.pallas_call(
        functools.partial(plane_swap, modes),
        out_shape=outs,
        in_specs=[hbm] * n,
        out_specs=(hbm,) * n,
        scratch_shapes=[dma((n, S)), dma((n, S)), dma((n,))],
        compiler_params=params(collective_id, 4),
        cost_estimate=pl.CostEstimate(flops=0, bytes_accessed=size * 40, transcendentals=0),
    )(*ins)


def plane_fill(S, T, L, slabs, *refs):
    pack, first, second, gates = refs[:4]
    pack_out, first_out, second_out, gates_out, lent = refs[4:9]
    pack_send, pack_recv, row_send, row_recv, gate_send, gate_recv, lent_send, lent_recv, own_sem = refs[9:]
    me, t = lax.axis_index("seq"), lax.axis_index("tok")
    px, py, pd = flip(me, 1), flip(me, 2), S - 1 - me
    H = L // CHUNKS
    barrier = pltpu.get_barrier_semaphore()
    for peer in (px, py, pd):
        pl.semaphore_signal(barrier, inc=1, device_id={"seq": peer}, device_id_type=MESH)

    @pl.loop(1, T)
    def _(d):
        pl.semaphore_signal(barrier, inc=1, device_id={"tok": lax.rem(t + d, T)}, device_id_type=MESH)

    pl.semaphore_wait(barrier, S - 1 + T - 1)

    def gate(d):
        return remote(gates, gates_out.at[t], gate_send.at[d], gate_recv.at[d], "tok", lax.rem(t + d, T))

    def piece(k):
        to = (pd, px, py)[k]
        return remote(pack.at[to], pack_out.at[me], pack_send.at[k], pack_recv.at[k], "seq", to)

    def row(a, c, k):
        src, out = ((first, first_out), (second, second_out))[a]
        f, g = (px, py) if c % 2 == 0 else (py, px)
        rows = pl.ds(c * H, H)
        sems = row_send.at[a, c, k], row_recv.at[a, c, k], "seq"
        if k == 2:
            place = out.at[f, rows, :]
            return remote(place, place, *sems, g)
        return remote(src.at[rows, :], out.at[me, rows, :], *sems, (f, g)[k])

    mine = [
        pltpu.make_async_copy(pack.at[me], pack_out.at[me], own_sem.at[0]),
        pltpu.make_async_copy(first, first_out.at[me], own_sem.at[1]),
        pltpu.make_async_copy(second, second_out.at[me], own_sem.at[2]),
        pltpu.make_async_copy(gates, gates_out.at[t], own_sem.at[3]),
    ]
    loan = remote(gates_out.at[pl.ds(0, slabs)], lent, lent_send, lent_recv, "seq", px)

    @pl.loop(1, T)
    def _(d):
        gate(d).start()

    for k in range(3):
        piece(k).start()
    for copy in mine:
        copy.start()
    for k in (0, 1):
        for c in range(CHUNKS):
            row(0, c, k).start()
    mine[3].wait()

    @pl.loop(1, T)
    def _(d):
        gate(d).wait_recv()

    @pl.when(lax.rem(me, 2) == 1)
    def _():
        loan.start()

    for c in range(CHUNKS):
        row(0, c, 0).wait_recv()
        row(0, c, 2).start()
    for k in (0, 1):
        for c in range(CHUNKS):
            row(1, c, k).start()
    for c in range(CHUNKS):
        row(1, c, 0).wait_recv()
        row(1, c, 2).start()
    for k in range(3):
        piece(k).wait()
    for a in (0, 1):
        for c in range(CHUNKS):
            row(a, c, 0).wait_send()
            row(a, c, 1).wait()
            row(a, c, 2).wait()
    for copy in mine[:3]:
        copy.wait()

    @pl.loop(1, T)
    def _(d):
        gate(d).wait_send()

    @pl.when(lax.rem(me, 2) == 1)
    def _():
        loan.wait_send()

    @pl.when(lax.rem(me, 2) == 0)
    def _():
        loan.wait_recv()


def run_fill(S, T, slabs, collective_id, pack, first, second, gates):
    L = first.shape[0]
    dma = pltpu.SemaphoreType.DMA
    hbm = pl.BlockSpec(memory_space=pl.ANY)
    return pl.pallas_call(
        functools.partial(plane_fill, S, T, L, slabs),
        out_shape=(
            shape(pack.shape, BF),
            shape((S,) + first.shape, BF),
            shape((S,) + second.shape, BF),
            shape((T,) + gates.shape, BF),
            shape((slabs,) + gates.shape, BF),
        ),
        in_specs=[hbm] * 4,
        out_specs=(hbm,) * 5,
        scratch_shapes=[
            dma((3,)),
            dma((3,)),
            dma((2, CHUNKS, 3)),
            dma((2, CHUNKS, 3)),
            dma((T,)),
            dma((T,)),
            dma,
            dma,
            dma((4,)),
        ],
        compiler_params=params(collective_id, 4),
        cost_estimate=pl.CostEstimate(flops=0, bytes_accessed=320000000, transcendentals=0),
    )(pack, first, second, gates)


def after(value, *others):
    return lax.optimization_barrier((value,) + others)[0]


def body(
    tokens,
    source_ids,
    loss_weights,
    grad_output,
    first_gain,
    input_weight,
    gelu_weight,
    conv_weight,
    conv_bias,
    decay_gate,
    decay_bias,
    input_gate,
    input_bias,
    decay_param,
    output_weight,
    second_gain,
    gate_weight,
    up_weight,
    down_weight,
):
    S, T = lax.axis_size("seq"), lax.axis_size("tok")
    me = lax.axis_index("seq")
    length, D = tokens.shape[1:]
    ds, R = input_weight.shape
    rs = output_weight.shape[0]
    F = gate_weight.shape[1]
    FQ = F // S
    heads = R // BW
    starts = [-(-i * heads // S) for i in range(S + 1)]
    C = max(starts[i + 1] - starts[i] for i in range(S)) * BW
    quarter = R // S
    offs = [starts[i] * BW - i * quarter for i in range(S)] + [0]
    most = max(offs)
    off = sum(jnp.where(me == i, offs[i], 0) for i in range(S))
    own = sum(jnp.where(me == i, (starts[i + 1] - starts[i]) * BW, 0) for i in range(S))

    def cols_for(w):
        parts = [w[:, starts[i] * BW : starts[i + 1] * BW] for i in range(S)]
        return jnp.stack([jnp.pad(p, ((0, 0), (0, C - p.shape[1]))) for p in parts])

    def d_rows(w):
        return lax.all_gather(w, "tok", axis=1, tiled=True).reshape((D, w.shape[-1]))

    def d_scatter(g):
        return lax.psum_scatter(g.reshape(S, T * ds, g.shape[-1]), "tok", scatter_dimension=1, tiled=True)

    def r_align(g):
        g = lax.dynamic_update_slice_in_dim(jnp.zeros((quarter + 2 * most, g.shape[1]), BF), g.astype(BF), off, axis=0)
        back = from_behind(g[quarter : quarter + most], "seq", 1)
        keep = lax.broadcasted_iota(jnp.int32, (quarter, 1), 0) < off
        return jnp.where(keep, jnp.pad(back, ((0, quarter - most), (0, 0))), g[:quarter])

    small = jnp.concatenate(
        [conv_weight, jnp.stack([conv_bias, decay_bias, input_bias, decay_param], axis=1)], axis=1
    )
    small = jnp.pad(small, ((0, 0), (0, SMALL - small.shape[1])))
    gates = jnp.concatenate([decay_gate, input_gate, small], axis=1)
    gains = jnp.pad(jnp.stack([first_gain, second_gain], axis=1), ((0, 0), (0, SMALL - 2)))
    pack_in = jnp.concatenate(
        [cols_for(input_weight), cols_for(gelu_weight), jnp.broadcast_to(gains, (S,) + gains.shape)], axis=2
    )
    (pack_in,) = run_swap(S, ("slice",), 2, pack_in)
    sources = lax.broadcasted_iota(jnp.int32, (1, loss_weights.shape[0]), 1)
    picked = jnp.sum(jnp.where(source_ids[:, None] == sources, loss_weights[None, :], 0.0), axis=1)
    cot_low = (grad_output[0].astype(F32) * picked[:, None]).astype(BF)
    pack_f = jnp.concatenate([w.reshape(ds, S, FQ).swapaxes(0, 1) for w in (gate_weight, up_weight)], axis=2)
    pack_f, everyone, cot_low, gates, lent = run_fill(
        S, T, -(-most // rs), 3, after(pack_f, pack_in), tokens[0], cot_low, gates
    )

    def r_rows(whole, lent):
        lent = lent[:most]
        whole = jnp.concatenate([whole, lent, jnp.zeros_like(lent)], axis=0)
        whole = lax.dynamic_slice_in_dim(whole, off, C, axis=0)
        return jnp.where(lax.broadcasted_iota(jnp.int32, whole.shape, 0) < own, whole, 0)

    output_weight = after(output_weight, pack_in)
    pack_in = d_rows(pack_in)
    weight_xy = pack_in[:, : 2 * C]
    gain_one, gain_two = pack_in[:, 2 * C].astype(F32), pack_in[:, 2 * C + 1].astype(F32)
    gates = r_rows(gates.reshape(quarter, -1), lent.reshape(-1, lent.shape[-1]))
    weight_decay, weight_input = gates[:, :BW], gates[:, BW : 2 * BW]
    rows = gates[:, 2 * BW : 2 * BW + 8].T.astype(F32)
    param = rows[7:8]
    rows = jnp.concatenate(
        [rows, 8.0 * jax.nn.softplus(param), jax.nn.sigmoid(param), jnp.zeros((6, C), F32)], axis=0
    )
    weight_out = gather(output_weight, "tok")
    weight_out = r_rows(weight_out, from_behind(weight_out[:most], "seq", -1))

    pack_f = d_rows(after(pack_f, pack_in))
    weight_gate, weight_up = pack_f[:, :FQ], pack_f[:, FQ:]

    everyone = everyone.astype(F32)
    normed = lax.optimization_barrier(rms_scale(everyone, gain_one).astype(BF))
    branches = forward_product(normed, weight_xy)
    weight_down = gather(after(down_weight, branches), "tok")
    mixed, states, conv_low, branch_x, halo, incoming = run_forward(T, branches, rows, weight_decay, weight_input)
    mixed = mixed.reshape(S, length, C)
    passed = from_behind(mixed[:, :, quarter:], "seq", 1)
    mixed_own = jnp.pad(mixed, ((0, 0), (0, 0), (most, 0)))[:, :, :quarter]
    mixed_own = jnp.where(off > 0, mixed_own, mixed[:, :, :quarter])
    mixed_own = jnp.where(
        lax.broadcasted_iota(jnp.int32, (1, 1, quarter), 2) < off,
        jnp.pad(passed, ((0, 0), (0, 0), (0, quarter - most))),
        mixed_own,
    )
    part = forward_product(mixed, weight_out).astype(BF)
    resid, second_normed = run_plane("first", 4, part, tokens[0], gain_two[None])

    gate_val = forward_product(second_normed, weight_gate)
    up_val = forward_product(second_normed, weight_up)
    hidden = gelu_product(gate_val, up_val).astype(BF)
    grad_down = token_product(hidden, cot_low).astype(BF)
    weight_down = after(weight_down, grad_down)
    grad_down = scatter(grad_down, "tok").astype(F32)

    grad_hidden = back_product(cot_low, weight_down)
    _, hidden_pull = jax.vjp(gelu_product, gate_val, up_val)
    grad_gate_val, grad_up_val = hidden_pull(grad_hidden)
    grad_gate_low, grad_up_low = grad_gate_val.astype(BF), grad_up_val.astype(BF)
    grad_gate_w = token_product(second_normed, grad_gate_low).astype(BF)
    grad_up_w = token_product(second_normed, grad_up_low).astype(BF)
    grad_gate_low, grad_up_low, _, _ = lax.optimization_barrier((grad_gate_low, grad_up_low, grad_gate_w, grad_up_w))
    grad_second = back_product(grad_gate_low, weight_gate) + back_product(grad_up_low, weight_up)
    grad_second = after(grad_second.astype(BF), grad_down)
    grad_gate_w = d_scatter(grad_gate_w)
    grad_up_w = d_scatter(grad_up_w)
    picked = jnp.broadcast_to(picked[None], (8, 128))
    grad_resid, grad_gain_two, resid_low = run_plane(
        "second", 6, grad_second, resid, gain_two[None], grad_output[0], picked
    )
    grad_gain_two = grad_gain_two[0]

    def whole_rows(parts):
        return to_seq(parts).swapaxes(0, 1).reshape(ds, F).astype(F32)

    grad_out_w = token_product(mixed_own, resid_low).astype(BF)
    grad_mixed = back_product(after(resid_low, grad_out_w, grad_gate_w), weight_out)
    grad_out_w = scatter(grad_out_w, "tok").astype(F32)
    grad_xy, grad_decay_w, grad_input_w, smalls = run_backward(
        T, grad_mixed.reshape(S * length, C), branches, states, conv_low, branch_x, halo, incoming, rows,
        weight_decay, weight_input,
    )
    grad_i = token_product(normed, after(grad_xy, grad_up_w)).astype(BF)
    smalls = jnp.pad(smalls.T, ((0, 0), (0, BW - 8)))
    grad_r = r_align(jnp.concatenate([grad_decay_w, grad_input_w, smalls], axis=1))
    grad_normed = back_product(after(grad_xy, grad_i), weight_xy)
    grad_normed = after(grad_normed, grad_out_w)
    hat = everyone * root_scale(everyone)
    gains = jnp.stack([jnp.sum(grad_normed * hat, axis=(0, 1)), grad_gain_two], axis=0).astype(BF)

    block = [p.reshape(T, rs, BW) for p in (grad_r[:, :BW], grad_r[:, BW : 2 * BW], grad_r[:, 2 * BW :])]
    gains = gains.reshape(2, S, T, ds).transpose(2, 0, 1, 3).reshape(T, 2, S * ds)
    tall = 3 * rs + 2 + -(3 * rs + 2) % (S * ds)
    across = tall // (S * ds)
    block = jnp.concatenate(block + [jnp.pad(gains, ((0, 0), (0, tall - 3 * rs - 2), (0, BW - S * ds)))], axis=1)
    block = block.reshape(T, S, ds, across, BW).transpose(1, 0, 2, 3, 4).reshape(D, across * BW)
    grad_i = jnp.concatenate([grad_i, block], axis=1)
    (grad_tokens,) = run_plane("third", 7, grad_normed.astype(BF), tokens[0], gain_one[None], grad_resid)
    part = forward_product(hidden, weight_down).astype(BF)
    (block_out,) = run_plane("out", 5, part, resid)
    grad_i = d_scatter(grad_i)
    block = grad_i[:, :, 2 * C :].reshape(tall, BW).astype(F32)
    grad_r = [block[i * rs : (i + 1) * rs] for i in range(3)]
    gains = block[3 * rs : 3 * rs + 2, : S * ds].reshape(2, S, ds).transpose(1, 2, 0)
    gains = jnp.pad(gains.astype(BF), ((0, 0), (0, 0), (0, SMALL - 2)))
    grad_i = to_seq(jnp.concatenate([grad_i[:, :, : 2 * C], gains], axis=2)).astype(F32)
    gain_grads = jnp.sum(grad_i[:, :, 2 * C : 2 * C + 2], axis=0)

    def columns(at):
        return jnp.concatenate(
            [grad_i[i, :, at : at + (starts[i + 1] - starts[i]) * BW] for i in range(S)], axis=1
        )

    smalls = grad_r[2]
    return (
        block_out[None],
        grad_tokens[None],
        gain_grads[:, 0],
        columns(0),
        columns(C),
        smalls[:, :CONV],
        smalls[:, 4],
        grad_r[0],
        smalls[:, 5],
        grad_r[1],
        smalls[:, 6],
        smalls[:, 7],
        grad_out_w,
        gain_grads[:, 1],
        whole_rows(grad_gate_w),
        whole_rows(grad_up_w),
        grad_down,
    )


def solution(mesh):
    one, two = P(("seq", "tok")), P(("seq", "tok"), None)
    data = P("seq", "tok", None)
    return jax.shard_map(
        body,
        mesh=mesh,
        in_specs=(data, P("seq"), P(), data, one, two, two, two, one, two, one, two, one, one, two, one, two, two, two),
        out_specs=(data, data, one, two, two, two, one, two, one, two, one, one, two, one, two, two, two),
        check_vma=False,
    )
```

time: 1820 us -> 784 us (0.43)
  waiting for transfers between devices: 789 us -> 44.2 us
  local copies, waits for them, and re-layouts: 522 us -> 52.9 us
  Pallas kernels: 0 us -> 440 us
  other arithmetic: 173 us -> 43.6 us
  blocking collectives: 100 us -> 0 us
  matrix products: 177 us -> 156 us
    pallas_call x0 -> x8, Pallas kernels: none -> 440 us  [the longest x4 227 us: run_plane(): pl.pallas_call(functools.partial(plane_sum, kind, L, D), out_shape=tuple(...]
    all_gather x8 -> x2, waiting for transfers between devices: 400 us -> 19.3 us  [gather(): return lax.all_gather(value, axis, axis=0, tiled=True)]
    slice x120 -> x11, local copies, waits for them, and re-layouts: 318 us -> 6.9 us  [the longest x1 1.18 us: body(): grad_i[:, :, :2 * C]]
    reduce_scatter x5 -> x2, waiting for transfers between devices: 243 us -> 0.75 us  [scatter(): lax.psum_scatter(value.astype(BF), axis, scatter_dimension=0, tiled=True)]
    unnamed x21 -> x9, waiting for transfers between devices: 130 us -> 0.83 us
    pad x56 -> x0, local copies, waits for them, and re-layouts: 67.7 us -> none  [the longest x28 35.4 us: body(): lax.associative_scan(combine, (next_decay, grad_local), axis=1, reverse=T...]
    all_to_all x2 -> x0, blocking collectives: 57.8 us -> none  [the longest x1 40.5 us: body(): lax.all_to_all(pack_f, 'seq', split_axis=1, concat_axis=1, tiled=True)]
    add x48 -> x0, other arithmetic: 55.5 us -> none  [the longest x14 21.6 us: combine(): return (earlier[0] * later[0], later[0] * earlier[1] + later[1])]
  transfers between devices with their start and end apart: 24 -> 15, of which waited for: 18 -> 3; matrix products, arithmetic and copies ran while one was open for 13% -> 26% of each run, Pallas kernels for 0% -> 55%
where the time goes in v2:
time: 784 us; the launch traced here: 775 us
  Pallas kernels  440 us (56%)
  matrix products  156 us (20%)
  local copies, waits for them, and re-layouts  52.9 us (7%)
  waiting for transfers between devices  44.2 us (6%)
  other arithmetic  43.6 us (6%)
  starting transfers between devices  21.3 us (3%)
  between operations  15.8 us (2%)
    pallas_call x4, Pallas kernels, run_plane(): pl.pallas_call(functools.partial(plane_sum, kind, L, D), out_shape=tuple(...  227 us
    pallas_call x1, Pallas kernels, run_fill(): pl.pallas_call(functools.partial(plane_fill, S, T, L, slabs), out_shape=(...  95.5 us
    dot_general x5, matrix products, back_product(): lax.dot_general(grad, weight, (((2,), (1,)), ((), ())), preferred_element...  61.4 us
    pallas_call x1, Pallas kernels, run_backward(): pl.pallas_call(functools.partial(recur_backward, T, S, L, C), out_shape=(...  59.9 us
    dot_general x5, matrix products, token_product(): lax.dot_general(left, grad, (((0, 1), (0, 1)), ((), ())), preferred_eleme...  47.7 us
    dot_general x5, matrix products, forward_product(): return jnp.dot(left, weight, preferred_element_type=F32)  47.2 us
    pallas_call x1, Pallas kernels, run_forward(): pl.pallas_call(functools.partial(recur_forward, T, S, L, C), out_shape=(s...  43.3 us
    unnamed x94, local copies, waits for them, and re-layouts  24.7 us
  transfers between devices with their start and end apart: 15, of which 3 were waited for; matrix products, arithmetic and copies ran while one was open for 26% of the time, Pallas kernels for 55%

profile of v2, /device:TPU:0, one launch (start us, length us, event | category | flops | bytes accessed | tf_op | source)
XLA Modules:
  0.0 774.5 jit_solution(2277918022157943435)
XLA Ops:
  11.3 14.3 %shard_map.314 = bf16[4,64,1664]{2,1,0:T(8,128)(2,1)} custom-call(bf16[4,64,1664]{2,1,0:T(8,128)(2,1)S(1)} %pad_maximum_fusion.2.refs_0_), custom_call_target="tpu_custom_call" | custom-call | bytes 25559040 | tf_op jit(solution)/shard_map/pallas_call | solution.py:690
  28.2 2.1 multiply_convert_fusion.2.refs_2_
  30.3 95.5 %shard_map.315 = (bf16[4,64,3072]{2,1,0:T(8,128)(2,1)S(1)}, bf16[4,256,2048]{2,1,0:T(8,128)(2,1)S(1)}, bf16[4,256,2048]{2,1,0:T(8,128)(2,1)S(1)}, bf16[8,80,640]{2,1,0:T(8,128)(2,1)S(1)}, bf16[2,80,640]{2,1,0:T(8,128)(2,1)S(1)}) custom-call(bf16[4,64,3072]{2,1,0:T(8,128)(2,1)S(1)} %pad_maximum_fusion.1.refs_0_, bf16[256,2048]{1,0:T(8,128)(2,1)S(1)} %bitcast.150, ...), custom_call_target="tpu_custom_call" | custom-call | bytes 320000000 | tf_op jit(solution)/shard_map/pallas_call | solution.py:800
  125.8 2.1 copy-done
  129.7 2.0 copy-done.15
  131.8 3.3 fusion.4
  138.0 2.1 copy-done.22
  141.4 8.6 %fusion.17.xy_ref = f32[4,256,1536]{2,1,0:T(8,128)} fusion(bf16[4,256,2048]{2,1,0:T(8,128)(2,1)S(1)} %fusion.2, bf16[2048,1664]{1,0:T(8,128)(2,1)S(1)} %bitcast.180), kind=kOutput, calls=%fused_computation.34 | convolution fusion | flops 6442450944 | bytes 16777216 | tf_op jit(solution)/shard_map/dot_general | solution.py:37
  155.8 43.3 %shard_map.316 = (bf16[1024,768]{1,0:T(8,128)(2,1)}, f32[1024,768]{1,0:T(8,128)}, bf16[4,256,768]{2,1,0:T(8,128)(2,1)}, bf16[4,256,768]{2,1,0:T(8,128)(2,1)}, bf...) custom-call(f32[4,256,1536]{2,1,0:T(8,128)} %fusion.17.xy_ref, f32[16,768]{1,0:T(8,128)} %maximum_maximum_fusion.rows_ref, ...), custom_call_target="tpu_custom_call" | custom-call | flops 805306368 | bytes 100000000 | tf_op jit(solution)/shard_map/pallas_call | solution.py:430
  199.2 5.1 convolution_convert_fusion.refs_0_
  204.3 77.1 %shard_map.317 = (f32[256,2048]{1,0:T(8,128)S(1)}, bf16[4,256,2048]{2,1,0:T(8,128)(2,1)S(1)}) custom-call(bf16[4,256,2048]{2,1,0:T(8,128)(2,1)S(1)} %convolution_convert_fusion.refs_0_, bf16[256,2048]{1,0:T(8,128)(2,1)S(1)} %bitcast.151, f32[1,2048]{1,0:T(1,128)S(1)} %bitcast.159), custom_call_target="tpu_custom_call" | custom-call | flops 20971520 | bytes 240000000 | tf_op jit(solution)/shard_map/pallas_call | solution.py:644
  281.4 2.0 copy-done.17
  283.4 11.9 %fusion.19 = f32[4,256,1536]{2,1,0:T(8,128)} fusion(bf16[4,256,2048]{2,1,0:T(8,128)(2,1)} %copy-done.17, bf16[2048,3072]{1,0:T(8,128)(2,1)} %bitcast.185), kind=kOutput, calls=%fused_computation.36 | convolution fusion | flops 6442450944 | bytes 16777216 | tf_op jit(solution)/shard_map/dot_general | solution.py:37
  295.3 11.7 %multiply_convert_fusion.1 = (bf16[4,256,1536]{2,1,0:T(8,128)(2,1)}, f32[4,256,1536]{2,1,0:T(8,128)}) fusion(f32[4,256,1536]{2,1,0:T(8,128)} %fusion.19, bf16[4,256,2048]{2,1,0:T(8,128)(2,1)S(1)} %copy-done.18, bf16[2048,3072]{1,0:T(8,128)(2,1)S(1)} %bitcast.187), kind=kOutput, calls=%fused_computation.30 | convolution fusion | flops 6458179584 | bytes 26214400 | tf_op jit(solution)/shard_map/dot_general | solution.py:37
  307.0 10.6 %bitcast_convert_fusion.3 = bf16[1536,2048]{1,0:T(8,128)(2,1)} fusion(bf16[4,256,1536]{2,1,0:T(8,128)(2,1)} %get-tuple-element.220, bf16[4,256,2048]{2,1,0:T(8,128)(2,1)S(1)} %copy-done.16), kind=kOutput, calls=%fused_computation.3 | convolution fusion | flops 6445596672 | bytes 13631488 | tf_op jit(solution)/shard_map/dot_general | solution.py:45
  317.6 19.3 %all-gather.11.cloned.1.call-done = bf16[1536,2048]{1,0:T(8,128)(2,1)} async-done(((bf16[192,2048]{1,0:T(8,128)(2,1)}), bf16[1536,2048]{1,0:T(8,128)(2,1)}) %all-gather.11.cloned.1.call-update) | async-done | bytes 6291472 | tf_op jit(solution)/shard_map/all_gather | solution.py:53
  336.9 18.5 %multiply_convert_fusion = (bf16[4,256,1536]{2,1,0:T(8,128)(2,1)}, bf16[4,256,1536]{2,1,0:T(8,128)(2,1)S(1)}) fusion(f32[4,256,1536]{2,1,0:T(8,128)} %fusion.19, f32[4,256,1536]{2,1,0:T(8,128)} %get-tuple-element.221, bf16[4,256,2048]{2,1,0:T(8,128)(2,1)} %copy-done.15, bf16[1536,2048]{1,0:T(8,128)(2,1)} %all-gather.11.cloned.1.call-done), kind=kOutput, calls=%fused_computation.29 | convolution fusion | flops 6480199680 | bytes 29360128 | tf_op jit(solution)/shard_map/dot_general | solution.py:41
  355.4 8.8 %bitcast_convert_fusion.2 = bf16[2048,1536]{1,0:T(8,128)(2,1)} fusion(bf16[4,256,2048]{2,1,0:T(8,128)(2,1)S(1)} %copy-done.19, bf16[4,256,1536]{2,1,0:T(8,128)(2,1)S(1)} %get-tuple-element.62), kind=kOutput, calls=%fused_computation.2 | convolution fusion | flops 6445596672 | bytes 13631488 | tf_op jit(solution)/shard_map/dot_general | solution.py:45
  364.3 11.6 %bitcast_convert_fusion.1 = bf16[2048,1536]{1,0:T(8,128)(2,1)} fusion(bf16[4,256,2048]{2,1,0:T(8,128)(2,1)} %copy-done.17, bf16[4,256,1536]{2,1,0:T(8,128)(2,1)} %get-tuple-element.63), kind=kOutput, calls=%fused_computation.1 | convolution fusion | flops 6445596672 | bytes 13631488 | tf_op jit(solution)/shard_map/dot_general | solution.py:45
  375.9 2.6 copy.172
  379.7 4.5 collective-permute-start.1
  384.1 12.0 %fusion.18 = f32[4,256,2048]{2,1,0:T(8,128)} fusion(bf16[4,256,1536]{2,1,0:T(8,128)(2,1)} %copy-done.40, bf16[2048,3072]{1,0:T(8,128)(2,1)} %bitcast.186), kind=kOutput, calls=%fused_computation.35 | convolution fusion | flops 6442450944 | bytes 17825792 | tf_op jit(solution)/shard_map/dot_general | solution.py:41
  396.1 10.7 %add_convert_fusion.refs_0_ = bf16[4,256,2048]{2,1,0:T(8,128)(2,1)} fusion(f32[4,256,2048]{2,1,0:T(8,128)} %fusion.18, bf16[4,256,1536]{2,1,0:T(8,128)(2,1)S(1)} %copy-done.41, bf16[2048,3072]{1,0:T(8,128)(2,1)S(1)} %bitcast.190), kind=kOutput, calls=%fused_computation.13 | convolution fusion | flops 6446645248 | bytes 22020096 | tf_op jit(solution)/shard_map/dot_general | solution.py:41
  407.5 2.6 convert_element_type.176
  410.8 2.2 copy-done.6
  414.4 71.8 %shard_map.319 = (f32[256,2048]{1,0:T(8,128)S(1)}, f32[8,2048]{1,0:T(8,128)S(1)}, bf16[4,256,2048]{2,1,0:T(8,128)(2,1)S(1)}) custom-call(bf16[4,256,2048]{2,1,0:T(8,128)(2,1)S(1)} %copy-done.6, f32[256,2048]{1,0:T(8,128)S(1)} %get-tuple-element.61.refs_1_, f32[1,2048]{1,0:T(1,128)S(1)} %bitcast.160, bf16[256,2048]{1,0:T(8,128)(2,1)S(1)} %bitcast.155, ...), custom_call_target="tpu_custom_call" | custom-call | flops 20971520 | bytes 240000000 | tf_op jit(solution)/shard_map/pallas_call | solution.py:644
  487.5 1.9 copy-done.20
  489.4 5.3 bitcast_convert_fusion.4
  494.8 8.5 %fusion.50 = f32[4,256,768]{2,1,0:T(8,128)} fusion(bf16[4,256,2048]{2,1,0:T(8,128)(2,1)} %copy-done.20, s32[]{:T(128)S(6)} %select_n.66, bf16[640,2048]{1,0:T(8,128)(2,1)} %all-gather.7.cloned.1.call-done, bf16[128,2048]{1,0:T(8,128)(2,1)} %collective-permute-done, pred[768]{0:T(1024)(128)(4,1)S(1)} %iota_compare_fusion.5, ...), kind=kOutput, calls=%fused_computation.125 | convolution fusion | flops 3232235520 | bytes 10488068 | tf_op jit(solution)/shard_map/dot_general | solution.py:41
  503.3 59.9 %shard_map.320 = (bf16[4,256,1536]{2,1,0:T(8,128)(2,1)}, f32[768,256]{1,0:T(8,128)}, f32[768,256]{1,0:T(8,128)}, f32[8,768]{1,0:T(8,128)}) custom-call(f32[1024,768]{1,0:T(8,128)} %bitcast.166, f32[4,256,1536]{2,1,0:T(8,128)} %fusion.17.xy_ref, f32[1024,768]{1,0:T(8,128)} %get-tuple-element.67.st_ref, bf16[4,256,768]{2,1,0:T(8,128)(2,1)} %get-tuple-element.68.conv_ref, ...), custom_call_target="tpu_custom_call" | custom-call | flops 2415919104 | bytes 180000000 | tf_op jit(solution)/shard_map/pallas_call | solution.py:464
  563.2 11.5 %bitcast_convert_fusion = bf16[2048,1536]{1,0:T(8,128)(2,1)} fusion(bf16[4,256,2048]{2,1,0:T(8,128)(2,1)} %copy-done.22, bf16[4,256,1536]{2,1,0:T(8,128)(2,1)} %get-tuple-element.74), kind=kOutput, calls=%fused_computation | convolution fusion | flops 6445596672 | bytes 13631488 | tf_op jit(solution)/shard_map/dot_general | solution.py:45
  574.7 2.0 copy.177
  576.8 2.1 copy.176
  578.8 2.2 fusion.39
  581.0 2.4 copy.178
  586.0 3.1 collective-permute-start.2
  589.1 11.7 %fusion.16 = f32[4,256,2048]{2,1,0:T(8,128)} fusion(bf16[4,256,1536]{2,1,0:T(8,128)(2,1)} %get-tuple-element.74, bf16[2048,1664]{1,0:T(8,128)(2,1)} %bitcast.179), kind=kOutput, calls=%fused_computation.33 | convolution fusion | flops 6442450944 | bytes 17825792 | tf_op jit(solution)/shard_map/dot_general | solution.py:41
  603.3 1.9 convert_element_type.179
  605.2 10.1 %fusion.3 = (bf16[2048]{0:T(1024)(128)(2,1)S(1)}, bf16[4,256,2048]{2,1,0:T(8,128)(2,1)}) fusion(f32[4,256,2048]{2,1,0:T(8,128)} %fusion.16, bf16[4,256,2048]{2,1,0:T(8,128)(2,1)} %copy-done, f32[4,256]{1,0:T(4,128)S(1)} %copy-done.31), kind=kLoop, calls=%fused_computation.11 | loop fusion | flops 10483712 | bytes 16785408 | tf_op jit(solution)/shard_map/reduce_sum | solution.py:982
  617.7 6.5 pad_maximum_fusion
  624.2 4.5 all-to-all-start.1
  628.7 9.9 %fusion.22.refs_0_ = bf16[4,256,2048]{2,1,0:T(8,128)(2,1)S(1)} fusion(bf16[4,256,1536]{2,1,0:T(8,128)(2,1)} %get-tuple-element.220, bf16[1536,2048]{1,0:T(8,128)(2,1)} %all-gather.11.cloned.1.call-done), kind=kOutput, calls=%fused_computation.39 | convolution fusion | flops 6444548096 | bytes 13631488 | tf_op jit(solution)/shard_map/dot_general | solution.py:37
  638.6 37.5 %shard_map.318 = bf16[256,2048]{1,0:T(8,128)(2,1)S(1)} custom-call(bf16[4,256,2048]{2,1,0:T(8,128)(2,1)S(1)} %fusion.22.refs_0_, f32[256,2048]{1,0:T(8,128)S(1)} %get-tuple-element.61.refs_1_), custom_call_target="tpu_custom_call" | custom-call | flops 20971520 | bytes 120000000 | tf_op jit(solution)/shard_map/pallas_call | solution.py:644
  677.1 3.5 all-to-all-start.2
  681.9 23.3 %reduce-scatter.14.cloned.1.call-done = bf16[4,64,1792]{2,1,0:T(8,128)(2,1)} async-done(((bf16[4,512,1792]{2,1,0:T(8,128)(2,1)}), bf16[4,64,1792]{2,1,0:T(8,128)(2,1)}) %reduce-scatter.14.cloned.1.call-update) | async-done | bytes 917520 | tf_op jit(solution)/shard_map/reduce_scatter | solution.py:876
  708.0 1.8 fusion.44
  709.9 4.2 all-to-all-start
  718.1 41.1 %shard_map.321 = f32[256,2048]{1,0:T(8,128)S(1)} custom-call(bf16[4,256,2048]{2,1,0:T(8,128)(2,1)S(1)} %copy-done.2, bf16[256,2048]{1,0:T(8,128)(2,1)S(1)} %bitcast.152, f32[1,2048]{1,0:T(1,128)S(1)} %bitcast.158, f32[256,2048]{1,0:T(8,128)S(1)} %copy-done.9), custom_call_target="tpu_custom_call" | custom-call | flops 20971520 | bytes 120000000 | tf_op jit(solution)/shard_map/pallas_call | solution.py:644
  (191 shorter events, 47.9 us)
Async XLA Ops:
  7.2 19.2 %copy-start.24 = (bf16[64,6144]{1,0:T(8,128)(2,1)S(1)}, bf16[64,6144]{1,0:T(8,128)(2,1)}, u32[]{:S(2)}) copy-start(bf16[64,6144]{1,0:T(8,128)(2,1)} %param.36) | copy-start | bytes 2359300
  7.2 19.2 %copy-start.25 = (bf16[64,6144]{1,0:T(8,128)(2,1)S(1)}, bf16[64,6144]{1,0:T(8,128)(2,1)}, u32[]{:S(2)}) copy-start(bf16[64,6144]{1,0:T(8,128)(2,1)} %param.35) | copy-start | bytes 2359300
  7.2 124.5 %all-gather.5.cloned.1.call-start = ((), (), s32[]{:S(2)}) async-start(), calls=%async_computation.8 | async-start | bytes 7667712 | tf_op jit(solution)/shard_map/all_gather | solution.py:873
  11.2 16.2 %copy-start.33 = (bf16[80,4]{0,1:T(4,128)(2,1)S(1)}, bf16[80,4]{0,1:T(4,128)(2,1)}, u32[]{:S(2)}) copy-start(bf16[80,4]{0,1:T(4,128)(2,1)} %param.26) | copy-start | bytes 1924
  11.2 16.2 %copy-start.34 = (bf16[80]{0:T(256)(128)(2,1)S(1)}, bf16[80]{0:T(256)(128)(2,1)}, u32[]{:S(2)}) copy-start(bf16[80]{0:T(256)(128)(2,1)} %param.27) | copy-start | bytes 484
  11.2 16.2 %copy-start.35 = (bf16[80]{0:T(256)(128)(2,1)S(1)}, bf16[80]{0:T(256)(128)(2,1)}, u32[]{:S(2)}) copy-start(bf16[80]{0:T(256)(128)(2,1)} %param.29) | copy-start | bytes 484
  11.2 16.2 %copy-start.36 = (bf16[80]{0:T(256)(128)(2,1)S(1)}, bf16[80]{0:T(256)(128)(2,1)}, u32[]{:S(2)}) copy-start(bf16[80]{0:T(256)(128)(2,1)} %param.31) | copy-start | bytes 484
  11.2 16.2 %copy-start.37 = (bf16[80]{0:T(256)(128)(2,1)S(1)}, bf16[80]{0:T(256)(128)(2,1)}, u32[]{:S(2)}) copy-start(bf16[80]{0:T(256)(128)(2,1)} %param.32) | copy-start | bytes 484
  11.2 16.4 %copy-start.39 = (f32[8]{0:T(128)S(1)}, f32[8]{0:T(128)}, u32[]{:S(2)}) copy-start(f32[8]{0:T(128)} %param.21) | copy-start | bytes 100
  11.2 17.0 %copy-start.28 = (bf16[80,256]{1,0:T(8,128)(2,1)S(1)}, bf16[80,256]{1,0:T(8,128)(2,1)}, u32[]{:S(2)}) copy-start(bf16[80,256]{1,0:T(8,128)(2,1)} %param.30) | copy-start | bytes 122884
  11.2 17.0 %copy-start.29 = (bf16[80,256]{1,0:T(8,128)(2,1)S(1)}, bf16[80,256]{1,0:T(8,128)(2,1)}, u32[]{:S(2)}) copy-start(bf16[80,256]{1,0:T(8,128)(2,1)} %param.28) | copy-start | bytes 122884
  25.5 126.2 %all-gather.7.cloned.1.call-start = ((), (), s32[]{:S(2)}) async-start(), calls=%async_computation.9 | async-start | bytes 2949120 | tf_op jit(solution)/shard_map/all_gather | solution.py:53
  26.3 257.1 %all-gather.9.cloned.1.call-start = ((), (), s32[]{:S(2)}) async-start(), calls=%async_computation.10 | async-start | bytes 14155776 | tf_op jit(solution)/shard_map/all_gather | solution.py:873
  26.4 3.9 copy-start.3
  131.7 205.2 %all-gather.11.cloned.1.call-start = ((), (), s32[]{:S(2)}) async-start(), calls=%async_computation.11 | async-start | bytes 7077888 | tf_op jit(solution)/shard_map/all_gather | solution.py:53
  131.8 5.1 copy-start.1
  136.9 4.5 copy-start.26
  137.9 2.1 copy-start.22
  141.4 8.7 %copy-start.12 = (bf16[2,80,640]{2,1,0:T(8,128)(2,1)S(1)}, bf16[2,80,640]{2,1,0:T(8,128)(2,1)}, u32[]{:S(2)}) copy-start(bf16[2,80,640]{2,1,0:T(8,128)(2,1)} %copy-done.11) | copy-start | bytes 614404
  150.0 257.5 %reduce-scatter.6.cloned.1.call-start = ((), (), s32[]{:S(2)}) async-start(), calls=%async_computation.12 | async-start | bytes 7077888 | tf_op jit(solution)/shard_map/reduce_scatter | solution.py:57
  152.9 46.3 %collective-permute-start = (bf16[128,2048]{1,0:T(8,128)(2,1)S(1)}, bf16[128,2048]{1,0:T(8,128)(2,1)}, u32[]{:S(2)}, u32[]{:S(2)}) collective-permute-start(bf16[128,2048]{1,0:T(8,128)(2,1)S(1)} %slice.211), channel_id=1, source_target_pairs={{8,0},{16,8},{24,16},{9,1},{17,9},{25,17},{10,2},{18,10},{26,18},{... | collective-permute-start | bytes 1572872 | tf_op jit(solution)/shard_map/ppermute | solution.py:21
  155.8 43.4 %copy-start.27 = (bf16[640,2048]{1,0:T(8,128)(2,1)S(1)}, bf16[640,2048]{1,0:T(8,128)(2,1)}, u32[]{:S(2)}) copy-start(bf16[640,2048]{1,0:T(8,128)(2,1)} %all-gather.7.cloned.1.call-done) | copy-start | bytes 7864324
  283.4 11.9 %copy-start.18 = (bf16[4,256,2048]{2,1,0:T(8,128)(2,1)S(1)}, bf16[4,256,2048]{2,1,0:T(8,128)(2,1)}, u32[]{:S(2)}) copy-start(bf16[4,256,2048]{2,1,0:T(8,128)(2,1)} %copy-done.17) | copy-start | bytes 12582916
  283.4 11.9 %copy-start.38 = (bf16[4,512,3072]{2,1,0:T(8,128)(2,1)S(1)}, bf16[4,512,3072]{2,1,0:T(8,128)(2,1)}, u32[]{:S(2)}) copy-start(bf16[4,512,3072]{2,1,0:T(8,128)(2,1)} %all-gather.9.cloned.1.call-done) | copy-start | bytes 37748740
  295.3 11.7 %copy-start.16 = (bf16[4,256,2048]{2,1,0:T(8,128)(2,1)S(1)}, bf16[4,256,2048]{2,1,0:T(8,128)(2,1)}, u32[]{:S(2)}) copy-start(bf16[4,256,2048]{2,1,0:T(8,128)(2,1)} %copy-done.15) | copy-start | bytes 12582916
  317.6 177.1 %reduce-scatter.8.cloned.1.call-start = ((), (), s32[]{:S(2)}) async-start(), calls=%async_computation.13 | async-start | bytes 7077888 | tf_op jit(solution)/shard_map/reduce_scatter | solution.py:876
  336.9 18.5 %copy-start.19 = (bf16[4,256,2048]{2,1,0:T(8,128)(2,1)S(1)}, bf16[4,256,2048]{2,1,0:T(8,128)(2,1)}, u32[]{:S(2)}) copy-start(bf16[4,256,2048]{2,1,0:T(8,128)(2,1)} %copy-done.17) | copy-start | bytes 12582916
  355.4 8.8 %copy-start.40 = (bf16[4,256,1536]{2,1,0:T(8,128)(2,1)}, bf16[4,256,1536]{2,1,0:T(8,128)(2,1)S(1)}, u32[]{:S(2)}) copy-start(bf16[4,256,1536]{2,1,0:T(8,128)(2,1)S(1)} %get-tuple-element.62) | copy-start | bytes 9437188
  364.2 199.0 %reduce-scatter.10.cloned.1.call-start = ((), (), s32[]{:S(2)}) async-start(), calls=%async_computation.14 | async-start | bytes 7077888 | tf_op jit(solution)/shard_map/reduce_scatter | solution.py:876
  375.9 227.4 %reduce-scatter.12.cloned.1.call-start = ((), (), s32[]{:S(2)}) async-start(), calls=%async_computation.15 | async-start | bytes 2949120 | tf_op jit(solution)/shard_map/reduce_scatter | solution.py:57
  378.5 17.6 %slice-start = ((s8[12582912]{0:T(1024)(128)(4,1)}), s8[4194304]{0:T(1024)(128)(4,1)S(1)}, s32[]{:S(2)}) async-start(s8[12582912]{0:T(1024)(128)(4,1)} %bitcast.188), calls=%async_computation.17 | async-start | bytes 8388608
  379.6 16.5 %slice-start.1 = ((s8[12582912]{0:T(1024)(128)(4,1)}), s8[4194304]{0:T(1024)(128)(4,1)S(1)}, s32[]{:S(2)}) async-start(s8[12582912]{0:T(1024)(128)(4,1)} %bitcast.188), calls=%async_computation.18 | async-start | bytes 8388608
  379.7 16.5 %slice-start.2 = ((s8[12582912]{0:T(1024)(128)(4,1)}), s8[4194304]{0:T(1024)(128)(4,1)S(1)}, s32[]{:S(2)}) async-start(s8[12582912]{0:T(1024)(128)(4,1)} %bitcast.188), calls=%async_computation.19 | async-start | bytes 8388608
  379.7 16.5 %copy-start.41 = (bf16[4,256,1536]{2,1,0:T(8,128)(2,1)S(1)}, bf16[4,256,1536]{2,1,0:T(8,128)(2,1)}, u32[]{:S(2)}) copy-start(bf16[4,256,1536]{2,1,0:T(8,128)(2,1)} %get-tuple-element.63) | copy-start | bytes 9437188
  379.7 107.8 %collective-permute-start.1 = (bf16[4,256,128]{1,2,0:T(8,128)(2,1)S(1)}, bf16[4,256,128]{1,2,0:T(8,128)(2,1)}, u32[]{:S(2)}, u32[]{:S(2)}) collective-permute-start(bf16[4,256,128]{1,2,0:T(8,128)(2,1)S(1)} %slice.215), channel_id=1, source_target_pairs={{0,8},{8,16},{16,24},{1,9},{9,17},{17,25},{2,10},{10,18},{18,26},{... | collective-permute-start | bytes 786440 | tf_op jit(solution)/shard_map/ppermute | solution.py:21
  407.5 81.9 %copy-start.23 = (bf16[4,256,768]{1,2,0:T(8,128)(2,1)S(1)}, bf16[4,256,768]{1,2,0:T(8,128)(2,1)}, u32[]{:S(2)}) copy-start(bf16[4,256,768]{1,2,0:T(8,128)(2,1)} %copy.172) | copy-start | bytes 4718596
  410.8 2.2 copy-start.6
  494.7 210.4 %reduce-scatter.14.cloned.1.call-start = ((), (), s32[]{:S(2)}) async-start(), calls=%async_computation.16 | async-start | bytes 8257536 | tf_op jit(solution)/shard_map/reduce_scatter | solution.py:876
  563.2 15.6 %copy-start.32 = (f32[8,768]{1,0:T(8,128)S(1)}, f32[8,768]{1,0:T(8,128)}, u32[]{:S(2)}) copy-start(f32[8,768]{1,0:T(8,128)} %get-tuple-element.79) | copy-start | bytes 73732
  586.0 14.9 %collective-permute-start.2 = (bf16[128,768]{1,0:T(8,128)(2,1)S(1)}, bf16[128,768]{1,0:T(8,128)(2,1)}, u32[]{:S(2)}, u32[]{:S(2)}) collective-permute-start(bf16[128,768]{1,0:T(8,128)(2,1)S(1)} %slice.217), channel_id=1, source_target_pairs={{0,8},{8,16},{16,24},{1,9},{9,17},{17,25},{2,10},{10,18},{18,26},{... | collective-permute-start | bytes 589832 | tf_op jit(solution)/shard_map/ppermute | solution.py:21
  600.8 4.4 copy-start.31
  624.2 52.9 %all-to-all-start.1 = ((bf16[4,64,1536]{2,1,0:T(8,128)(2,1)}), bf16[4,64,1536]{2,1,0:T(8,128)(2,1)}, u32[]{:S(2)}, u32[]{:S(2)}) async-start(bf16[4,64,1536]{2,1,0:T(8,128)(2,1)} %reduce-scatter.8.cloned.1.call-done), calls=%async_computation.6 | async-start | bytes 1572864 | tf_op jit(solution)/shard_map/all_to_all | solution.py:49
  677.1 32.8 %all-to-all-start.2 = ((bf16[4,64,1536]{2,1,0:T(8,128)(2,1)}), bf16[4,64,1536]{2,1,0:T(8,128)(2,1)S(1)}, u32[]{:S(2)}, u32[]{:S(2)}) async-start(bf16[4,64,1536]{2,1,0:T(8,128)(2,1)} %reduce-scatter.10.cloned.1.call-done), calls=%async_computation.7 | async-start | bytes 1572864 | tf_op jit(solution)/shard_map/all_to_all | solution.py:49
  709.9 51.5 %all-to-all-start = ((bf16[4,64,1664]{2,1,0:T(8,128)(2,1)}), bf16[4,64,1664]{2,1,0:T(8,128)(2,1)}, u32[]{:S(2)}, u32[]{:S(2)}) async-start(bf16[4,64,1664]{2,1,0:T(8,128)(2,1)} %fusion.44), calls=%async_computation.5 | async-start | bytes 1703936 | tf_op jit(solution)/shard_map/all_to_all | solution.py:49
  714.1 3.3 copy-start.2
  714.1 4.0 copy-start.9
  714.1 4.0 copy-start.14
  760.7 4.6 copy-start.5
  (12 other events, 17.5 us)
Sparse Core Ops, SparseCore 0:
  25.7 84.0 all-gather.4
  111.4 33.7 all-gather.6
  147.4 117.4 all-gather.8
  266.4 70.4 all-gather.10
  339.1 68.4 reduce-scatter.5
  409.7 68.1 reduce-scatter.7
  480.2 75.5 reduce-scatter.9
  558.1 35.8 reduce-scatter.11
  624.3 80.7 reduce-scatter.13

commit v3 on v2

--- a/solution.py
+++ b/solution.py
@@ -77,6 +77,112 @@
     )
 
 
+CHUNKS = 4
+
+
+def flip(me, bit):
+    return me + bit - 2 * bit * lax.rem(me // bit, 2)
+
+
+def greet_all(T, mine, peers):
+    barrier = pltpu.get_barrier_semaphore()
+    for peer in peers:
+        pl.semaphore_signal(barrier, inc=1, device_id={"seq": peer}, device_id_type=MESH)
+    for d in range(1, T):
+        pl.semaphore_signal(barrier, inc=1, device_id={"tok": lax.rem(mine + d, T)}, device_id_type=MESH)
+    pl.semaphore_wait(barrier, T - 1 + len(peers))
+
+
+def gather_rows(L, src, out, send, recv):
+    me = lax.axis_index("seq")
+    px, py = flip(me, 1), flip(me, 2)
+    H = L // CHUNKS
+
+    def copy(c, k):
+        f, g = (px, py) if c % 2 == 0 else (py, px)
+        rows = pl.ds(c * H, H)
+        sems = send.at[c, k], recv.at[c, k], "seq"
+        if k == 2:
+            place = out.at[f, rows, :]
+            return remote(place, place, *sems, g)
+        return remote(src.at[rows, :], out.at[me, rows, :], *sems, (f, g)[k])
+
+    def start():
+        for k in (0, 1):
+            for c in range(CHUNKS):
+                copy(c, k).start()
+
+    def forward():
+        for c in range(CHUNKS):
+            copy(c, 0).wait_recv()
+            copy(c, 2).start()
+
+    def drain():
+        for c in range(CHUNKS):
+            copy(c, 0).wait_send()
+            copy(c, 1).wait()
+            copy(c, 2).wait()
+
+    return start, forward, drain
+
+
+def sum_rows(L, part, one_s, two_s, two_out, one_send, one_recv, two_send, two_recv):
+    me = lax.axis_index("seq")
+    px, py, pd = flip(me, 1), flip(me, 2), 3 - me
+    H = L // CHUNKS
+
+    def peers(c):
+        return (px, py) if c % 2 == 0 else (py, px)
+
+    def rows(c):
+        return pl.ds(c * H, H)
+
+    def one(c, k):
+        f, _ = peers(c)
+        src = (f, pd)[k]
+        return remote(part.at[src, rows(c), :], one_s.at[c, k], one_send.at[c, k], one_recv.at[c, k], "seq", f)
+
+    def two(c):
+        return remote(two_out.at[c], two_s.at[c], two_send.at[c], two_recv.at[c], "seq", peers(c)[1])
+
+    def start():
+        for c in range(CHUNKS):
+            for k in (1, 0):
+                one(c, k).start()
+
+    def middle(c):
+        one(c, 1).wait_recv()
+        two_out[c] = (part[peers(c)[1], rows(c), :].astype(F32) + one_s[c, 1].astype(F32)).astype(BF)
+        two(c).start()
+
+    def total(c):
+        one(c, 0).wait_recv()
+        two(c).wait_recv()
+        return part[me, rows(c), :].astype(F32) + one_s[c, 0].astype(F32) + two_s[c].astype(F32)
+
+    def drain():
+        for c in range(CHUNKS):
+            for k in (0, 1):
+                one(c, k).wait_send()
+            two(c).wait_send()
+
+    return start, middle, total, drain
+
+
+def sum_scratch(L, D):
+    H = L // CHUNKS
+    dma = pltpu.SemaphoreType.DMA
+    return [
+        pltpu.VMEM((CHUNKS, 2, H, D), BF),
+        pltpu.VMEM((CHUNKS, H, D), BF),
+        pltpu.VMEM((CHUNKS, H, D), BF),
+        dma((CHUNKS, 2)),
+        dma((CHUNKS, 2)),
+        dma((CHUNKS,)),
+        dma((CHUNKS,)),
+    ]
+
+
 def minus_expm1(x, whole):
     series = 1.0 + x * (1.0 / 7)
     for n in (6, 5, 4, 3, 2):
@@ -120,14 +226,17 @@
 
 
 def recur_forward(
-    T, S, L, C, xy_ref, rows_ref, wd_ref, wi_ref,
-    mixed_ref, states_ref, conv_ref, x_ref, halo_ref, inc_ref,
-    a_s, b_s, ext_s, fin_s, got_s, halo_send, halo_recv, send_sem, recv_sem,
+    T, S, L, C, xy_ref, rows_ref, wd_ref, wi_ref, cot_ref,
+    mixed_ref, states_ref, conv_ref, x_ref, halo_ref, inc_ref, cots_ref,
+    a_s, b_s, ext_s, fin_s, got_s, halo_send, halo_recv, send_sem, recv_sem, cot_send, cot_recv, own_sem,
 ):
     t = lax.axis_index("tok")
     SL = S * L // 8
     half = 8 // S
-    greet("tok", T, t)
+    me = lax.axis_index("seq")
+    greet_all(T, t, (flip(me, 1), flip(me, 2)))
+    start_cot, forward_cot, drain_cot = gather_rows(L, cot_ref, cots_ref, cot_send, cot_recv)
+    own_cot = pltpu.make_async_copy(cot_ref, cots_ref.at[me], own_sem)
     for q in range(S):
         x_ref[q, L - LAP : L, :] = xy_ref[q, L - LAP : L, 0:C].astype(BF)
     lap = remote(x_ref.at[:, pl.ds(L - LAP, LAP), :], halo_ref, halo_send, halo_recv, "tok", lax.rem(t + 1, T))
@@ -135,6 +244,9 @@
     @pl.when(t < T - 1)
     def _():
         lap.start()
+
+    start_cot()
+    own_cot.start()
 
     @pl.when(t > 0)
     def _():
@@ -182,6 +294,7 @@
         put_wide(b_s, here, col, b)
 
     over_tiles(S, L, C, make)
+    forward_cot()
 
     NC = C // LANE
 
@@ -246,16 +359,23 @@
     def _():
         lap.wait_send()
 
+    drain_cot()
+    own_cot.wait()
+
 
 def recur_backward(
-    T, S, L, C, gm_ref, xy_ref, st_ref, conv_ref, x_ref, halo_ref, inc_ref, rows_ref, wd_ref, wi_ref,
-    gxy_ref, gwd_ref, gwi_ref, small_ref,
+    T, S, L, C, gm_ref, xy_ref, st_ref, conv_ref, x_ref, halo_ref, inc_ref, rows_ref, wd_ref, wi_ref, part_ref, resid_ref,
+    gxy_ref, gwd_ref, gwi_ref, small_ref, block_ref,
     a_s, g_s, r_s, sg_s, si_s, gc_s, ext_s, pst_s, fin_s, got_s, car_s, lap_send, lap_recv, send_sem, recv_sem,
+    *sum_refs,
 ):
     t = lax.axis_index("tok")
     SL = S * L // 8
     half = 8 // S
-    greet("tok", T, t)
+    me = lax.axis_index("seq")
+    greet_all(T, t, (flip(me, 1), flip(me, 2)))
+    start_sum, middle_sum, total_sum, drain_sum = sum_rows(L, part_ref, *sum_refs)
+    start_sum()
 
     def prepare(q, r0, col):
         cs = pl.ds(col, BW)
@@ -314,6 +434,8 @@
             if k > 0:
                 car = fin_s[c, pl.ds(k, S, stride=half), :] * car + fin_s[c, pl.ds(8 + k, S, stride=half), :]
 
+    for c in range(CHUNKS):
+        middle_sum(c)
     small_ref[...] = jnp.zeros_like(small_ref)
     gwd_ref[...] = jnp.zeros_like(gwd_ref)
     gwi_ref[...] = jnp.zeros_like(gwi_ref)
@@ -367,6 +489,10 @@
     def _():
         lap.start()
 
+    for c in range(CHUNKS):
+        rows = pl.ds(c * (L // CHUNKS), L // CHUNKS)
+        block_ref[rows, :] = (resid_ref[rows, :] + total_sum(c)).astype(BF)
+
     @pl.when(t < T - 1)
     def _():
         lap.wait_recv()
@@ -407,6 +533,8 @@
     def _():
         lap.wait_send()
 
+    drain_sum()
+
 
 VM = pl.BlockSpec(memory_space=pltpu.VMEM)
 
@@ -421,8 +549,9 @@
     )
 
 
-def run_forward(T, branches, rows, wd, wi):
+def run_forward(T, branches, rows, wd, wi, cot):
     S, L, C = branches.shape
+    hbm = pl.BlockSpec(memory_space=pl.ANY)
     C //= 2
     M = S * L
     dma = pltpu.SemaphoreType.DMA
@@ -436,9 +565,10 @@
             shape((S, L, C), BF),
             shape((S, LAP, C), BF),
             shape((C // LANE, 8, LANE)),
+            shape((S,) + cot.shape, BF),
         ),
-        in_specs=[VM] * 4,
-        out_specs=(VM,) * 6,
+        in_specs=[VM] * 4 + [hbm],
+        out_specs=(VM,) * 6 + (hbm,),
         scratch_shapes=[
             split,
             split,
@@ -449,13 +579,16 @@
             dma,
             dma((T,)),
             dma((T,)),
+            dma((CHUNKS, 3)),
+            dma((CHUNKS, 3)),
+            dma,
         ],
         compiler_params=params(0),
         cost_estimate=pl.CostEstimate(flops=4 * M * C * BW, bytes_accessed=100000000, transcendentals=6 * M * C),
-    )(branches, rows, wd, wi)
-
-
-def run_backward(T, grad_mixed, branches, states, conv, branch_x, halo, inc, rows, wd, wi):
+    )(branches, rows, wd, wi, cot)
+
+
+def run_backward(T, grad_mixed, branches, states, conv, branch_x, halo, inc, rows, wd, wi, part, resid):
     S, L, C = branch_x.shape
     M = S * L
     dma = pltpu.SemaphoreType.DMA
@@ -463,9 +596,15 @@
     split = pltpu.VMEM((C // LANE, M, LANE), F32)
     return pl.pallas_call(
         functools.partial(recur_backward, T, S, L, C),
-        out_shape=(shape((S, L, 2 * C), BF), shape((C, BW)), shape((C, BW)), shape((8, C))),
-        in_specs=[VM] * 10,
-        out_specs=(VM,) * 4,
+        out_shape=(
+            shape((S, L, 2 * C), BF),
+            shape((C, BW)),
+            shape((C, BW)),
+            shape((8, C)),
+            shape(resid.shape, BF),
+        ),
+        in_specs=[VM] * 12,
+        out_specs=(VM,) * 5,
         scratch_shapes=[split] * 3
         + [big] * 2
         + [
@@ -479,13 +618,11 @@
             dma,
             dma((T,)),
             dma((T,)),
-        ],
+        ]
+        + sum_scratch(*resid.shape),
         compiler_params=params(1),
         cost_estimate=pl.CostEstimate(flops=12 * M * C * BW, bytes_accessed=180000000, transcendentals=6 * M * C),
-    )(grad_mixed, branches, states, conv, branch_x, halo, inc, rows, wd, wi)
-
-
-CHUNKS = 4
+    )(grad_mixed, branches, states, conv, branch_x, halo, inc, rows, wd, wi, part, resid)
 
 
 def root_scale(v):
@@ -496,11 +633,7 @@
     scale = root_scale(v)
     hat = v * scale
     inner = grad * gain
-    return scale * (inner - hat * jnp.mean(inner * hat, axis=-1, keepdims=True)), grad * hat
-
-
-def flip(me, bit):
-    return me + bit - 2 * bit * lax.rem(me // bit, 2)
+    return scale * (inner - hat * jnp.mean(inner * hat, axis=-1, keepdims=True))
 
 
 def plane_sum(kind, L, D, *refs):
@@ -510,42 +643,27 @@
         tokens, gain, keep, everyone = refs[1:5]
         rest = refs[5:]
     elif kind == "second":
-        resid, gain, cot, weight, keep, gain_grad, everyone = refs[1:8]
-        rest = refs[8:]
-    elif kind == "third":
+        resid, gain, cot, weight, keep, everyone = refs[1:7]
+        rest = refs[7:]
+    else:
         tokens, gain, before, keep = refs[1:5]
         rest = refs[5:]
-    else:
-        resid, keep = refs[1:3]
-        rest = refs[3:]
-    one_s, two_s, two_out, one_send, one_recv, two_send, two_recv = rest[:7]
     if shares:
         own_s, all_send, all_recv, own_sem = rest[7:]
     me = lax.axis_index("seq")
     H = L // CHUNKS
     px, py = flip(me, 1), flip(me, 2)
-    pd = 3 - me
     barrier = pltpu.get_barrier_semaphore()
     for peer in (px, py):
         pl.semaphore_signal(barrier, inc=1, device_id={"seq": peer}, device_id_type=MESH)
     pl.semaphore_wait(barrier, 2)
-
-    def peers(c):
-        return (px, py) if c % 2 == 0 else (py, px)
+    start, middle, sums, drain = sum_rows(L, part, *rest[:7])
 
     def rows(c):
         return pl.ds(c * H, H)
 
-    def one(c, k):
-        f, _ = peers(c)
-        src = (f, pd)[k]
-        return remote(part.at[src, rows(c), :], one_s.at[c, k], one_send.at[c, k], one_recv.at[c, k], "seq", f)
-
-    def two(c):
-        return remote(two_out.at[c], two_s.at[c], two_send.at[c], two_recv.at[c], "seq", peers(c)[1])
-
     def share(c, k):
-        f, g = peers(c)
+        f, g = (px, py) if c % 2 == 0 else (py, px)
         if k == 2:
             place = everyone.at[f, rows(c), :]
             return remote(place, place, all_send.at[c, k], all_recv.at[c, k], "seq", g)
@@ -555,32 +673,21 @@
     def own(c):
         return pltpu.make_async_copy(own_s.at[rows(c), :], everyone.at[me, rows(c), :], own_sem.at[c])
 
-    def middle(c):
-        one(c, 1).wait_recv()
-        two_out[c] = (part[peers(c)[1], rows(c), :].astype(F32) + one_s[c, 1].astype(F32)).astype(BF)
-        two(c).start()
-
     def finish(c):
-        one(c, 0).wait_recv()
-        two(c).wait_recv()
-        total = part[me, rows(c), :].astype(F32) + one_s[c, 0].astype(F32) + two_s[c].astype(F32)
+        total = sums(c)
         r = rows(c)
         if kind == "first":
             total = tokens[r, :].astype(F32) + total
             keep[r, :] = total
             own_s[r, :] = (total * root_scale(total) * gain[0:1, :]).astype(BF)
         elif kind == "second":
-            back, gg = rms_back(resid[r, :], gain[0:1, :], total)
-            gg = jnp.sum(gg, axis=0, keepdims=True)
-            gain_grad[0:1, :] = gg if c == 0 else gain_grad[0:1, :] + gg
+            back = rms_back(resid[r, :], gain[0:1, :], total)
             total = cot[r, :].astype(F32) * weight[0:1, 0:1] + back
             keep[r, :] = total
             own_s[r, :] = total.astype(BF)
-        elif kind == "third":
-            back, _ = rms_back(tokens[r, :].astype(F32), gain[0:1, :], total)
+        else:
+            back = rms_back(tokens[r, :].astype(F32), gain[0:1, :], total)
             keep[r, :] = before[r, :] + back
-        else:
-            keep[r, :] = (resid[r, :] + total).astype(BF)
         if shares:
             share(c, 0).start()
             share(c, 1).start()
@@ -590,11 +697,7 @@
         share(c, 0).wait_recv()
         share(c, 2).start()
 
-    if kind == "second":
-        gain_grad[...] = jnp.zeros_like(gain_grad)
-    for c in range(CHUNKS):
-        for k in (1, 0):
-            one(c, k).start()
+    start()
     for c in range(CHUNKS):
         middle(c)
         if c > 0:
@@ -605,11 +708,9 @@
     if shares:
         forward(CHUNKS - 2)
         forward(CHUNKS - 1)
-    for c in range(CHUNKS):
-        for k in (0, 1):
-            one(c, k).wait_send()
-        two(c).wait_send()
-        if shares:
+    drain()
+    if shares:
+        for c in range(CHUNKS):
             for k in (1, 2):
                 share(c, k).wait_recv()
             for k in (0, 1, 2):
@@ -619,26 +720,14 @@
 
 def run_plane(kind, collective_id, part, *ins):
     S, L, D = part.shape
-    H = L // CHUNKS
     dma = pltpu.SemaphoreType.DMA
     shares = kind in ("first", "second")
-    outs = [shape((L, D), BF if kind == "out" else F32)]
+    outs = [shape((L, D))]
     specs = [VM]
-    if kind == "second":
-        outs.append(shape((8, D)))
-        specs.append(VM)
     if shares:
         outs.append(shape((S, L, D), BF))
         specs.append(pl.BlockSpec(memory_space=pl.ANY))
-    scratch = [
-        pltpu.VMEM((CHUNKS, 2, H, D), BF),
-        pltpu.VMEM((CHUNKS, H, D), BF),
-        pltpu.VMEM((CHUNKS, H, D), BF),
-        dma((CHUNKS, 2)),
-        dma((CHUNKS, 2)),
-        dma((CHUNKS,)),
-        dma((CHUNKS,)),
-    ]
+    scratch = sum_scratch(L, D)
     if shares:
         scratch += [pltpu.VMEM((L, D), BF), dma((CHUNKS, 3)), dma((CHUNKS, 3)), dma((CHUNKS,))]
     return pl.pallas_call(
@@ -699,90 +788,81 @@
 
 
 def plane_fill(S, T, L, slabs, *refs):
-    pack, first, second, gates = refs[:4]
-    pack_out, first_out, second_out, gates_out, lent = refs[4:9]
-    pack_send, pack_recv, row_send, row_recv, gate_send, gate_recv, lent_send, lent_recv, own_sem = refs[9:]
+    pack, first, gates, pack_out, first_out, gates_out, lent = refs[:7]
+    pack_send, pack_recv, row_send, row_recv, gate_send, gate_recv, relay_send, relay_recv = refs[7:15]
+    lent_send, lent_recv, own_sem = refs[15:]
     me, t = lax.axis_index("seq"), lax.axis_index("tok")
     px, py, pd = flip(me, 1), flip(me, 2), S - 1 - me
-    H = L // CHUNKS
     barrier = pltpu.get_barrier_semaphore()
     for peer in (px, py, pd):
         pl.semaphore_signal(barrier, inc=1, device_id={"seq": peer}, device_id_type=MESH)
 
-    @pl.loop(1, T)
+    @pl.loop(1, T // 2)
     def _(d):
-        pl.semaphore_signal(barrier, inc=1, device_id={"tok": lax.rem(t + d, T)}, device_id_type=MESH)
-
-    pl.semaphore_wait(barrier, S - 1 + T - 1)
+        pl.semaphore_signal(barrier, inc=1, device_id={"tok": lax.rem(t + 2 * d, T)}, device_id_type=MESH)
+
+    mate = flip(t, 1)
+    pl.semaphore_signal(barrier, inc=1, device_id={"tok": mate}, device_id_type=MESH)
+    pl.semaphore_wait(barrier, S - 1 + T // 2)
 
     def gate(d):
-        return remote(gates, gates_out.at[t], gate_send.at[d], gate_recv.at[d], "tok", lax.rem(t + d, T))
+        return remote(gates, gates_out.at[t], gate_send.at[d], gate_recv.at[d], "tok", lax.rem(t + 2 * d, T))
+
+    def relay(d):
+        place = gates_out.at[lax.rem(t - 2 * d + T, T)]
+        return remote(place, place, relay_send.at[d], relay_recv.at[d], "tok", mate)
 
     def piece(k):
         to = (pd, px, py)[k]
         return remote(pack.at[to], pack_out.at[me], pack_send.at[k], pack_recv.at[k], "seq", to)
 
-    def row(a, c, k):
-        src, out = ((first, first_out), (second, second_out))[a]
-        f, g = (px, py) if c % 2 == 0 else (py, px)
-        rows = pl.ds(c * H, H)
-        sems = row_send.at[a, c, k], row_recv.at[a, c, k], "seq"
-        if k == 2:
-            place = out.at[f, rows, :]
-            return remote(place, place, *sems, g)
-        return remote(src.at[rows, :], out.at[me, rows, :], *sems, (f, g)[k])
-
     mine = [
         pltpu.make_async_copy(pack.at[me], pack_out.at[me], own_sem.at[0]),
         pltpu.make_async_copy(first, first_out.at[me], own_sem.at[1]),
-        pltpu.make_async_copy(second, second_out.at[me], own_sem.at[2]),
-        pltpu.make_async_copy(gates, gates_out.at[t], own_sem.at[3]),
+        pltpu.make_async_copy(gates, gates_out.at[t], own_sem.at[2]),
     ]
     loan = remote(gates_out.at[pl.ds(0, slabs)], lent, lent_send, lent_recv, "seq", px)
-
-    @pl.loop(1, T)
+    start, forward, drain = gather_rows(L, first, first_out, row_send, row_recv)
+
+    @pl.loop(1, T // 2)
     def _(d):
         gate(d).start()
 
+    for copy in mine:
+        copy.start()
+    start()
     for k in range(3):
         piece(k).start()
-    for copy in mine:
-        copy.start()
-    for k in (0, 1):
-        for c in range(CHUNKS):
-            row(0, c, k).start()
-    mine[3].wait()
-
-    @pl.loop(1, T)
+    mine[2].wait()
+    relay(0).start()
+
+    @pl.loop(1, T // 2)
     def _(d):
         gate(d).wait_recv()
+        relay(d).start()
+
+    @pl.loop(0, T // 2)
+    def _(d):
+        relay(d).wait_recv()
 
     @pl.when(lax.rem(me, 2) == 1)
     def _():
         loan.start()
 
-    for c in range(CHUNKS):
-        row(0, c, 0).wait_recv()
-        row(0, c, 2).start()
-    for k in (0, 1):
-        for c in range(CHUNKS):
-            row(1, c, k).start()
-    for c in range(CHUNKS):
-        row(1, c, 0).wait_recv()
-        row(1, c, 2).start()
+    forward()
     for k in range(3):
         piece(k).wait()
-    for a in (0, 1):
-        for c in range(CHUNKS):
-            row(a, c, 0).wait_send()
-            row(a, c, 1).wait()
-            row(a, c, 2).wait()
-    for copy in mine[:3]:
+    drain()
+    for copy in mine[:2]:
         copy.wait()
 
-    @pl.loop(1, T)
+    @pl.loop(1, T // 2)
     def _(d):
         gate(d).wait_send()
+
+    @pl.loop(0, T // 2)
+    def _(d):
+        relay(d).wait_send()
 
     @pl.when(lax.rem(me, 2) == 1)
     def _():
@@ -793,7 +873,7 @@
         loan.wait_recv()
 
 
-def run_fill(S, T, slabs, collective_id, pack, first, second, gates):
+def run_fill(S, T, slabs, collective_id, pack, first, gates):
     L = first.shape[0]
     dma = pltpu.SemaphoreType.DMA
     hbm = pl.BlockSpec(memory_space=pl.ANY)
@@ -802,26 +882,18 @@
         out_shape=(
             shape(pack.shape, BF),
             shape((S,) + first.shape, BF),
-            shape((S,) + second.shape, BF),
             shape((T,) + gates.shape, BF),
             shape((slabs,) + gates.shape, BF),
         ),
-        in_specs=[hbm] * 4,
-        out_specs=(hbm,) * 5,
-        scratch_shapes=[
-            dma((3,)),
-            dma((3,)),
-            dma((2, CHUNKS, 3)),
-            dma((2, CHUNKS, 3)),
-            dma((T,)),
-            dma((T,)),
-            dma,
-            dma,
-            dma((4,)),
-        ],
+        in_specs=[hbm] * 3,
+        out_specs=(hbm,) * 4,
+        scratch_shapes=[dma((3,))] * 2
+        + [dma((CHUNKS, 3))] * 2
+        + [dma((T // 2,))] * 4
+        + [dma, dma, dma((3,))],
         compiler_params=params(collective_id, 4),
-        cost_estimate=pl.CostEstimate(flops=0, bytes_accessed=320000000, transcendentals=0),
-    )(pack, first, second, gates)
+        cost_estimate=pl.CostEstimate(flops=0, bytes_accessed=220000000, transcendentals=0),
+    )(pack, first, gates)
 
 
 def after(value, *others):
@@ -895,8 +967,9 @@
     picked = jnp.sum(jnp.where(source_ids[:, None] == sources, loss_weights[None, :], 0.0), axis=1)
     cot_low = (grad_output[0].astype(F32) * picked[:, None]).astype(BF)
     pack_f = jnp.concatenate([w.reshape(ds, S, FQ).swapaxes(0, 1) for w in (gate_weight, up_weight)], axis=2)
-    pack_f, everyone, cot_low, gates, lent = run_fill(
-        S, T, -(-most // rs), 3, after(pack_f, pack_in), tokens[0], cot_low, gates
+    weight_out = gather(output_weight, "tok")
+    pack_f, everyone, gates, lent = run_fill(
+        S, T, -(-most // rs), 3, after(pack_f, pack_in, weight_out), tokens[0], gates
     )
 
     def r_rows(whole, lent):
@@ -905,7 +978,6 @@
         whole = lax.dynamic_slice_in_dim(whole, off, C, axis=0)
         return jnp.where(lax.broadcasted_iota(jnp.int32, whole.shape, 0) < own, whole, 0)
 
-    output_weight = after(output_weight, pack_in)
     pack_in = d_rows(pack_in)
     weight_xy = pack_in[:, : 2 * C]
     gain_one, gain_two = pack_in[:, 2 * C].astype(F32), pack_in[:, 2 * C + 1].astype(F32)
@@ -916,7 +988,6 @@
     rows = jnp.concatenate(
         [rows, 8.0 * jax.nn.softplus(param), jax.nn.sigmoid(param), jnp.zeros((6, C), F32)], axis=0
     )
-    weight_out = gather(output_weight, "tok")
     weight_out = r_rows(weight_out, from_behind(weight_out[:most], "seq", -1))
 
     pack_f = d_rows(after(pack_f, pack_in))
@@ -926,7 +997,9 @@
     normed = lax.optimization_barrier(rms_scale(everyone, gain_one).astype(BF))
     branches = forward_product(normed, weight_xy)
     weight_down = gather(after(down_weight, branches), "tok")
-    mixed, states, conv_low, branch_x, halo, incoming = run_forward(T, branches, rows, weight_decay, weight_input)
+    mixed, states, conv_low, branch_x, halo, incoming, cot_low = run_forward(
+        T, branches, rows, weight_decay, weight_input, cot_low
+    )
     mixed = mixed.reshape(S, length, C)
     passed = from_behind(mixed[:, :, quarter:], "seq", 1)
     mixed_own = jnp.pad(mixed, ((0, 0), (0, 0), (most, 0)))[:, :, :quarter]
@@ -949,79 +1022,65 @@
     grad_hidden = back_product(cot_low, weight_down)
     _, hidden_pull = jax.vjp(gelu_product, gate_val, up_val)
     grad_gate_val, grad_up_val = hidden_pull(grad_hidden)
-    grad_gate_low, grad_up_low = grad_gate_val.astype(BF), grad_up_val.astype(BF)
-    grad_gate_w = token_product(second_normed, grad_gate_low).astype(BF)
-    grad_up_w = token_product(second_normed, grad_up_low).astype(BF)
-    grad_gate_low, grad_up_low, _, _ = lax.optimization_barrier((grad_gate_low, grad_up_low, grad_gate_w, grad_up_w))
-    grad_second = back_product(grad_gate_low, weight_gate) + back_product(grad_up_low, weight_up)
+    grad_gate_up = jnp.concatenate([grad_gate_val.astype(BF), grad_up_val.astype(BF)], axis=2)
+    grad_pack = token_product(second_normed, grad_gate_up).astype(BF)
+    grad_second = back_product(after(grad_gate_up, grad_pack), pack_f)
     grad_second = after(grad_second.astype(BF), grad_down)
-    grad_gate_w = d_scatter(grad_gate_w)
-    grad_up_w = d_scatter(grad_up_w)
+    grad_pack = d_scatter(grad_pack)
     picked = jnp.broadcast_to(picked[None], (8, 128))
-    grad_resid, grad_gain_two, resid_low = run_plane(
+    grad_resid, resid_low = run_plane(
         "second", 6, grad_second, resid, gain_two[None], grad_output[0], picked
     )
-    grad_gain_two = grad_gain_two[0]
-
-    def whole_rows(parts):
-        return to_seq(parts).swapaxes(0, 1).reshape(ds, F).astype(F32)
 
     grad_out_w = token_product(mixed_own, resid_low).astype(BF)
-    grad_mixed = back_product(after(resid_low, grad_out_w, grad_gate_w), weight_out)
+    grad_mixed = back_product(after(resid_low, grad_out_w), weight_out)
     grad_out_w = scatter(grad_out_w, "tok").astype(F32)
-    grad_xy, grad_decay_w, grad_input_w, smalls = run_backward(
+    part = forward_product(hidden, weight_down).astype(BF)
+    grad_xy, grad_decay_w, grad_input_w, smalls, block_out = run_backward(
         T, grad_mixed.reshape(S * length, C), branches, states, conv_low, branch_x, halo, incoming, rows,
-        weight_decay, weight_input,
-    )
-    grad_i = token_product(normed, after(grad_xy, grad_up_w)).astype(BF)
+        weight_decay, weight_input, part, resid,
+    )
+    grad_i = token_product(normed, after(grad_xy, grad_pack)).astype(BF)
     smalls = jnp.pad(smalls.T, ((0, 0), (0, BW - 8)))
-    grad_r = r_align(jnp.concatenate([grad_decay_w, grad_input_w, smalls], axis=1))
+    grad_r = r_align(after(jnp.concatenate([grad_decay_w, grad_input_w, smalls], axis=1), grad_i))
     grad_normed = back_product(after(grad_xy, grad_i), weight_xy)
     grad_normed = after(grad_normed, grad_out_w)
-    hat = everyone * root_scale(everyone)
-    gains = jnp.stack([jnp.sum(grad_normed * hat, axis=(0, 1)), grad_gain_two], axis=0).astype(BF)
-
-    block = [p.reshape(T, rs, BW) for p in (grad_r[:, :BW], grad_r[:, BW : 2 * BW], grad_r[:, 2 * BW :])]
-    gains = gains.reshape(2, S, T, ds).transpose(2, 0, 1, 3).reshape(T, 2, S * ds)
-    tall = 3 * rs + 2 + -(3 * rs + 2) % (S * ds)
-    across = tall // (S * ds)
-    block = jnp.concatenate(block + [jnp.pad(gains, ((0, 0), (0, tall - 3 * rs - 2), (0, BW - S * ds)))], axis=1)
-    block = block.reshape(T, S, ds, across, BW).transpose(1, 0, 2, 3, 4).reshape(D, across * BW)
-    grad_i = jnp.concatenate([grad_i, block], axis=1)
+
+    grad_i = to_seq(d_scatter(grad_i)).astype(F32)
     (grad_tokens,) = run_plane("third", 7, grad_normed.astype(BF), tokens[0], gain_one[None], grad_resid)
-    part = forward_product(hidden, weight_down).astype(BF)
-    (block_out,) = run_plane("out", 5, part, resid)
-    grad_i = d_scatter(grad_i)
-    block = grad_i[:, :, 2 * C :].reshape(tall, BW).astype(F32)
-    grad_r = [block[i * rs : (i + 1) * rs] for i in range(3)]
-    gains = block[3 * rs : 3 * rs + 2, : S * ds].reshape(2, S, ds).transpose(1, 2, 0)
-    gains = jnp.pad(gains.astype(BF), ((0, 0), (0, 0), (0, SMALL - 2)))
-    grad_i = to_seq(jnp.concatenate([grad_i[:, :, : 2 * C], gains], axis=2)).astype(F32)
-    gain_grads = jnp.sum(grad_i[:, :, 2 * C : 2 * C + 2], axis=0)
+    grad_r = scatter(grad_r, "tok").astype(F32)
+    grad_pack = to_seq(grad_pack).swapaxes(0, 1).astype(F32)
+    grad_gate_w = grad_pack[:, :, :FQ].reshape(ds, F)
+    grad_up_w = grad_pack[:, :, FQ:].reshape(ds, F)
 
     def columns(at):
         return jnp.concatenate(
             [grad_i[i, :, at : at + (starts[i + 1] - starts[i]) * BW] for i in range(S)], axis=1
         )
 
-    smalls = grad_r[2]
+    grad_in_w, grad_gelu_w = columns(0), columns(C)
+
+    def gain_grad(gain, *pairs):
+        return sum(jnp.sum(w.astype(F32) * g, axis=1) for w, g in pairs) / gain.astype(F32)
+
+    smalls = grad_r[:, 2 * BW :]
     return (
         block_out[None],
         grad_tokens[None],
-        gain_grads[:, 0],
-        columns(0),
-        columns(C),
+        gain_grad(first_gain, (input_weight, grad_in_w), (gelu_weight, grad_gelu_w)),
+        grad_in_w,
+        grad_gelu_w,
         smalls[:, :CONV],
         smalls[:, 4],
-        grad_r[0],
+        grad_r[:, :BW],
         smalls[:, 5],
-        grad_r[1],
+        grad_r[:, BW : 2 * BW],
         smalls[:, 6],
         smalls[:, 7],
         grad_out_w,
-        gain_grads[:, 1],
-        whole_rows(grad_gate_w),
-        whole_rows(grad_up_w),
+        gain_grad(second_gain, (gate_weight, grad_gate_w), (up_weight, grad_up_w)),
+        grad_gate_w,
+        grad_up_w,
         grad_down,
     )
 

time: 784 us -> 696 us (0.89)
  Pallas kernels: 440 us -> 379 us
  waiting for transfers between devices: 44.2 us -> 59.2 us
  local copies, waits for them, and re-layouts: 52.9 us -> 38.2 us
  other arithmetic: 43.6 us -> 29.4 us
    pallas_call x4 -> x3, Pallas kernels: 227 us -> 190 us  [run_plane(): pl.pallas_call(functools.partial(plane_sum, kind, L, D), out_shape=tuple(...]
    pallas_call x1, Pallas kernels: 95.5 us -> 59.6 us  [run_fill(): pl.pallas_call(functools.partial(plane_fill, S, T, L, slabs), out_shape=(...]
    reduce_scatter x2 -> x3, waiting for transfers between devices: 0.75 us -> 32 us  [scatter(): lax.psum_scatter(value.astype(BF), axis, scatter_dimension=0, tiled=True)]
    reduce_scatter x3 -> x2, waiting for transfers between devices: 23.3 us -> 0.04 us  [d_scatter(): lax.psum_scatter(g.reshape(S, T * ds, g.shape[-1]), 'tok', scatter_dimens...]
    pallas_call x1, Pallas kernels: 43.3 us -> 53.2 us  [run_forward(): pl.pallas_call(functools.partial(recur_forward, T, S, L, C), out_shape=(s...]
    dot_general x5 -> x4, matrix products: 61.4 us -> 52.5 us  [back_product(): lax.dot_general(grad, weight, (((2,), (1,)), ((), ())), preferred_element...]
    unnamed x94 -> x101, local copies, waits for them, and re-layouts: 24.7 us -> 22.6 us
    dot_general x5 -> x4, matrix products: 47.7 us -> 46.6 us  [token_product(): lax.dot_general(left, grad, (((0, 1), (0, 1)), ((), ())), preferred_eleme...]
  transfers between devices with their start and end apart: 15 -> 14, of which waited for: 3 -> 4; matrix products, arithmetic and copies ran while one was open for 26% -> 28% of each run, Pallas kernels for 55% -> 55%
where the time goes in v3:
time: 696 us; the launch traced here: 688 us
  Pallas kernels  379 us (54%)
  matrix products  149 us (21%)
  waiting for transfers between devices  59.2 us (9%)
  local copies, waits for them, and re-layouts  38.2 us (5%)
  other arithmetic  29.4 us (4%)
  starting transfers between devices  17.6 us (3%)
  between operations  15.8 us (2%)
    pallas_call x3, Pallas kernels, run_plane(): pl.pallas_call(functools.partial(plane_sum, kind, L, D), out_shape=tuple(...  190 us
    pallas_call x1, Pallas kernels, run_backward(): pl.pallas_call(functools.partial(recur_backward, T, S, L, C), out_shape=(...  61.3 us
    pallas_call x1, Pallas kernels, run_fill(): pl.pallas_call(functools.partial(plane_fill, S, T, L, slabs), out_shape=(...  59.6 us
    pallas_call x1, Pallas kernels, run_forward(): pl.pallas_call(functools.partial(recur_forward, T, S, L, C), out_shape=(s...  53.2 us
    dot_general x4, matrix products, back_product(): lax.dot_general(grad, weight, (((2,), (1,)), ((), ())), preferred_element...  52.5 us
    dot_general x5, matrix products, forward_product(): return jnp.dot(left, weight, preferred_element_type=F32)  49.6 us
    dot_general x4, matrix products, token_product(): lax.dot_general(left, grad, (((0, 1), (0, 1)), ((), ())), preferred_eleme...  46.6 us
    reduce_scatter x3, waiting for transfers between devices, scatter(): lax.psum_scatter(value.astype(BF), axis, scatter_dimension=0, tiled=True)  32 us
  transfers between devices with their start and end apart: 14, of which 4 were waited for; matrix products, arithmetic and copies ran while one was open for 28% of the time, Pallas kernels for 55%

profile of v3, /device:TPU:0, one launch (start us, length us, event | category | flops | bytes accessed | tf_op | source)
XLA Modules:
  0.0 687.7 jit_solution(10709313263430093685)
XLA Ops:
  11.9 14.3 %shard_map.314 = bf16[4,64,1664]{2,1,0:T(8,128)(2,1)} custom-call(bf16[4,64,1664]{2,1,0:T(8,128)(2,1)S(1)} %pad_maximum_fusion.2.refs_0_), custom_call_target="tpu_custom_call" | custom-call | bytes 25559040 | tf_op jit(solution)/shard_map/pallas_call | solution.py:779
  26.8 19.6 %all-gather.5.cloned.1.call-done = bf16[640,2048]{1,0:T(8,128)(2,1)} async-done(((bf16[80,2048]{1,0:T(8,128)(2,1)}), bf16[640,2048]{1,0:T(8,128)(2,1)}) %all-gather.5.cloned.1.call-update) | async-done | bytes 2621456 | tf_op jit(solution)/shard_map/all_gather | solution.py:53
  46.4 59.6 %shard_map.315 = (bf16[4,64,3072]{2,1,0:T(8,128)(2,1)S(1)}, bf16[4,256,2048]{2,1,0:T(8,128)(2,1)S(1)}, bf16[8,80,640]{2,1,0:T(8,128)(2,1)S(1)}, bf16[2,80,640]{2,1,0:T(8,128)(2,1)S(1)}) custom-call(bf16[4,64,3072]{2,1,0:T(8,128)(2,1)S(1)} %pad_maximum_fusion.1.refs_0_, bf16[256,2048]{1,0:T(8,128)(2,1)S(1)} %bitcast.127, bf16[80,640]{1,0:T(8,128)(2,1)S(1)} %fusion.36.refs_2_), custom_call_target="tpu_custom_call" | custom-call | bytes 220000000 | tf_op jit(solution)/shard_map/pallas_call | solution.py:880
  106.0 2.0 copy-done
  109.8 6.8 all-gather.7.cloned.1.call-done
  116.6 3.2 fusion
  119.9 1.8 convert_reduce_fusion
  123.3 2.2 copy-done.22
  126.4 8.5 %fusion.17.xy_ref = f32[4,256,1536]{2,1,0:T(8,128)} fusion(bf16[4,256,2048]{2,1,0:T(8,128)(2,1)S(1)} %fusion.2, bf16[2048,1664]{1,0:T(8,128)(2,1)S(1)} %bitcast.151), kind=kOutput, calls=%fused_computation.32 | convolution fusion | flops 6442450944 | bytes 16777216 | tf_op jit(solution)/shard_map/dot_general | solution.py:37
  136.5 1.8 multiply_convert_fusion.2.cot_ref
  140.9 1.3 collective-permute-start
  143.8 53.2 %shard_map.316 = (bf16[1024,768]{1,0:T(8,128)(2,1)}, f32[1024,768]{1,0:T(8,128)}, bf16[4,256,768]{2,1,0:T(8,128)(2,1)}, bf16[4,256,768]{2,1,0:T(8,128)(2,1)}, bf...) custom-call(f32[4,256,1536]{2,1,0:T(8,128)} %fusion.17.xy_ref, ...), custom_call_target="tpu_custom_call" | custom-call | flops 805306368 | bytes 100000000 | tf_op jit(solution)/shard_map/pallas_call | solution.py:559
  197.0 5.3 convolution_convert_fusion.1.refs_0_
  202.2 71.6 %shard_map.317 = (f32[256,2048]{1,0:T(8,128)S(1)}, bf16[4,256,2048]{2,1,0:T(8,128)(2,1)S(1)}) custom-call(bf16[4,256,2048]{2,1,0:T(8,128)(2,1)S(1)} %convolution_convert_fusion.1.refs_0_, bf16[256,2048]{1,0:T(8,128)(2,1)S(1)} %bitcast.128, f32[1,2048]{1,0:T(1,128)S(1)} %bitcast.135), custom_call_target="tpu_custom_call" | custom-call | flops 20971520 | bytes 240000000 | tf_op jit(solution)/shard_map/pallas_call | solution.py:733
  273.9 2.1 copy-done.14
  276.0 12.7 %fusion.11 = f32[4,256,1536]{2,1,0:T(8,128)} fusion(bf16[4,256,2048]{2,1,0:T(8,128)(2,1)} %copy-done.14, bf16[2048,3072]{1,0:T(8,128)(2,1)} %bitcast.159), kind=kOutput, calls=%fused_computation.20 | convolution fusion | flops 6442450944 | bytes 16777216 | tf_op jit(solution)/shard_map/dot_general | solution.py:37
  288.7 11.6 %multiply_convert_fusion.1 = (bf16[4,256,1536]{2,1,0:T(8,128)(2,1)}, f32[4,256,1536]{2,1,0:T(8,128)}) fusion(f32[4,256,1536]{2,1,0:T(8,128)} %fusion.11, bf16[4,256,2048]{2,1,0:T(8,128)(2,1)S(1)} %copy-done.15, bf16[2048,3072]{1,0:T(8,128)(2,1)S(1)} %bitcast.161), kind=kOutput, calls=%fused_computation.28 | convolution fusion | flops 6458179584 | bytes 26214400 | tf_op jit(solution)/shard_map/dot_general | solution.py:37
  300.3 10.5 %bitcast_convert_fusion.2 = bf16[1536,2048]{1,0:T(8,128)(2,1)} fusion(bf16[4,256,1536]{2,1,0:T(8,128)(2,1)} %get-tuple-element.183, bf16[4,256,2048]{2,1,0:T(8,128)(2,1)S(1)} %copy-done.47), kind=kOutput, calls=%fused_computation.2 | convolution fusion | flops 6445596672 | bytes 13631488 | tf_op jit(solution)/shard_map/dot_general | solution.py:45
  310.9 18.4 %fusion.9 = (bf16[4,256,1536]{2,1,0:T(8,128)(2,1)S(1)}, bf16[4,256,1536]{2,1,0:T(8,128)(2,1)}) fusion(f32[4,256,1536]{2,1,0:T(8,128)} %fusion.11, f32[4,256,1536]{2,1,0:T(8,128)} %get-tuple-element.184, bf16[4,256,2048]{2,1,0:T(8,128)(2,1)} %get-tuple-element.52, bf16[1536,2048]{1,0:T(8,128)(2,1)} %all-gather.9.cloned.1.call-done), kind=kOutput, calls=%fused_computation.16 | convolution fusion | flops 6480199680 | bytes 29360128 | tf_op jit(solution)/shard_map/dot_general | solution.py:41
  329.3 18.9 %bitcast_convert_fusion = bf16[2048,3072]{1,0:T(8,128)(2,1)} fusion(bf16[4,256,2048]{2,1,0:T(8,128)(2,1)S(1)} %copy-done.16, bf16[4,256,1536]{2,1,0:T(8,128)(2,1)} %get-tuple-element.158, bf16[4,256,1536]{2,1,0:T(8,128)(2,1)S(1)} %get-tuple-element.157), kind=kOutput, calls=%fused_computation | convolution fusion | flops 12903776256 | bytes 23068672 | tf_op jit(solution)/shard_map/dot_general | solution.py:45
  348.3 2.6 copy.109
  351.9 5.0 collective-permute-start.1
  356.9 3.6 pad_maximum_fusion
  360.4 17.8 %convolution_convert_fusion.refs_0_ = bf16[4,256,2048]{2,1,0:T(8,128)(2,1)} fusion(bf16[4,256,3072]{2,1,0:T(8,128)(2,1)S(1)} %pad_maximum_fusion, bf16[2048,3072,1]{1,0,2:T(8,128)(2,1)} %bitcast.160), kind=kOutput, calls=%fused_computation.33 | convolution fusion | flops 12886999040 | bytes 23068672 | tf_op jit(solution)/shard_map/dot_general | solution.py:41
  378.2 6.5 reduce-scatter.6.cloned.1.call-done
  384.7 2.6 convert_element_type.163
  387.9 2.2 copy-done.4
  390.1 1.5 copy-done.6
  391.6 70.9 %shard_map.318 = (f32[256,2048]{1,0:T(8,128)S(1)}, bf16[4,256,2048]{2,1,0:T(8,128)(2,1)S(1)}) custom-call(bf16[4,256,2048]{2,1,0:T(8,128)(2,1)S(1)} %copy-done.4, f32[256,2048]{1,0:T(8,128)S(1)} %get-tuple-element.61.refs_1_.resid_ref, f32[1,2048]{1,0:T(1,128)S(1)} %bitcast.136, bf16[256,2048]{1,0:T(8,128)(2,1)S(1)} %bitcast.131, ...), custom_call_target="tpu_custom_call" | custom-call | flops 20971520 | bytes 240000000 | tf_op jit(solution)/shard_map/pallas_call | solution.py:733
  462.5 1.3 copy-done.7
  463.8 1.9 copy-done.17
  465.8 5.4 bitcast_convert_fusion.3
  471.3 11.5 %fusion.18.part_ref = bf16[4,256,2048]{2,1,0:T(8,128)(2,1)} fusion(bf16[4,256,1536]{2,1,0:T(8,128)(2,1)} %get-tuple-element.183, bf16[1536,2048]{1,0:T(8,128)(2,1)} %all-gather.9.cloned.1.call-done), kind=kOutput, calls=%fused_computation.34 | convolution fusion | flops 6444548096 | bytes 13631488 | tf_op jit(solution)/shard_map/dot_general | solution.py:37
  482.8 6.5 fusion.39
  489.3 61.3 %shard_map.319 = (bf16[4,256,1536]{2,1,0:T(8,128)(2,1)}, f32[768,256]{1,0:T(8,128)}, f32[768,256]{1,0:T(8,128)}, f32[8,768]{1,0:T(8,128)}, bf16[256,2048]{1,0:T(8,128)(2,1)}) custom-call(f32[1024,768]{1,0:T(8,128)} %bitcast.145, f32[4,256,1536]{2,1,0:T(8,128)} %fusion.17.xy_ref, f32[1024,768]{1,0:T(8,128)} %get-tuple-element.64.st_ref, ...), custom_call_target="tpu_custom_call" | custom-call | flops 2415919104 | bytes 180000000 | tf_op jit(solution)/shard_map/pallas_call | solution.py:597
  550.6 11.8 %bitcast_convert_fusion.1 = bf16[2048,1536]{1,0:T(8,128)(2,1)} fusion(bf16[4,256,2048]{2,1,0:T(8,128)(2,1)} %copy-done.22, bf16[4,256,1536]{2,1,0:T(8,128)(2,1)} %get-tuple-element.72), kind=kOutput, calls=%fused_computation.1 | convolution fusion | flops 6445596672 | bytes 13631488 | tf_op jit(solution)/shard_map/dot_general | solution.py:45
  564.0 1.9 convert_element_type.167
  567.9 3.0 collective-permute-start.2
  570.9 4.4 all-to-all-start.1
  575.4 9.9 %fusion.16.refs_0_ = bf16[4,256,2048]{2,1,0:T(8,128)(2,1)S(1)} fusion(bf16[4,256,1536]{2,1,0:T(8,128)(2,1)} %get-tuple-element.72, bf16[2048,1664]{1,0:T(8,128)(2,1)} %bitcast.150), kind=kOutput, calls=%fused_computation.31 | convolution fusion | flops 6442450944 | bytes 13631488 | tf_op jit(solution)/shard_map/dot_general | solution.py:41
  585.4 47.8 %shard_map.320 = f32[256,2048]{1,0:T(8,128)S(1)} custom-call(bf16[4,256,2048]{2,1,0:T(8,128)(2,1)S(1)} %fusion.16.refs_0_, bf16[256,2048]{1,0:T(8,128)(2,1)S(1)} %bitcast.129, f32[1,2048]{1,0:T(1,128)S(1)} %bitcast.134, f32[256,2048]{1,0:T(8,128)S(1)} %copy-done.8), custom_call_target="tpu_custom_call" | custom-call | flops 20971520 | bytes 120000000 | tf_op jit(solution)/shard_map/pallas_call | solution.py:733
  634.5 1.8 convert_bitcast_fusion
  638.6 3.5 all-to-all-start
  642.2 1.9 multiply_reduce_fusion.1
  644.6 25.5 %reduce-scatter.14.cloned.1.call-done = bf16[80,768]{1,0:T(8,128)(2,1)} async-done(((bf16[640,768]{1,0:T(8,128)(2,1)}), bf16[80,768]{1,0:T(8,128)(2,1)}) %reduce-scatter.14.cloned.1.call-update) | async-done | bytes 122896 | tf_op jit(solution)/shard_map/reduce_scatter | solution.py:57
  673.2 1.5 fusion.45
  676.0 2.0 multiply_reduce_fusion.3
  679.5 1.3 copy.134
  (177 shorter events, 29.8 us)
Async XLA Ops:
  7.2 19.0 %copy-start.39 = (bf16[80]{0:T(256)(128)(2,1)S(1)}, bf16[80]{0:T(256)(128)(2,1)}, u32[]{:S(2)}) copy-start(bf16[80]{0:T(256)(128)(2,1)} %param.27) | copy-start | bytes 484
  7.2 19.0 %copy-start.40 = (bf16[80]{0:T(256)(128)(2,1)S(1)}, bf16[80]{0:T(256)(128)(2,1)}, u32[]{:S(2)}) copy-start(bf16[80]{0:T(256)(128)(2,1)} %param.29) | copy-start | bytes 484
  7.2 19.0 %copy-start.41 = (bf16[80]{0:T(256)(128)(2,1)S(1)}, bf16[80]{0:T(256)(128)(2,1)}, u32[]{:S(2)}) copy-start(bf16[80]{0:T(256)(128)(2,1)} %param.31) | copy-start | bytes 484
  7.2 19.0 %copy-start.42 = (bf16[80]{0:T(256)(128)(2,1)S(1)}, bf16[80]{0:T(256)(128)(2,1)}, u32[]{:S(2)}) copy-start(bf16[80]{0:T(256)(128)(2,1)} %param.32) | copy-start | bytes 484
  7.2 19.0 %copy-start.38 = (bf16[80,4]{0,1:T(4,128)(2,1)S(1)}, bf16[80,4]{0,1:T(4,128)(2,1)}, u32[]{:S(2)}) copy-start(bf16[80,4]{0,1:T(4,128)(2,1)} %param.26) | copy-start | bytes 1924
  7.2 19.2 %copy-start.36 = (bf16[80,256]{1,0:T(8,128)(2,1)S(1)}, bf16[80,256]{1,0:T(8,128)(2,1)}, u32[]{:S(2)}) copy-start(bf16[80,256]{1,0:T(8,128)(2,1)} %param.28) | copy-start | bytes 122884
  7.3 19.2 %copy-start.35 = (bf16[80,256]{1,0:T(8,128)(2,1)S(1)}, bf16[80,256]{1,0:T(8,128)(2,1)}, u32[]{:S(2)}) copy-start(bf16[80,256]{1,0:T(8,128)(2,1)} %param.30) | copy-start | bytes 122884
  7.3 19.2 %copy-start.25 = (bf16[64,6144]{1,0:T(8,128)(2,1)S(1)}, bf16[64,6144]{1,0:T(8,128)(2,1)}, u32[]{:S(2)}) copy-start(bf16[64,6144]{1,0:T(8,128)(2,1)} %param.35) | copy-start | bytes 2359300
  7.3 19.2 %copy-start.23 = (bf16[64,6144]{1,0:T(8,128)(2,1)S(1)}, bf16[64,6144]{1,0:T(8,128)(2,1)}, u32[]{:S(2)}) copy-start(bf16[64,6144]{1,0:T(8,128)(2,1)} %param.36) | copy-start | bytes 2359300
  7.3 39.1 %all-gather.5.cloned.1.call-start = ((), (), s32[]{:S(2)}) async-start(), calls=%async_computation.7 | async-start | bytes 2949120 | tf_op jit(solution)/shard_map/all_gather | solution.py:53
  8.0 108.5 %all-gather.7.cloned.1.call-start = ((), (), s32[]{:S(2)}) async-start(), calls=%async_computation.8 | async-start | bytes 7667712 | tf_op jit(solution)/shard_map/all_gather | solution.py:945
  11.9 34.5 %copy-start.2 = (bf16[1,256,2048]{2,1,0:T(8,128)(2,1)S(1)}, bf16[1,256,2048]{2,1,0:T(8,128)(2,1)}, u32[]{:S(2)}) copy-start(bf16[1,256,2048]{2,1,0:T(8,128)(2,1)} %param.19) | copy-start | bytes 3145732
  26.2 249.8 %all-gather.11.cloned.1.call-start = ((), (), s32[]{:S(2)}) async-start(), calls=%async_computation.10 | async-start | bytes 14155776 | tf_op jit(solution)/shard_map/all_gather | solution.py:945
  116.6 194.3 %all-gather.9.cloned.1.call-start = ((), (), s32[]{:S(2)}) async-start(), calls=%async_computation.9 | async-start | bytes 7077888 | tf_op jit(solution)/shard_map/all_gather | solution.py:53
  116.6 5.1 copy-start.1
  121.7 4.7 copy-start.32
  123.3 2.2 copy-start.22
  126.4 9.5 %copy-start.46 = (f32[8]{0:T(128)S(1)}, f32[8]{0:T(128)}, u32[]{:S(2)}) copy-start(f32[8]{0:T(128)} %param.21) | copy-start | bytes 100
  126.4 10.1 %copy-start.5 = (bf16[1,256,2048]{2,1,0:T(8,128)(2,1)S(1)}, bf16[1,256,2048]{2,1,0:T(8,128)(2,1)}, u32[]{:S(2)}) copy-start(bf16[1,256,2048]{2,1,0:T(8,128)(2,1)} %param.22) | copy-start | bytes 3145732
  126.4 11.9 %copy-start.11 = (bf16[2,80,640]{2,1,0:T(8,128)(2,1)S(1)}, bf16[2,80,640]{2,1,0:T(8,128)(2,1)}, u32[]{:S(2)}) copy-start(bf16[2,80,640]{2,1,0:T(8,128)(2,1)} %copy-done.10) | copy-start | bytes 614404
  135.0 249.7 %reduce-scatter.6.cloned.1.call-start = ((), (), s32[]{:S(2)}) async-start(), calls=%async_computation.11 | async-start | bytes 7077888 | tf_op jit(solution)/shard_map/reduce_scatter | solution.py:57
  140.9 56.1 %collective-permute-start = (bf16[128,2048]{1,0:T(8,128)(2,1)S(1)}, bf16[128,2048]{1,0:T(8,128)(2,1)}, u32[]{:S(2)}, u32[]{:S(2)}) collective-permute-start(bf16[128,2048]{1,0:T(8,128)(2,1)S(1)} %slice.177), channel_id=1, source_target_pairs={{8,0},{16,8},{24,16},{9,1},{17,9},{25,17},{10,2},{18,10},{26,18},{... | collective-permute-start | bytes 1572872 | tf_op jit(solution)/shard_map/ppermute | solution.py:21
  143.8 53.2 %copy-start.33 = (bf16[640,2048]{1,0:T(8,128)(2,1)S(1)}, bf16[640,2048]{1,0:T(8,128)(2,1)}, u32[]{:S(2)}) copy-start(bf16[640,2048]{1,0:T(8,128)(2,1)} %all-gather.5.cloned.1.call-done) | copy-start | bytes 7864324
  276.0 111.9 %copy-start.3 = (f32[256,2048]{1,0:T(8,128)}, f32[256,2048]{1,0:T(8,128)S(1)}, u32[]{:S(2)}) copy-start(f32[256,2048]{1,0:T(8,128)S(1)} %get-tuple-element.61.refs_1_.resid_ref) | copy-start | bytes 6291460
  276.0 12.7 %copy-start.15 = (bf16[4,256,2048]{2,1,0:T(8,128)(2,1)S(1)}, bf16[4,256,2048]{2,1,0:T(8,128)(2,1)}, u32[]{:S(2)}) copy-start(bf16[4,256,2048]{2,1,0:T(8,128)(2,1)} %copy-done.14) | copy-start | bytes 12582916
  276.0 12.7 %copy-start.45 = (bf16[4,512,3072]{2,1,0:T(8,128)(2,1)S(1)}, bf16[4,512,3072]{2,1,0:T(8,128)(2,1)}, u32[]{:S(2)}) copy-start(bf16[4,512,3072]{2,1,0:T(8,128)(2,1)} %all-gather.11.cloned.1.call-done) | copy-start | bytes 37748740
  288.7 11.6 %copy-start.47 = (bf16[4,256,2048]{2,1,0:T(8,128)(2,1)S(1)}, bf16[4,256,2048]{2,1,0:T(8,128)(2,1)}, u32[]{:S(2)}) copy-start(bf16[4,256,2048]{2,1,0:T(8,128)(2,1)} %get-tuple-element.52) | copy-start | bytes 12582916
  310.8 239.8 %reduce-scatter.8.cloned.1.call-start = ((), (), s32[]{:S(2)}) async-start(), calls=%async_computation.12 | async-start | bytes 14155776 | tf_op jit(solution)/shard_map/reduce_scatter | solution.py:948
  310.9 18.4 %copy-start.16 = (bf16[4,256,2048]{2,1,0:T(8,128)(2,1)S(1)}, bf16[4,256,2048]{2,1,0:T(8,128)(2,1)}, u32[]{:S(2)}) copy-start(bf16[4,256,2048]{2,1,0:T(8,128)(2,1)} %copy-done.14) | copy-start | bytes 12582916
  329.3 18.9 %copy-start.26 = (bf16[4,256,1536]{2,1,0:T(8,128)(2,1)}, bf16[4,256,1536]{2,1,0:T(8,128)(2,1)S(1)}, u32[]{:S(2)}) copy-start(bf16[4,256,1536]{2,1,0:T(8,128)(2,1)S(1)} %get-tuple-element.157) | copy-start | bytes 9437188
  348.2 215.8 %reduce-scatter.10.cloned.1.call-start = ((), (), s32[]{:S(2)}) async-start(), calls=%async_computation.13 | async-start | bytes 2949120 | tf_op jit(solution)/shard_map/reduce_scatter | solution.py:57
  351.9 112.0 %collective-permute-start.1 = (bf16[4,256,128]{1,2,0:T(8,128)(2,1)S(1)}, bf16[4,256,128]{1,2,0:T(8,128)(2,1)}, u32[]{:S(2)}, u32[]{:S(2)}) collective-permute-start(bf16[4,256,128]{1,2,0:T(8,128)(2,1)S(1)} %slice.181), channel_id=1, source_target_pairs={{0,8},{8,16},{16,24},{1,9},{9,17},{17,25},{2,10},{10,18},{18,26},{... | collective-permute-start | bytes 786440 | tf_op jit(solution)/shard_map/ppermute | solution.py:21
  384.7 81.1 %copy-start.27 = (bf16[4,256,768]{1,2,0:T(8,128)(2,1)S(1)}, bf16[4,256,768]{1,2,0:T(8,128)(2,1)}, u32[]{:S(2)}) copy-start(bf16[4,256,768]{1,2,0:T(8,128)(2,1)} %copy.109) | copy-start | bytes 4718596
  387.9 2.2 copy-start.4
  471.2 167.4 %reduce-scatter.12.cloned.1.call-start = ((), (), s32[]{:S(2)}) async-start(), calls=%async_computation.14 | async-start | bytes 7077888 | tf_op jit(solution)/shard_map/reduce_scatter | solution.py:948
  471.2 11.5 %copy-start.18 = (bf16[4,256,2048]{2,1,0:T(8,128)(2,1)S(1)}, bf16[4,256,2048]{2,1,0:T(8,128)(2,1)}, u32[]{:S(2)}) copy-start(bf16[4,256,2048]{2,1,0:T(8,128)(2,1)} %copy-done.17) | copy-start | bytes 12582916
  471.3 11.5 %copy-start.34 = (bf16[640,2048]{1,0:T(8,128)(2,1)S(1)}, bf16[640,2048]{1,0:T(8,128)(2,1)}, u32[]{:S(2)}) copy-start(bf16[640,2048]{1,0:T(8,128)(2,1)} %all-gather.5.cloned.1.call-done) | copy-start | bytes 7864324
  567.9 65.3 %collective-permute-start.2 = (bf16[128,768]{1,0:T(8,128)(2,1)S(1)}, bf16[128,768]{1,0:T(8,128)(2,1)S(1)}, u32[]{:S(2)}, u32[]{:S(2)}) collective-permute-start(bf16[128,768]{1,0:T(8,128)(2,1)S(1)} %slice.191), channel_id=1, source_target_pairs={{0,8},{8,16},{16,24},{1,9},{9,17},{17,25},{2,10},{10,18},{18,26},{... | collective-permute-start | bytes 589832 | tf_op jit(solution)/shard_map/ppermute | solution.py:21
  570.9 63.5 %all-to-all-start.1 = ((bf16[4,64,3072]{2,1,0:T(8,128)(2,1)}), bf16[4,64,3072]{2,1,0:T(8,128)(2,1)}, u32[]{:S(2)}, u32[]{:S(2)}) async-start(bf16[4,64,3072]{2,1,0:T(8,128)(2,1)} %reduce-scatter.8.cloned.1.call-done), calls=%async_computation.6 | async-start | bytes 3145728 | tf_op jit(solution)/shard_map/all_to_all | solution.py:49
  575.4 10.0 %copy-start.13 = (f32[2048]{0:T(1024)S(1)}, f32[2048]{0:T(1024)}, u32[]{:S(2)}) copy-start(f32[2048]{0:T(1024)} %copy-done.12) | copy-start | bytes 24580
  575.4 94.7 %reduce-scatter.14.cloned.1.call-start = ((), (), s32[]{:S(2)}) async-start(), calls=%async_computation.15 | async-start | bytes 1105920 | tf_op jit(solution)/shard_map/reduce_scatter | solution.py:57
  575.4 9.9 %copy-start.8 = (f32[256,2048]{1,0:T(8,128)S(1)}, f32[256,2048]{1,0:T(8,128)}, u32[]{:S(2)}) copy-start(f32[256,2048]{1,0:T(8,128)} %copy-done.7) | copy-start | bytes 6291460
  585.4 47.8 %copy-start.21 = (bf16[896,768]{1,0:T(8,128)(2,1)S(1)}, bf16[896,768]{1,0:T(8,128)(2,1)}, u32[]{:S(2)}) copy-start(bf16[896,768]{1,0:T(8,128)(2,1)} %copy-done.20) | copy-start | bytes 4128772
  636.7 7.4 %copy-start.43 = (bf16[64]{0:T(256)(128)(2,1)S(1)}, bf16[64]{0:T(256)(128)(2,1)}, u32[]{:S(2)}) copy-start(bf16[64]{0:T(256)(128)(2,1)} %param.34) | copy-start | bytes 388
  638.6 36.0 %all-to-all-start = ((bf16[4,64,1536]{2,1,0:T(8,128)(2,1)}), bf16[4,64,1536]{2,1,0:T(8,128)(2,1)S(1)}, u32[]{:S(2)}, u32[]{:S(2)}) async-start(bf16[4,64,1536]{2,1,0:T(8,128)(2,1)} %reduce-scatter.12.cloned.1.call-done), calls=%async_computation.4 | async-start | bytes 1572864 | tf_op jit(solution)/shard_map/all_to_all | solution.py:49
  642.2 32.8 %copy-start.28 = (bf16[64,2560]{1,0:T(8,128)(2,1)S(1)}, bf16[64,2560]{1,0:T(8,128)(2,1)}, u32[]{:S(2)}) copy-start(bf16[64,2560]{1,0:T(8,128)(2,1)} %param.25) | copy-start | bytes 983044
  674.7 3.3 copy-start.44
  674.7 3.8 copy-start.29
  (14 other events, 19.8 us)
Sparse Core Ops, SparseCore 0:
  9.8 36.5 all-gather.4
  48.0 68.5 all-gather.6
  118.8 116.6 all-gather.10
  237.0 70.4 all-gather.8
  311.0 73.6 reduce-scatter.5
  386.8 127.5 reduce-scatter.7
  516.7 39.1 reduce-scatter.9
  562.5 74.3 reduce-scatter.11
  639.8 30.2 reduce-scatter.13

commit v4 on v3

--- a/solution.py
+++ b/solution.py
@@ -227,8 +227,9 @@
 
 def recur_forward(
     T, S, L, C, xy_ref, rows_ref, wd_ref, wi_ref, cot_ref,
-    mixed_ref, states_ref, conv_ref, x_ref, halo_ref, inc_ref, cots_ref,
+    mixed_ref, own_ref, states_ref, conv_ref, x_ref, halo_ref, inc_ref, cots_ref,
     a_s, b_s, ext_s, fin_s, got_s, halo_send, halo_recv, send_sem, recv_sem, cot_send, cot_recv, own_sem,
+    pass_send, pass_recv,
 ):
     t = lax.axis_index("tok")
     SL = S * L // 8
@@ -354,6 +355,22 @@
         return 0
 
     lax.fori_loop(t + 1, T, drain, 0)
+    kept = own_ref.shape[1]
+    more = C - kept
+    handed = remote(
+        mixed_ref.at[:, pl.ds(kept, more)], own_ref.at[:, pl.ds(0, more)], pass_send, pass_recv, "seq", flip(me, 1)
+    )
+
+    @pl.when(lax.rem(me, 2) == 0)
+    def _():
+        handed.start()
+        own_ref[...] = mixed_ref[:, 0:kept]
+        handed.wait_send()
+
+    @pl.when(lax.rem(me, 2) == 1)
+    def _():
+        own_ref[:, more:kept] = mixed_ref[:, 0 : kept - more]
+        handed.wait_recv()
 
     @pl.when(t < T - 1)
     def _():
@@ -364,18 +381,21 @@
 
 
 def recur_backward(
-    T, S, L, C, gm_ref, xy_ref, st_ref, conv_ref, x_ref, halo_ref, inc_ref, rows_ref, wd_ref, wi_ref, part_ref, resid_ref,
+    T, S, L, C, gm_ref, xy_ref, st_ref, conv_ref, x_ref, halo_ref, inc_ref, rows_ref, wd_ref, wi_ref, part_ref,
     gxy_ref, gwd_ref, gwi_ref, small_ref, block_ref,
     a_s, g_s, r_s, sg_s, si_s, gc_s, ext_s, pst_s, fin_s, got_s, car_s, lap_send, lap_recv, send_sem, recv_sem,
-    *sum_refs,
+    y_s, y_sem, *sum_refs,
 ):
     t = lax.axis_index("tok")
     SL = S * L // 8
     half = 8 // S
     me = lax.axis_index("seq")
     greet_all(T, t, (flip(me, 1), flip(me, 2)))
+    load = pltpu.make_async_copy(xy_ref.at[:, :, pl.ds(C, C)], y_s, y_sem)
+    load.start()
     start_sum, middle_sum, total_sum, drain_sum = sum_rows(L, part_ref, *sum_refs)
     start_sum()
+    load.wait()
 
     def prepare(q, r0, col):
         cs = pl.ds(col, BW)
@@ -385,7 +405,7 @@
         sg_s[here, cs] = sg
         si_s[here, cs] = jax.nn.sigmoid(dot(low, wi_ref[cs, :]) + rows_ref[6:7, cs])
         put_wide(a_s, here, col, jnp.exp(-sg * rows_ref[8:9, cs]))
-        value, slope = gelu_parts(xy_ref[q, pl.ds(r0, TILE), pl.ds(C + col, BW)])
+        value, slope = gelu_parts(y_s[q, pl.ds(r0, TILE), cs])
         gm = gm_ref[here, cs]
         put_wide(g_s, here, col, gm * value)
         gxy_ref[q, pl.ds(r0, TILE), pl.ds(C + col, BW)] = (gm * st_ref[here, cs] * slope).astype(BF)
@@ -491,7 +511,7 @@
 
     for c in range(CHUNKS):
         rows = pl.ds(c * (L // CHUNKS), L // CHUNKS)
-        block_ref[rows, :] = (resid_ref[rows, :] + total_sum(c)).astype(BF)
+        block_ref[rows, :] = total_sum(c)
 
     @pl.when(t < T - 1)
     def _():
@@ -549,7 +569,7 @@
     )
 
 
-def run_forward(T, branches, rows, wd, wi, cot):
+def run_forward(T, quarter, branches, rows, wd, wi, cot):
     S, L, C = branches.shape
     hbm = pl.BlockSpec(memory_space=pl.ANY)
     C //= 2
@@ -560,6 +580,7 @@
         functools.partial(recur_forward, T, S, L, C),
         out_shape=(
             shape((M, C), BF),
+            shape((M, quarter), BF),
             shape((M, C)),
             shape((S, L, C), BF),
             shape((S, L, C), BF),
@@ -568,7 +589,7 @@
             shape((S,) + cot.shape, BF),
         ),
         in_specs=[VM] * 4 + [hbm],
-        out_specs=(VM,) * 6 + (hbm,),
+        out_specs=(VM,) * 7 + (hbm,),
         scratch_shapes=[
             split,
             split,
@@ -582,13 +603,15 @@
             dma((CHUNKS, 3)),
             dma((CHUNKS, 3)),
             dma,
+            dma,
+            dma,
         ],
         compiler_params=params(0),
         cost_estimate=pl.CostEstimate(flops=4 * M * C * BW, bytes_accessed=100000000, transcendentals=6 * M * C),
     )(branches, rows, wd, wi, cot)
 
 
-def run_backward(T, grad_mixed, branches, states, conv, branch_x, halo, inc, rows, wd, wi, part, resid):
+def run_backward(T, grad_mixed, branches, states, conv, branch_x, halo, inc, rows, wd, wi, part):
     S, L, C = branch_x.shape
     M = S * L
     dma = pltpu.SemaphoreType.DMA
@@ -601,9 +624,9 @@
             shape((C, BW)),
             shape((C, BW)),
             shape((8, C)),
-            shape(resid.shape, BF),
+            shape(part.shape[1:]),
         ),
-        in_specs=[VM] * 12,
+        in_specs=[VM, pl.BlockSpec(memory_space=pl.ANY)] + [VM] * 9,
         out_specs=(VM,) * 5,
         scratch_shapes=[split] * 3
         + [big] * 2
@@ -619,10 +642,11 @@
             dma((T,)),
             dma((T,)),
         ]
-        + sum_scratch(*resid.shape),
+        + [pltpu.VMEM((S, L, C), F32), dma]
+        + sum_scratch(*part.shape[1:]),
         compiler_params=params(1),
-        cost_estimate=pl.CostEstimate(flops=12 * M * C * BW, bytes_accessed=180000000, transcendentals=6 * M * C),
-    )(grad_mixed, branches, states, conv, branch_x, halo, inc, rows, wd, wi, part, resid)
+        cost_estimate=pl.CostEstimate(flops=12 * M * C * BW, bytes_accessed=40000000, transcendentals=0),
+    )(grad_mixed, branches, states, conv, branch_x, halo, inc, rows, wd, wi, part)
 
 
 def root_scale(v):
@@ -646,8 +670,9 @@
         resid, gain, cot, weight, keep, everyone = refs[1:7]
         rest = refs[7:]
     else:
-        tokens, gain, before, keep = refs[1:5]
-        rest = refs[5:]
+        tokens, gain, gates, keep, gates_sum = refs[1:6]
+        rest = refs[6:]
+        pair_s, pair_out, far_s, pair_send, pair_recv, far_send, far_recv = rest[7:]
     if shares:
         own_s, all_send, all_recv, own_sem = rest[7:]
     me = lax.axis_index("seq")
@@ -656,7 +681,30 @@
     barrier = pltpu.get_barrier_semaphore()
     for peer in (px, py):
         pl.semaphore_signal(barrier, inc=1, device_id={"seq": peer}, device_id_type=MESH)
-    pl.semaphore_wait(barrier, 2)
+    if kind == "third":
+        t, T = lax.axis_index("tok"), gates.shape[0]
+        pairs, spot, side = T // 2, t // 2, lax.rem(t, 2)
+        pl.semaphore_signal(barrier, inc=1, device_id={"tok": flip(t, 1)}, device_id_type=MESH)
+
+        @pl.loop(1, pairs)
+        def _(d):
+            pl.semaphore_signal(barrier, inc=1, device_id={"tok": lax.rem(t + 2 * d, T)}, device_id_type=MESH)
+
+        pl.semaphore_wait(barrier, 2 + pairs)
+
+        def near(k):
+            return remote(gates.at[2 * k + 1 - side], pair_s.at[k], pair_send.at[k], pair_recv.at[k], "tok", flip(t, 1))
+
+        def far(d):
+            k = lax.rem(spot + d, pairs)
+            return remote(pair_out.at[k], far_s.at[spot], far_send.at[d], far_recv.at[d], "tok", 2 * k + side)
+
+        @pl.loop(0, pairs)
+        def _(k):
+            near(k).start()
+
+    else:
+        pl.semaphore_wait(barrier, 2)
     start, middle, sums, drain = sum_rows(L, part, *rest[:7])
 
     def rows(c):
@@ -687,7 +735,7 @@
             own_s[r, :] = total.astype(BF)
         else:
             back = rms_back(tokens[r, :].astype(F32), gain[0:1, :], total)
-            keep[r, :] = before[r, :] + back
+            keep[r, :] = back
         if shares:
             share(c, 0).start()
             share(c, 1).start()
@@ -700,6 +748,17 @@
     start()
     for c in range(CHUNKS):
         middle(c)
+        if kind == "third" and c == 0:
+
+            @pl.loop(0, pairs)
+            def _(k):
+                near(k).wait()
+                pair_out[k] = (gates[2 * k + side].astype(F32) + pair_s[k].astype(F32)).astype(BF)
+
+            @pl.loop(1, pairs)
+            def _(d):
+                far(d).start()
+
         if c > 0:
             finish(c - 1)
         if shares and c > 1:
@@ -709,6 +768,14 @@
         forward(CHUNKS - 2)
         forward(CHUNKS - 1)
     drain()
+    if kind == "third":
+        gates_sum[...] = gates[t].astype(F32) + pair_s[spot].astype(F32)
+
+        @pl.loop(1, pairs)
+        def _(d):
+            far(d).wait()
+            gates_sum[...] += far_s[lax.rem(spot - d + pairs, pairs)].astype(F32)
+
     if shares:
         for c in range(CHUNKS):
             for k in (1, 2):
@@ -728,6 +795,11 @@
         outs.append(shape((S, L, D), BF))
         specs.append(pl.BlockSpec(memory_space=pl.ANY))
     scratch = sum_scratch(L, D)
+    if kind == "third":
+        T, *slab = ins[-1].shape
+        outs.append(shape(tuple(slab)))
+        specs.append(VM)
+        scratch += [pltpu.VMEM((T // 2, *slab), BF)] * 3 + [dma((T // 2,))] * 4
     if shares:
         scratch += [pltpu.VMEM((L, D), BF), dma((CHUNKS, 3)), dma((CHUNKS, 3)), dma((CHUNKS,))]
     return pl.pallas_call(
@@ -738,7 +810,7 @@
         scratch_shapes=scratch,
         compiler_params=params(collective_id, 40),
         cost_estimate=pl.CostEstimate(
-            flops=40 * L * D, bytes_accessed=(240 if shares else 120) * 1000000, transcendentals=L
+            flops=40 * L * D, bytes_accessed=20000000, transcendentals=L
         ),
     )(part, *ins)
 
@@ -787,10 +859,9 @@
     )(*ins)
 
 
-def plane_fill(S, T, L, slabs, *refs):
-    pack, first, gates, pack_out, first_out, gates_out, lent = refs[:7]
-    pack_send, pack_recv, row_send, row_recv, gate_send, gate_recv, relay_send, relay_recv = refs[7:15]
-    lent_send, lent_recv, own_sem = refs[15:]
+def plane_fill(S, T, slabs, *refs):
+    pack, gates, pack_out, gates_out, lent = refs[:5]
+    pack_send, pack_recv, gate_send, gate_recv, relay_send, relay_recv, lent_send, lent_recv, own_sem = refs[5:]
     me, t = lax.axis_index("seq"), lax.axis_index("tok")
     px, py, pd = flip(me, 1), flip(me, 2), S - 1 - me
     barrier = pltpu.get_barrier_semaphore()
@@ -818,11 +889,9 @@
 
     mine = [
         pltpu.make_async_copy(pack.at[me], pack_out.at[me], own_sem.at[0]),
-        pltpu.make_async_copy(first, first_out.at[me], own_sem.at[1]),
-        pltpu.make_async_copy(gates, gates_out.at[t], own_sem.at[2]),
+        pltpu.make_async_copy(gates, gates_out.at[t], own_sem.at[1]),
     ]
     loan = remote(gates_out.at[pl.ds(0, slabs)], lent, lent_send, lent_recv, "seq", px)
-    start, forward, drain = gather_rows(L, first, first_out, row_send, row_recv)
 
     @pl.loop(1, T // 2)
     def _(d):
@@ -830,10 +899,9 @@
 
     for copy in mine:
         copy.start()
-    start()
     for k in range(3):
         piece(k).start()
-    mine[2].wait()
+    mine[1].wait()
     relay(0).start()
 
     @pl.loop(1, T // 2)
@@ -849,12 +917,9 @@
     def _():
         loan.start()
 
-    forward()
     for k in range(3):
         piece(k).wait()
-    drain()
-    for copy in mine[:2]:
-        copy.wait()
+    mine[0].wait()
 
     @pl.loop(1, T // 2)
     def _(d):
@@ -873,27 +938,51 @@
         loan.wait_recv()
 
 
-def run_fill(S, T, slabs, collective_id, pack, first, gates):
-    L = first.shape[0]
+def run_fill(S, T, slabs, collective_id, pack, gates):
     dma = pltpu.SemaphoreType.DMA
     hbm = pl.BlockSpec(memory_space=pl.ANY)
     return pl.pallas_call(
-        functools.partial(plane_fill, S, T, L, slabs),
+        functools.partial(plane_fill, S, T, slabs),
         out_shape=(
             shape(pack.shape, BF),
-            shape((S,) + first.shape, BF),
             shape((T,) + gates.shape, BF),
             shape((slabs,) + gates.shape, BF),
         ),
-        in_specs=[hbm] * 3,
-        out_specs=(hbm,) * 4,
-        scratch_shapes=[dma((3,))] * 2
-        + [dma((CHUNKS, 3))] * 2
-        + [dma((T // 2,))] * 4
-        + [dma, dma, dma((3,))],
+        in_specs=[hbm] * 2,
+        out_specs=(hbm,) * 3,
+        scratch_shapes=[dma((3,))] * 2 + [dma((T // 2,))] * 4 + [dma, dma, dma((2,))],
         compiler_params=params(collective_id, 4),
-        cost_estimate=pl.CostEstimate(flops=0, bytes_accessed=220000000, transcendentals=0),
-    )(pack, first, gates)
+        cost_estimate=pl.CostEstimate(flops=0, bytes_accessed=80000000, transcendentals=0),
+    )(pack, gates)
+
+
+def plane_rows(S, L, first, out, send, recv, own_sem):
+    me = lax.axis_index("seq")
+    barrier = pltpu.get_barrier_semaphore()
+    for bit in (1, 2):
+        pl.semaphore_signal(barrier, inc=1, device_id={"seq": flip(me, bit)}, device_id_type=MESH)
+    pl.semaphore_wait(barrier, 2)
+    start, forward, drain = gather_rows(L, first, out, send, recv)
+    own = pltpu.make_async_copy(first, out.at[me], own_sem)
+    start()
+    own.start()
+    forward()
+    drain()
+    own.wait()
+
+
+def run_rows(S, collective_id, first):
+    dma = pltpu.SemaphoreType.DMA
+    hbm = pl.BlockSpec(memory_space=pl.ANY)
+    return pl.pallas_call(
+        functools.partial(plane_rows, S, first.shape[0]),
+        out_shape=shape((S,) + first.shape, BF),
+        in_specs=[hbm],
+        out_specs=hbm,
+        scratch_shapes=[dma((CHUNKS, 3)), dma((CHUNKS, 3)), dma],
+        compiler_params=params(collective_id, 4),
+        cost_estimate=pl.CostEstimate(flops=0, bytes_accessed=140000000, transcendentals=0),
+    )(first)
 
 
 def after(value, *others):
@@ -956,21 +1045,20 @@
     small = jnp.concatenate(
         [conv_weight, jnp.stack([conv_bias, decay_bias, input_bias, decay_param], axis=1)], axis=1
     )
+    gains = jnp.pad(jnp.stack([first_gain, second_gain], axis=1), ((0, 0), (0, SMALL - 2)))
+    pack_in = jnp.concatenate([cols_for(input_weight), cols_for(gelu_weight)], axis=2)
+    pack_in, gains = run_swap(S, ("slice", "all"), 2, pack_in, gains)
+    gains = jnp.pad(gains[:, :, :2].transpose(1, 0, 2).reshape(ds, 2 * S), ((0, rs - ds), (0, 0)))
+    small = jnp.concatenate([small, gains], axis=1)
     small = jnp.pad(small, ((0, 0), (0, SMALL - small.shape[1])))
     gates = jnp.concatenate([decay_gate, input_gate, small], axis=1)
-    gains = jnp.pad(jnp.stack([first_gain, second_gain], axis=1), ((0, 0), (0, SMALL - 2)))
-    pack_in = jnp.concatenate(
-        [cols_for(input_weight), cols_for(gelu_weight), jnp.broadcast_to(gains, (S,) + gains.shape)], axis=2
-    )
-    (pack_in,) = run_swap(S, ("slice",), 2, pack_in)
     sources = lax.broadcasted_iota(jnp.int32, (1, loss_weights.shape[0]), 1)
     picked = jnp.sum(jnp.where(source_ids[:, None] == sources, loss_weights[None, :], 0.0), axis=1)
     cot_low = (grad_output[0].astype(F32) * picked[:, None]).astype(BF)
     pack_f = jnp.concatenate([w.reshape(ds, S, FQ).swapaxes(0, 1) for w in (gate_weight, up_weight)], axis=2)
     weight_out = gather(output_weight, "tok")
-    pack_f, everyone, gates, lent = run_fill(
-        S, T, -(-most // rs), 3, after(pack_f, pack_in, weight_out), tokens[0], gates
-    )
+    pack_f, gates, lent = run_fill(S, T, -(-most // rs), 3, after(pack_f, pack_in), gates)
+    everyone = run_rows(S, 8, after(tokens[0], pack_f, weight_out))
 
     def r_rows(whole, lent):
         lent = lent[:most]
@@ -980,7 +1068,8 @@
 
     pack_in = d_rows(pack_in)
     weight_xy = pack_in[:, : 2 * C]
-    gain_one, gain_two = pack_in[:, 2 * C].astype(F32), pack_in[:, 2 * C + 1].astype(F32)
+    gains = gates[:, :ds, 2 * BW + 8 : 2 * BW + 8 + 2 * S].reshape(T, ds, S, 2).transpose(3, 2, 0, 1)
+    gain_one, gain_two = gains.reshape(2, D).astype(F32)
     gates = r_rows(gates.reshape(quarter, -1), lent.reshape(-1, lent.shape[-1]))
     weight_decay, weight_input = gates[:, :BW], gates[:, BW : 2 * BW]
     rows = gates[:, 2 * BW : 2 * BW + 8].T.astype(F32)
@@ -990,25 +1079,19 @@
     )
     weight_out = r_rows(weight_out, from_behind(weight_out[:most], "seq", -1))
 
-    pack_f = d_rows(after(pack_f, pack_in))
-    weight_gate, weight_up = pack_f[:, :FQ], pack_f[:, FQ:]
-
     everyone = everyone.astype(F32)
     normed = lax.optimization_barrier(rms_scale(everyone, gain_one).astype(BF))
+    ready = (pack_f, normed, rows, weight_decay, weight_input, weight_out)
+    pack_f, normed, rows, weight_decay, weight_input, weight_out = lax.optimization_barrier(ready)
+    pack_f, weight_xy = lax.optimization_barrier((pack_f, weight_xy))
+    pack_f = d_rows(pack_f)
+    weight_gate, weight_up = pack_f[:, :FQ], pack_f[:, FQ:]
     branches = forward_product(normed, weight_xy)
     weight_down = gather(after(down_weight, branches), "tok")
-    mixed, states, conv_low, branch_x, halo, incoming, cot_low = run_forward(
-        T, branches, rows, weight_decay, weight_input, cot_low
+    mixed, mixed_own, states, conv_low, branch_x, halo, incoming, cot_low = run_forward(
+        T, quarter, branches, rows, weight_decay, weight_input, cot_low
     )
-    mixed = mixed.reshape(S, length, C)
-    passed = from_behind(mixed[:, :, quarter:], "seq", 1)
-    mixed_own = jnp.pad(mixed, ((0, 0), (0, 0), (most, 0)))[:, :, :quarter]
-    mixed_own = jnp.where(off > 0, mixed_own, mixed[:, :, :quarter])
-    mixed_own = jnp.where(
-        lax.broadcasted_iota(jnp.int32, (1, 1, quarter), 2) < off,
-        jnp.pad(passed, ((0, 0), (0, 0), (0, quarter - most))),
-        mixed_own,
-    )
+    mixed, mixed_own = mixed.reshape(S, length, C), mixed_own.reshape(S, length, quarter)
     part = forward_product(mixed, weight_out).astype(BF)
     resid, second_normed = run_plane("first", 4, part, tokens[0], gain_two[None])
 
@@ -1017,7 +1100,7 @@
     hidden = gelu_product(gate_val, up_val).astype(BF)
     grad_down = token_product(hidden, cot_low).astype(BF)
     weight_down = after(weight_down, grad_down)
-    grad_down = scatter(grad_down, "tok").astype(F32)
+    grad_down = scatter(grad_down, "tok")
 
     grad_hidden = back_product(cot_low, weight_down)
     _, hidden_pull = jax.vjp(gelu_product, gate_val, up_val)
@@ -1025,33 +1108,46 @@
     grad_gate_up = jnp.concatenate([grad_gate_val.astype(BF), grad_up_val.astype(BF)], axis=2)
     grad_pack = token_product(second_normed, grad_gate_up).astype(BF)
     grad_second = back_product(after(grad_gate_up, grad_pack), pack_f)
-    grad_second = after(grad_second.astype(BF), grad_down)
+    grad_second = grad_second.astype(BF)
     grad_pack = d_scatter(grad_pack)
     picked = jnp.broadcast_to(picked[None], (8, 128))
     grad_resid, resid_low = run_plane(
         "second", 6, grad_second, resid, gain_two[None], grad_output[0], picked
     )
 
-    grad_out_w = token_product(mixed_own, resid_low).astype(BF)
+    grad_out_w = token_product(mixed_own, after(resid_low, grad_down)).astype(BF)
     grad_mixed = back_product(after(resid_low, grad_out_w), weight_out)
-    grad_out_w = scatter(grad_out_w, "tok").astype(F32)
+    grad_out_w = scatter(grad_out_w, "tok")
     part = forward_product(hidden, weight_down).astype(BF)
     grad_xy, grad_decay_w, grad_input_w, smalls, block_out = run_backward(
         T, grad_mixed.reshape(S * length, C), branches, states, conv_low, branch_x, halo, incoming, rows,
-        weight_decay, weight_input, part, resid,
+        weight_decay, weight_input, part,
     )
+    block_out = (resid + block_out).astype(BF)
     grad_i = token_product(normed, after(grad_xy, grad_pack)).astype(BF)
-    smalls = jnp.pad(smalls.T, ((0, 0), (0, BW - 8)))
+    smalls = jnp.pad(smalls.T, ((0, 0), (0, SMALL - 8)))
     grad_r = r_align(after(jnp.concatenate([grad_decay_w, grad_input_w, smalls], axis=1), grad_i))
     grad_normed = back_product(after(grad_xy, grad_i), weight_xy)
     grad_normed = after(grad_normed, grad_out_w)
 
-    grad_i = to_seq(d_scatter(grad_i)).astype(F32)
-    (grad_tokens,) = run_plane("third", 7, grad_normed.astype(BF), tokens[0], gain_one[None], grad_resid)
-    grad_r = scatter(grad_r, "tok").astype(F32)
+    grad_i = d_scatter(grad_i)
+    grad_tokens, grad_r = run_plane(
+        "third", 7, grad_normed.astype(BF), tokens[0], gain_one[None], grad_r.reshape(T, rs, -1)
+    )
+    grad_tokens = grad_resid + grad_tokens
     grad_pack = to_seq(grad_pack).swapaxes(0, 1).astype(F32)
     grad_gate_w = grad_pack[:, :, :FQ].reshape(ds, F)
     grad_up_w = grad_pack[:, :, FQ:].reshape(ds, F)
+    grad_down, grad_out_w = grad_down.astype(F32), grad_out_w.astype(F32)
+
+    def gain_grad(gain, *pairs):
+        return sum(jnp.sum(w.astype(F32) * g, axis=1) for w, g in pairs) / gain.astype(F32)
+
+    grad_gain_two = gain_grad(second_gain, (gate_weight, grad_gate_w), (up_weight, grad_up_w))
+    early = (block_out, grad_tokens, grad_r, grad_down, grad_out_w, grad_gate_w, grad_up_w, grad_gain_two)
+    grad_i, *early = lax.optimization_barrier((grad_i,) + early)
+    block_out, grad_tokens, grad_r, grad_down, grad_out_w, grad_gate_w, grad_up_w, grad_gain_two = early
+    grad_i = to_seq(grad_i).astype(F32)
 
     def columns(at):
         return jnp.concatenate(
@@ -1059,9 +1155,6 @@
         )
 
     grad_in_w, grad_gelu_w = columns(0), columns(C)
-
-    def gain_grad(gain, *pairs):
-        return sum(jnp.sum(w.astype(F32) * g, axis=1) for w, g in pairs) / gain.astype(F32)
 
     smalls = grad_r[:, 2 * BW :]
     return (
@@ -1078,7 +1171,7 @@
         smalls[:, 6],
         smalls[:, 7],
         grad_out_w,
-        gain_grad(second_gain, (gate_weight, grad_gate_w), (up_weight, grad_up_w)),
+        grad_gain_two,
         grad_gate_w,
         grad_up_w,
         grad_down,

time: 696 us -> 673 us (0.967)
  waiting for transfers between devices: 59.2 us -> 37.6 us
  local copies, waits for them, and re-layouts: 38.2 us -> 21 us
  Pallas kernels: 379 us -> 390 us
    reduce_scatter x3 -> x2, waiting for transfers between devices: 32 us -> 3.62 us  [scatter(): lax.psum_scatter(value.astype(BF), axis, scatter_dimension=0, tiled=True)]
    unnamed x101 -> x83, local copies, waits for them, and re-layouts: 22.6 us -> 9.73 us
    all_gather x2, waiting for transfers between devices: 19.6 us -> 8.16 us  [gather(): return lax.all_gather(value, axis, axis=0, tiled=True)]
    ppermute x3 -> x2, waiting for transfers between devices: 0.01 us -> 9.01 us  [from_behind(): return lax.ppermute(block, axis, route)]
    all_to_all x2, waiting for transfers between devices: 0.01 us -> 8.01 us  [to_seq(): return lax.all_to_all(parts, 'seq', split_axis=0, concat_axis=0, tiled=True)]
    pallas_call x1 -> x2, Pallas kernels: 59.6 us -> 62.3 us  [the longest x1 36 us: run_rows(): pl.pallas_call(functools.partial(plane_rows, S, first.shape[0]), out_shap...]
  transfers between devices with their start and end apart: 14 -> 12, of which waited for: 4 -> 6; matrix products, arithmetic and copies ran while one was open for 28% -> 29% of each run, Pallas kernels for 55% -> 59%
where the time goes in v4:
time: 673 us; the launch traced here: 664 us
  Pallas kernels  390 us (58%)
  matrix products  150 us (22%)
  waiting for transfers between devices  37.6 us (6%)
  other arithmetic  35 us (5%)
  local copies, waits for them, and re-layouts  21 us (3%)
  between operations  16.1 us (2%)
  starting transfers between devices  13.9 us (2%)
    pallas_call x3, Pallas kernels, run_plane(): pl.pallas_call(functools.partial(plane_sum, kind, L, D), out_shape=tuple(...  195 us
    pallas_call x1, Pallas kernels, run_backward(): pl.pallas_call(functools.partial(recur_backward, T, S, L, C), out_shape=(...  65.5 us
    pallas_call x1, Pallas kernels, run_forward(): pl.pallas_call(functools.partial(recur_forward, T, S, L, C), out_shape=(s...  53.9 us
    dot_general x5, matrix products, forward_product(): return jnp.dot(left, weight, preferred_element_type=F32)  51.6 us
    dot_general x4, matrix products, back_product(): lax.dot_general(grad, weight, (((2,), (1,)), ((), ())), preferred_element...  50.6 us
    dot_general x4, matrix products, token_product(): lax.dot_general(left, grad, (((0, 1), (0, 1)), ((), ())), preferred_eleme...  48 us
    pallas_call x1, Pallas kernels, run_rows(): pl.pallas_call(functools.partial(plane_rows, S, first.shape[0]), out_shap...  36 us
    pallas_call x1, Pallas kernels, run_fill(): pl.pallas_call(functools.partial(plane_fill, S, T, slabs), out_shape=(sha...  26.4 us
  transfers between devices with their start and end apart: 12, of which 6 were waited for; matrix products, arithmetic and copies ran while one was open for 29% of the time, Pallas kernels for 59%

profile of v4, /device:TPU:0, one launch (start us, length us, event | category | flops | bytes accessed | tf_op | source)
XLA Modules:
  0.0 664.2 jit_solution(2531943673969238947)
XLA Ops:
  10.6 1.1 slice_bitcast_fusion.15
  11.8 14.2 %shard_map.314 = (bf16[4,64,1536]{2,1,0:T(8,128)(2,1)}, bf16[4,64,128]{2,1,0:T(8,128)(2,1)S(1)}) custom-call(bf16[4,64,1536]{2,1,0:T(8,128)(2,1)S(1)} %maximum_maximum_fusion.refs_0_, bf16[64,128]{1,0:T(8,128)(2,1)S(1)} %pad.37.refs_1_), custom_call_target="tpu_custom_call" | custom-call | bytes 25559040 | tf_op jit(solution)/shard_map/pallas_call | solution.py:851
  26.9 26.4 %shard_map.315 = (bf16[4,64,3072]{2,1,0:T(8,128)(2,1)}, bf16[8,80,640]{2,1,0:T(8,128)(2,1)S(1)}, bf16[2,80,640]{2,1,0:T(8,128)(2,1)S(1)}) custom-call(bf16[4,64,3072]{2,1,0:T(8,128)(2,1)S(1)} %pad_maximum_fusion.1.refs_0_, bf16[80,640]{1,0:T(8,128)(2,1)S(1)} %fusion.33.refs_1_), custom_call_target="tpu_custom_call" | custom-call | bytes 80000000 | tf_op jit(solution)/shard_map/pallas_call | solution.py:944
  54.2 1.2 compare_select_fusion
  55.4 1.1 copy.101
  56.5 1.2 copy.105
  59.7 36.0 %shard_map.316 = bf16[4,256,2048]{2,1,0:T(8,128)(2,1)S(1)} custom-call(bf16[256,2048]{1,0:T(8,128)(2,1)S(1)} %bitcast.148), custom_call_target="tpu_custom_call" | custom-call | bytes 140000000 | tf_op jit(solution)/shard_map/pallas_call | solution.py:977
  95.8 1.3 collective-permute-start
  98.0 3.1 fusion.2
  101.1 9.0 %collective-permute-done = bf16[128,2048]{1,0:T(8,128)(2,1)S(1)} collective-permute-done((bf16[128,2048]{1,0:T(8,128)(2,1)S(1)}, bf16[128,2048]{1,0:T(8,128)(2,1)S(1)}, u32[]{:S(2)}, u32[]{:S(2)}) %collective-permute-start) | collective-permute-done | bytes 524320 | tf_op jit(solution)/shard_map/ppermute | solution.py:21
  110.1 3.1 fusion.25
  113.2 7.2 %all-gather.7.cloned.1.call-done = bf16[4,512,1536]{2,1,0:T(8,128)(2,1)} async-done(((bf16[4,64,1536]{2,1,0:T(8,128)(2,1)}), bf16[4,512,1536]{2,1,0:T(8,128)(2,1)}) %all-gather.7.cloned.1.call-update) | async-done | bytes 6291472 | tf_op jit(solution)/shard_map/all_gather | solution.py:1034
  120.5 11.9 %fusion.18.xy_ref = f32[4,256,1536]{2,1,0:T(8,128)} fusion(bf16[4,256,2048]{2,1,0:T(8,128)(2,1)} %fusion.2, bf16[2048,1536]{1,0:T(8,128)(2,1)} %bitcast.178), kind=kOutput, calls=%fused_computation.28 | convolution fusion | flops 6442450944 | bytes 16777216 | tf_op jit(solution)/shard_map/dot_general | solution.py:37
  133.7 1.8 multiply_convert_fusion.2.cot_ref
  135.6 53.9 %shard_map.317 = (bf16[1024,768]{1,0:T(8,128)(2,1)}, bf16[1024,640]{1,0:T(8,128)(2,1)}, f32[1024,768]{1,0:T(8,128)}, bf16[4,256,768]{2,1,0:T(8,128)(2,1)}, bf16[...) custom-call(f32[4,256,1536]{2,1,0:T(8,128)} %fusion.18.xy_ref, ...), custom_call_target="tpu_custom_call" | custom-call | flops 805306368 | bytes 100000000 | tf_op jit(solution)/shard_map/pallas_call | solution.py:579
  189.4 5.1 convolution_convert_fusion.1.refs_0_
  194.5 71.9 %shard_map.318 = (f32[256,2048]{1,0:T(8,128)S(1)}, bf16[4,256,2048]{2,1,0:T(8,128)(2,1)S(1)}) custom-call(bf16[4,256,2048]{2,1,0:T(8,128)(2,1)S(1)} %convolution_convert_fusion.1.refs_0_, bf16[256,2048]{1,0:T(8,128)(2,1)S(1)} %bitcast.149, f32[1,2048]{1,0:T(1,128)S(1)} %unstack.12.refs_2_), custom_call_target="tpu_custom_call" | custom-call | flops 20971520 | bytes 20000000 | tf_op jit(solution)/shard_map/pallas_call | solution.py:805
  266.5 2.0 copy-done.5
  268.5 11.9 %fusion.11 = f32[4,256,1536]{2,1,0:T(8,128)} fusion(bf16[4,256,2048]{2,1,0:T(8,128)(2,1)} %copy-done.5, bf16[2048,3072]{1,0:T(8,128)(2,1)} %bitcast.175), kind=kOutput, calls=%fused_computation.20 | convolution fusion | flops 6442450944 | bytes 16777216 | tf_op jit(solution)/shard_map/dot_general | solution.py:37
  280.4 11.6 %multiply_convert_fusion.1 = (bf16[4,256,1536]{2,1,0:T(8,128)(2,1)}, f32[4,256,1536]{2,1,0:T(8,128)}) fusion(f32[4,256,1536]{2,1,0:T(8,128)} %fusion.11, bf16[4,256,2048]{2,1,0:T(8,128)(2,1)S(1)} %copy-done.6, bf16[2048,3072]{1,0:T(8,128)(2,1)S(1)} %bitcast.177), kind=kOutput, calls=%fused_computation.31 | convolution fusion | flops 6458179584 | bytes 26214400 | tf_op jit(solution)/shard_map/dot_general | solution.py:37
  292.0 10.6 %bitcast_convert_fusion.2 = bf16[1536,2048]{1,0:T(8,128)(2,1)} fusion(bf16[4,256,1536]{2,1,0:T(8,128)(2,1)} %get-tuple-element.225, bf16[4,256,2048]{2,1,0:T(8,128)(2,1)S(1)} %copy-done.39), kind=kOutput, calls=%fused_computation.2 | convolution fusion | flops 6445596672 | bytes 13631488 | tf_op jit(solution)/shard_map/dot_general | solution.py:45
  303.0 8.2 %all-gather.9.cloned.1.call-done = bf16[1536,2048]{1,0:T(8,128)(2,1)} async-done(((bf16[192,2048]{1,0:T(8,128)(2,1)}), bf16[1536,2048]{1,0:T(8,128)(2,1)}) %all-gather.9.cloned.1.call-update) | async-done | bytes 6291472 | tf_op jit(solution)/shard_map/all_gather | solution.py:53
  311.2 17.8 %fusion.9 = (bf16[4,256,1536]{2,1,0:T(8,128)(2,1)S(1)}, bf16[4,256,1536]{2,1,0:T(8,128)(2,1)}) fusion(f32[4,256,1536]{2,1,0:T(8,128)} %fusion.11, f32[4,256,1536]{2,1,0:T(8,128)} %get-tuple-element.226, bf16[4,256,2048]{2,1,0:T(8,128)(2,1)} %get-tuple-element.82, bf16[1536,2048]{1,0:T(8,128)(2,1)} %all-gather.9.cloned.1.call-done), kind=kOutput, calls=%fused_computation.16 | convolution fusion | flops 6480199680 | bytes 29360128 | tf_op jit(solution)/shard_map/dot_general | solution.py:41
  329.0 18.9 %bitcast_convert_fusion = bf16[2048,3072]{1,0:T(8,128)(2,1)} fusion(bf16[4,256,2048]{2,1,0:T(8,128)(2,1)S(1)} %copy-done.7, bf16[4,256,1536]{2,1,0:T(8,128)(2,1)} %get-tuple-element.198, bf16[4,256,1536]{2,1,0:T(8,128)(2,1)S(1)} %get-tuple-element.197), kind=kOutput, calls=%fused_computation | convolution fusion | flops 12903776256 | bytes 23068672 | tf_op jit(solution)/shard_map/dot_general | solution.py:45
  348.1 6.3 pad_maximum_fusion
  354.4 17.8 %convolution_convert_fusion.refs_0_ = bf16[4,256,2048]{2,1,0:T(8,128)(2,1)S(1)} fusion(bf16[4,256,3072]{2,1,0:T(8,128)(2,1)} %pad_maximum_fusion, bf16[2048,3072,1]{1,0,2:T(8,128)(2,1)} %bitcast.176), kind=kOutput, calls=%fused_computation.34 | convolution fusion | flops 12886999040 | bytes 23068672 | tf_op jit(solution)/shard_map/dot_general | solution.py:41
  372.8 74.5 %shard_map.319 = (f32[256,2048]{1,0:T(8,128)S(1)}, bf16[4,256,2048]{2,1,0:T(8,128)(2,1)S(1)}) custom-call(bf16[4,256,2048]{2,1,0:T(8,128)(2,1)S(1)} %convolution_convert_fusion.refs_0_, f32[256,2048]{1,0:T(8,128)S(1)} %get-tuple-element.90.refs_1_, f32[1,2048]{1,0:T(1,128)S(1)} %unstack.12.refs_2_, bf16[256,2048]{1,0:T(8,128)(2,1)S(1)} %bitcast.151, ...), custom_call_target="tpu_custom_call" | custom-call | flops 20971520 | bytes 20000000 | tf_op jit(solution)/shard_map/pallas_call | solution.py:805
  447.3 1.3 copy-done.3
  448.6 2.0 copy-done.8
  450.6 7.0 %bitcast_convert_fusion.3 = bf16[640,2048]{1,0:T(8,128)(2,1)} fusion(bf16[4,256,640]{2,1,0:T(8,128)(2,1)} %bitcast.181, bf16[4,256,2048]{2,1,0:T(8,128)(2,1)} %copy-done.8), kind=kOutput, calls=%fused_computation.33 | convolution fusion | flops 2685665280 | bytes 8126464 | tf_op jit(solution)/shard_map/dot_general | solution.py:45
  457.9 11.2 %fusion.20.part_ref = bf16[4,256,2048]{2,1,0:T(8,128)(2,1)} fusion(bf16[4,256,1536]{2,1,0:T(8,128)(2,1)} %get-tuple-element.225, bf16[1536,2048]{1,0:T(8,128)(2,1)} %all-gather.9.cloned.1.call-done), kind=kOutput, calls=%fused_computation.35 | convolution fusion | flops 6444548096 | bytes 13631488 | tf_op jit(solution)/shard_map/dot_general | solution.py:37
  469.2 5.1 fusion.26
  474.3 65.5 %shard_map.320 = (bf16[4,256,1536]{2,1,0:T(8,128)(2,1)}, f32[768,256]{1,0:T(8,128)}, f32[768,256]{1,0:T(8,128)}, f32[8,768]{1,0:T(8,128)}, f32[256,2048]{1,0:T(8,128)}) custom-call(f32[1024,768]{1,0:T(8,128)} %bitcast.161, f32[4,256,1536]{2,1,0:T(8,128)} %fusion.18.xy_ref, f32[1024,768]{1,0:T(8,128)} %get-tuple-element.95.st_ref, ...), custom_call_target="tpu_custom_call" | custom-call | flops 2415919104 | bytes 40000000 | tf_op jit(solution)/shard_map/pallas_call | solution.py:620
  539.8 11.6 %bitcast_convert_fusion.1 = bf16[2048,1536]{1,0:T(8,128)(2,1)} fusion(bf16[4,256,2048]{2,1,0:T(8,128)(2,1)} %fusion.2, bf16[4,256,1536]{2,1,0:T(8,128)(2,1)} %get-tuple-element.104), kind=kOutput, calls=%fused_computation.1 | convolution fusion | flops 6445596672 | bytes 13631488 | tf_op jit(solution)/shard_map/dot_general | solution.py:45
  552.4 2.6 convert_element_type.141
  555.0 2.5 select_maximum_fusion
  557.4 1.3 add_convert_fusion
  558.7 3.6 reduce-scatter.11.cloned.1.call-done
  562.3 1.9 convert_element_type.142
  564.3 1.4 convert_dynamic-update-slice_fusion
  566.7 3.4 collective-permute-start.1
  570.0 4.3 all-to-all-start
  574.4 9.9 %fusion.16.refs_0_ = bf16[4,256,2048]{2,1,0:T(8,128)(2,1)S(1)} fusion(bf16[4,256,1536]{2,1,0:T(8,128)(2,1)} %get-tuple-element.104, bf16[2048,1536]{1,0:T(8,128)(2,1)} %bitcast.179), kind=kOutput, calls=%fused_computation.26 | convolution fusion | flops 6442450944 | bytes 13631488 | tf_op jit(solution)/shard_map/dot_general | solution.py:41
  584.6 48.2 %shard_map.321 = (f32[256,2048]{1,0:T(8,128)S(1)}, f32[80,640]{1,0:T(8,128)S(1)}) custom-call(bf16[4,256,2048]{2,1,0:T(8,128)(2,1)S(1)} %fusion.16.refs_0_, bf16[256,2048]{1,0:T(8,128)(2,1)S(1)} %bitcast.150, f32[1,2048]{1,0:T(1,128)S(1)} %unstack.13.refs_2_, bf16[8,80,640]{2,1,0:T(8,128)(2,1)S(1)} %bitcast.152), custom_call_target="tpu_custom_call" | custom-call | flops 20971520 | bytes 20000000 | tf_op jit(solution)/shard_map/pallas_call | solution.py:805
  632.7 1.7 add.96
  634.4 1.8 convert_bitcast_fusion
  640.2 3.8 all-to-all-start.1
  646.0 8.0 %all-to-all-done.1 = bf16[4,64,1536]{2,1,0:T(8,128)(2,1)S(1)} async-done(((bf16[4,64,1536]{2,1,0:T(8,128)(2,1)}), bf16[4,64,1536]{2,1,0:T(8,128)(2,1)S(1)}, u32[]{:S(2)}, u32[]{:S(2)}) %all-to-all-start.1) | async-done | bytes 786464 | tf_op jit(solution)/shard_map/all_to_all | solution.py:49
  (160 shorter events, 21.5 us)
Async XLA Ops:
  7.2 19.0 %copy-start.19 = (bf16[64,6144]{1,0:T(8,128)(2,1)S(1)}, bf16[64,6144]{1,0:T(8,128)(2,1)}, u32[]{:S(2)}) copy-start(bf16[64,6144]{1,0:T(8,128)(2,1)} %param.35) | copy-start | bytes 2359300
  7.2 19.0 %copy-start.17 = (bf16[64,6144]{1,0:T(8,128)(2,1)S(1)}, bf16[64,6144]{1,0:T(8,128)(2,1)}, u32[]{:S(2)}) copy-start(bf16[64,6144]{1,0:T(8,128)(2,1)} %param.36) | copy-start | bytes 2359300
  7.2 52.5 %all-gather.5.cloned.1.call-start = ((), (), s32[]{:S(2)}) async-start(), calls=%async_computation.6 | async-start | bytes 2949120 | tf_op jit(solution)/shard_map/all_gather | solution.py:53
  7.9 112.4 %all-gather.7.cloned.1.call-start = ((), (), s32[]{:S(2)}) async-start(), calls=%async_computation.7 | async-start | bytes 7077888 | tf_op jit(solution)/shard_map/all_gather | solution.py:1034
  11.8 14.9 %copy-start.30 = (bf16[80,4]{0,1:T(4,128)(2,1)S(1)}, bf16[80,4]{0,1:T(4,128)(2,1)}, u32[]{:S(2)}) copy-start(bf16[80,4]{0,1:T(4,128)(2,1)} %param.26) | copy-start | bytes 1924
  11.8 14.9 %copy-start.31 = (bf16[80]{0:T(256)(128)(2,1)S(1)}, bf16[80]{0:T(256)(128)(2,1)}, u32[]{:S(2)}) copy-start(bf16[80]{0:T(256)(128)(2,1)} %param.27) | copy-start | bytes 484
  11.8 14.9 %copy-start.32 = (bf16[80]{0:T(256)(128)(2,1)S(1)}, bf16[80]{0:T(256)(128)(2,1)}, u32[]{:S(2)}) copy-start(bf16[80]{0:T(256)(128)(2,1)} %param.29) | copy-start | bytes 484
  11.8 14.9 %copy-start.33 = (bf16[80]{0:T(256)(128)(2,1)S(1)}, bf16[80]{0:T(256)(128)(2,1)}, u32[]{:S(2)}) copy-start(bf16[80]{0:T(256)(128)(2,1)} %param.31) | copy-start | bytes 484
  11.8 14.9 %copy-start.34 = (bf16[80]{0:T(256)(128)(2,1)S(1)}, bf16[80]{0:T(256)(128)(2,1)}, u32[]{:S(2)}) copy-start(bf16[80]{0:T(256)(128)(2,1)} %param.32) | copy-start | bytes 484
  11.8 15.1 %copy-start.27 = (bf16[80,256]{1,0:T(8,128)(2,1)S(1)}, bf16[80,256]{1,0:T(8,128)(2,1)}, u32[]{:S(2)}) copy-start(bf16[80,256]{1,0:T(8,128)(2,1)} %param.30) | copy-start | bytes 122884
  11.8 15.0 %copy-start.28 = (bf16[80,256]{1,0:T(8,128)(2,1)S(1)}, bf16[80,256]{1,0:T(8,128)(2,1)}, u32[]{:S(2)}) copy-start(bf16[80,256]{1,0:T(8,128)(2,1)} %param.28) | copy-start | bytes 122884
  26.1 242.3 %all-gather.11.cloned.1.call-start = ((), (), s32[]{:S(2)}) async-start(), calls=%async_computation.9 | async-start | bytes 14155776 | tf_op jit(solution)/shard_map/all_gather | solution.py:1034
  53.3 6.4 copy-start
  57.9 40.0 %copy-start.25 = (f32[1,4,8,64]{3,2,0,1:T(8,128)}, f32[1,4,8,64]{3,2,0,1:T(8,128)S(1)}, u32[]{:S(2)}) copy-start(f32[1,4,8,64]{3,2,0,1:T(8,128)S(1)} %get-tuple-element.224) | copy-start | bytes 24580
  59.7 36.0 %copy-start.14 = (bf16[640,2048]{1,0:T(8,128)(2,1)S(1)}, bf16[640,2048]{1,0:T(8,128)(2,1)}, u32[]{:S(2)}) copy-start(bf16[640,2048]{1,0:T(8,128)(2,1)} %all-gather.5.cloned.1.call-done) | copy-start | bytes 7864324
  95.8 14.3 %collective-permute-start = (bf16[128,2048]{1,0:T(8,128)(2,1)S(1)}, bf16[128,2048]{1,0:T(8,128)(2,1)S(1)}, u32[]{:S(2)}, u32[]{:S(2)}) collective-permute-start(bf16[128,2048]{1,0:T(8,128)(2,1)S(1)} %slice.161), channel_id=1, source_target_pairs={{8,0},{16,8},{24,16},{9,1},{17,9},{25,17},{10,2},{18,10},{26,18},{... | collective-permute-start | bytes 1572872 | tf_op jit(solution)/shard_map/ppermute | solution.py:21
  120.4 12.7 %copy-start.38 = (f32[8]{0:T(128)S(1)}, f32[8]{0:T(128)}, u32[]{:S(2)}) copy-start(f32[8]{0:T(128)} %param.21) | copy-start | bytes 100
  120.4 13.3 %copy-start.1 = (bf16[1,256,2048]{2,1,0:T(8,128)(2,1)S(1)}, bf16[1,256,2048]{2,1,0:T(8,128)(2,1)}, u32[]{:S(2)}) copy-start(bf16[1,256,2048]{2,1,0:T(8,128)(2,1)} %param.22) | copy-start | bytes 3145732
  120.4 190.8 %all-gather.9.cloned.1.call-start = ((), (), s32[]{:S(2)}) async-start(), calls=%async_computation.8 | async-start | bytes 7077888 | tf_op jit(solution)/shard_map/all_gather | solution.py:53
  132.3 318.2 %reduce-scatter.5.cloned.1.call-start = ((), (), s32[]{:S(2)}) async-start(), calls=%async_computation.10 | async-start | bytes 7077888 | tf_op jit(solution)/shard_map/reduce_scatter | solution.py:57
  135.6 53.9 %copy-start.15 = (bf16[768,2048]{1,0:T(8,128)(2,1)S(1)}, bf16[768,2048]{1,0:T(8,128)(2,1)}, u32[]{:S(2)}) copy-start(bf16[768,2048]{1,0:T(8,128)(2,1)} %fusion.25) | copy-start | bytes 9437188
  266.5 2.0 copy-start.5
  268.5 11.9 %copy-start.6 = (bf16[4,256,2048]{2,1,0:T(8,128)(2,1)S(1)}, bf16[4,256,2048]{2,1,0:T(8,128)(2,1)}, u32[]{:S(2)}) copy-start(bf16[4,256,2048]{2,1,0:T(8,128)(2,1)} %copy-done.5) | copy-start | bytes 12582916
  268.5 11.9 %copy-start.37 = (bf16[4,512,3072]{2,1,0:T(8,128)(2,1)S(1)}, bf16[4,512,3072]{2,1,0:T(8,128)(2,1)}, u32[]{:S(2)}) copy-start(bf16[4,512,3072]{2,1,0:T(8,128)(2,1)} %all-gather.11.cloned.1.call-done) | copy-start | bytes 37748740
  280.4 11.6 %copy-start.39 = (bf16[4,256,2048]{2,1,0:T(8,128)(2,1)S(1)}, bf16[4,256,2048]{2,1,0:T(8,128)(2,1)}, u32[]{:S(2)}) copy-start(bf16[4,256,2048]{2,1,0:T(8,128)(2,1)} %get-tuple-element.82) | copy-start | bytes 12582916
  302.6 237.2 %reduce-scatter.7.cloned.1.call-start = ((), (), s32[]{:S(2)}) async-start(), calls=%async_computation.11 | async-start | bytes 14155776 | tf_op jit(solution)/shard_map/reduce_scatter | solution.py:1037
  311.2 17.8 %copy-start.7 = (bf16[4,256,2048]{2,1,0:T(8,128)(2,1)S(1)}, bf16[4,256,2048]{2,1,0:T(8,128)(2,1)}, u32[]{:S(2)}) copy-start(bf16[4,256,2048]{2,1,0:T(8,128)(2,1)} %copy-done.5) | copy-start | bytes 12582916
  329.0 18.9 %copy-start.21 = (bf16[4,256,1536]{2,1,0:T(8,128)(2,1)}, bf16[4,256,1536]{2,1,0:T(8,128)(2,1)S(1)}, u32[]{:S(2)}) copy-start(bf16[4,256,1536]{2,1,0:T(8,128)(2,1)S(1)} %get-tuple-element.197) | copy-start | bytes 9437188
  347.9 214.4 %reduce-scatter.11.cloned.1.call-start = ((), (), s32[]{:S(2)}) async-start(), calls=%async_computation.13 | async-start | bytes 2949120 | tf_op jit(solution)/shard_map/reduce_scatter | solution.py:57
  354.4 18.4 %copy-start.2 = (bf16[1,256,2048]{2,1,0:T(8,128)(2,1)S(1)}, bf16[1,256,2048]{2,1,0:T(8,128)(2,1)}, u32[]{:S(2)}) copy-start(bf16[1,256,2048]{2,1,0:T(8,128)(2,1)} %param.22) | copy-start | bytes 3145732
  447.3 1.3 copy-start.3
  448.6 2.0 copy-start.8
  457.6 182.5 %reduce-scatter.9.cloned.1.call-start = ((), (), s32[]{:S(2)}) async-start(), calls=%async_computation.12 | async-start | bytes 7077888 | tf_op jit(solution)/shard_map/reduce_scatter | solution.py:1037
  457.9 11.3 %copy-start.9 = (bf16[4,256,2048]{2,1,0:T(8,128)(2,1)S(1)}, bf16[4,256,2048]{2,1,0:T(8,128)(2,1)}, u32[]{:S(2)}) copy-start(bf16[4,256,2048]{2,1,0:T(8,128)(2,1)} %copy-done.8) | copy-start | bytes 12582916
  457.9 11.2 %copy-start.16 = (bf16[768,2048]{1,0:T(8,128)(2,1)S(1)}, bf16[768,2048]{1,0:T(8,128)(2,1)}, u32[]{:S(2)}) copy-start(bf16[768,2048]{1,0:T(8,128)(2,1)} %fusion.25) | copy-start | bytes 9437188
  552.3 5.1 copy-start.22
  566.7 17.6 %collective-permute-start.1 = (bf16[128,640]{1,0:T(8,128)(2,1)S(1)}, bf16[128,640]{1,0:T(8,128)(2,1)S(1)}, u32[]{:S(2)}, u32[]{:S(2)}) collective-permute-start(bf16[128,640]{1,0:T(8,128)(2,1)S(1)} %slice.164), channel_id=1, source_target_pairs={{0,8},{8,16},{16,24},{1,9},{9,17},{17,25},{2,10},{10,18},{18,26},{... | collective-permute-start | bytes 491528 | tf_op jit(solution)/shard_map/ppermute | solution.py:21
  570.0 64.4 %all-to-all-start = ((bf16[4,64,3072]{2,1,0:T(8,128)(2,1)}), bf16[4,64,3072]{2,1,0:T(8,128)(2,1)}, u32[]{:S(2)}, u32[]{:S(2)}) async-start(bf16[4,64,3072]{2,1,0:T(8,128)(2,1)} %reduce-scatter.7.cloned.1.call-done), calls=%async_computation.4 | async-start | bytes 3145728 | tf_op jit(solution)/shard_map/all_to_all | solution.py:49
  574.4 9.9 %copy-start.13 = (bf16[896,640]{1,0:T(8,128)(2,1)S(1)}, bf16[896,640]{1,0:T(8,128)(2,1)}, u32[]{:S(2)}) copy-start(bf16[896,640]{1,0:T(8,128)(2,1)} %copy-done.12) | copy-start | bytes 3440644
  584.3 48.4 %copy-start.4 = (f32[256,2048]{1,0:T(8,128)S(1)}, f32[256,2048]{1,0:T(8,128)}, u32[]{:S(2)}) copy-start(f32[256,2048]{1,0:T(8,128)} %copy-done.3) | copy-start | bytes 6291460
  636.5 2.1 copy-start.20
  636.6 3.6 copy-start.10
  636.6 2.2 copy-start.35
  636.7 1.3 copy-start.11
  638.6 15.8 %copy-start.23 = (bf16[64,2560]{1,0:T(8,128)(2,1)S(1)}, bf16[64,2560]{1,0:T(8,128)(2,1)}, u32[]{:S(2)}) copy-start(bf16[64,2560]{1,0:T(8,128)(2,1)} %param.25) | copy-start | bytes 983044
  640.2 15.2 %copy-start.24 = (bf16[64,2560]{1,0:T(8,128)(2,1)S(1)}, bf16[64,2560]{1,0:T(8,128)(2,1)}, u32[]{:S(2)}) copy-start(bf16[64,2560]{1,0:T(8,128)(2,1)} %param.24) | copy-start | bytes 983044
  640.2 13.9 %all-to-all-start.1 = ((bf16[4,64,1536]{2,1,0:T(8,128)(2,1)}), bf16[4,64,1536]{2,1,0:T(8,128)(2,1)S(1)}, u32[]{:S(2)}, u32[]{:S(2)}) async-start(bf16[4,64,1536]{2,1,0:T(8,128)(2,1)} %reduce-scatter.9.cloned.1.call-done), calls=%async_computation.5 | async-start | bytes 1572864 | tf_op jit(solution)/shard_map/all_to_all | solution.py:49
  646.0 10.4 %copy-start.36 = (bf16[64]{0:T(256)(128)(2,1)S(1)}, bf16[64]{0:T(256)(128)(2,1)}, u32[]{:S(2)}) copy-start(bf16[64]{0:T(256)(128)(2,1)} %param.23) | copy-start | bytes 388
  (4 other events, 3.8 us)
Sparse Core Ops, SparseCore 0:
  9.7 45.4 all-gather.4
  56.7 63.5 all-gather.6
  122.0 117.1 all-gather.10
  240.7 70.4 all-gather.8
  313.3 73.2 reduce-scatter.4
  388.7 133.8 reduce-scatter.6
  525.0 37.2 reduce-scatter.10
  564.6 75.5 reduce-scatter.8

commit v5 on v4

--- a/solution.py
+++ b/solution.py
@@ -216,12 +216,12 @@
         ref[col // LANE + c, rows, :] = value[:, c * LANE : (c + 1) * LANE]
 
 
-def over_tiles(S, L, C, step):
+def over_tiles(S, L, C, step, first=0):
     per = L // TILE
 
     @pl.loop(0, S * per)
     def _(i):
-        for col in range(0, C, BW):
+        for col in range(first, C, BW):
             step(i // per, pl.multiple_of(lax.rem(i, per) * TILE, TILE), col)
 
 
@@ -348,22 +348,27 @@
         value, _ = gelu_parts(xy_ref[q, pl.ds(r0, TILE), pl.ds(C + col, BW)])
         mixed_ref[here, cs] = (st * value).astype(BF)
 
-    over_tiles(S, L, C, finish)
-
-    def drain(j, _):
-        remote(fin_s, got_s.at[t], send_sem.at[j], recv_sem.at[t], "tok", j).wait_send()
-        return 0
-
-    lax.fori_loop(t + 1, T, drain, 0)
     kept = own_ref.shape[1]
     more = C - kept
     handed = remote(
         mixed_ref.at[:, pl.ds(kept, more)], own_ref.at[:, pl.ds(0, more)], pass_send, pass_recv, "seq", flip(me, 1)
     )
+    over_tiles(S, L, C, finish, C - BW)
 
     @pl.when(lax.rem(me, 2) == 0)
     def _():
         handed.start()
+
+    over_tiles(S, L, C - BW, finish)
+
+    def drain(j, _):
+        remote(fin_s, got_s.at[t], send_sem.at[j], recv_sem.at[t], "tok", j).wait_send()
+        return 0
+
+    lax.fori_loop(t + 1, T, drain, 0)
+
+    @pl.when(lax.rem(me, 2) == 0)
+    def _():
         own_ref[...] = mixed_ref[:, 0:kept]
         handed.wait_send()
 

time: 673 us -> 672 us (level)
  transfers between devices with their start and end apart: 12 -> 12, of which waited for: 6 -> 6; matrix products, arithmetic and copies ran while one was open for 29% -> 29% of each run, Pallas kernels for 59% -> 58%
where the time goes in v5:
time: 672 us; the launch traced here: 663 us
  Pallas kernels  388 us (58%)
  matrix products  150 us (22%)
  waiting for transfers between devices  39.1 us (6%)
  other arithmetic  35 us (5%)
  local copies, waits for them, and re-layouts  21 us (3%)
  between operations  16.1 us (2%)
  starting transfers between devices  13.9 us (2%)
    pallas_call x3, Pallas kernels, run_plane(): pl.pallas_call(functools.partial(plane_sum, kind, L, D), out_shape=tuple(...  197 us
    pallas_call x1, Pallas kernels, run_backward(): pl.pallas_call(functools.partial(recur_backward, T, S, L, C), out_shape=(...  64.5 us
    dot_general x5, matrix products, forward_product(): return jnp.dot(left, weight, preferred_element_type=F32)  51.7 us
    dot_general x4, matrix products, back_product(): lax.dot_general(grad, weight, (((2,), (1,)), ((), ())), preferred_element...  50.5 us
    pallas_call x1, Pallas kernels, run_forward(): pl.pallas_call(functools.partial(recur_forward, T, S, L, C), out_shape=(s...  49.5 us
    dot_general x4, matrix products, token_product(): lax.dot_general(left, grad, (((0, 1), (0, 1)), ((), ())), preferred_eleme...  48.2 us
    pallas_call x1, Pallas kernels, run_rows(): pl.pallas_call(functools.partial(plane_rows, S, first.shape[0]), out_shap...  36 us
    pallas_call x1, Pallas kernels, run_fill(): pl.pallas_call(functools.partial(plane_fill, S, T, slabs), out_shape=(sha...  26.4 us
  transfers between devices with their start and end apart: 12, of which 6 were waited for; matrix products, arithmetic and copies ran while one was open for 29% of the time, Pallas kernels for 58%

profile of v5, /device:TPU:0, one launch (start us, length us, event | category | flops | bytes accessed | tf_op | source)
XLA Modules:
  0.0 663.3 jit_solution(893542113649412468)
XLA Ops:
  10.6 1.1 slice_bitcast_fusion.15
  11.8 14.2 %shard_map.314 = (bf16[4,64,1536]{2,1,0:T(8,128)(2,1)}, bf16[4,64,128]{2,1,0:T(8,128)(2,1)S(1)}) custom-call(bf16[4,64,1536]{2,1,0:T(8,128)(2,1)S(1)} %maximum_maximum_fusion.refs_0_, bf16[64,128]{1,0:T(8,128)(2,1)S(1)} %pad.37.refs_1_), custom_call_target="tpu_custom_call" | custom-call | bytes 25559040 | tf_op jit(solution)/shard_map/pallas_call | solution.py:856
  26.9 26.4 %shard_map.315 = (bf16[4,64,3072]{2,1,0:T(8,128)(2,1)}, bf16[8,80,640]{2,1,0:T(8,128)(2,1)S(1)}, bf16[2,80,640]{2,1,0:T(8,128)(2,1)S(1)}) custom-call(bf16[4,64,3072]{2,1,0:T(8,128)(2,1)S(1)} %pad_maximum_fusion.1.refs_0_, bf16[80,640]{1,0:T(8,128)(2,1)S(1)} %fusion.33.refs_1_), custom_call_target="tpu_custom_call" | custom-call | bytes 80000000 | tf_op jit(solution)/shard_map/pallas_call | solution.py:949
  54.2 1.2 compare_select_fusion
  55.4 1.1 copy.101
  56.5 1.2 copy.105
  59.7 36.0 %shard_map.316 = bf16[4,256,2048]{2,1,0:T(8,128)(2,1)S(1)} custom-call(bf16[256,2048]{1,0:T(8,128)(2,1)S(1)} %bitcast.148), custom_call_target="tpu_custom_call" | custom-call | bytes 140000000 | tf_op jit(solution)/shard_map/pallas_call | solution.py:982
  95.8 1.3 collective-permute-start
  98.0 3.1 fusion.2
  101.1 9.0 %collective-permute-done = bf16[128,2048]{1,0:T(8,128)(2,1)S(1)} collective-permute-done((bf16[128,2048]{1,0:T(8,128)(2,1)S(1)}, bf16[128,2048]{1,0:T(8,128)(2,1)S(1)}, u32[]{:S(2)}, u32[]{:S(2)}) %collective-permute-start) | collective-permute-done | bytes 524320 | tf_op jit(solution)/shard_map/ppermute | solution.py:21
  110.1 3.1 fusion.25
  113.2 7.2 %all-gather.7.cloned.1.call-done = bf16[4,512,1536]{2,1,0:T(8,128)(2,1)} async-done(((bf16[4,64,1536]{2,1,0:T(8,128)(2,1)}), bf16[4,512,1536]{2,1,0:T(8,128)(2,1)}) %all-gather.7.cloned.1.call-update) | async-done | bytes 6291472 | tf_op jit(solution)/shard_map/all_gather | solution.py:1039
  120.5 11.9 %fusion.18.xy_ref = f32[4,256,1536]{2,1,0:T(8,128)} fusion(bf16[4,256,2048]{2,1,0:T(8,128)(2,1)} %fusion.2, bf16[2048,1536]{1,0:T(8,128)(2,1)} %bitcast.178), kind=kOutput, calls=%fused_computation.28 | convolution fusion | flops 6442450944 | bytes 16777216 | tf_op jit(solution)/shard_map/dot_general | solution.py:37
  133.7 1.8 multiply_convert_fusion.2.cot_ref
  135.6 49.5 %shard_map.317 = (bf16[1024,768]{1,0:T(8,128)(2,1)}, bf16[1024,640]{1,0:T(8,128)(2,1)}, f32[1024,768]{1,0:T(8,128)}, bf16[4,256,768]{2,1,0:T(8,128)(2,1)}, bf16[...) custom-call(f32[4,256,1536]{2,1,0:T(8,128)} %fusion.18.xy_ref, ...), custom_call_target="tpu_custom_call" | custom-call | flops 805306368 | bytes 100000000 | tf_op jit(solution)/shard_map/pallas_call | solution.py:584
  185.1 5.0 convolution_convert_fusion.1.refs_0_
  190.1 74.8 %shard_map.318 = (f32[256,2048]{1,0:T(8,128)S(1)}, bf16[4,256,2048]{2,1,0:T(8,128)(2,1)S(1)}) custom-call(bf16[4,256,2048]{2,1,0:T(8,128)(2,1)S(1)} %convolution_convert_fusion.1.refs_0_, bf16[256,2048]{1,0:T(8,128)(2,1)S(1)} %bitcast.149, f32[1,2048]{1,0:T(1,128)S(1)} %unstack.12.refs_2_), custom_call_target="tpu_custom_call" | custom-call | flops 20971520 | bytes 20000000 | tf_op jit(solution)/shard_map/pallas_call | solution.py:810
  265.0 2.0 copy-done.5
  267.0 12.0 %fusion.11 = f32[4,256,1536]{2,1,0:T(8,128)} fusion(bf16[4,256,2048]{2,1,0:T(8,128)(2,1)} %copy-done.5, bf16[2048,3072]{1,0:T(8,128)(2,1)} %bitcast.175), kind=kOutput, calls=%fused_computation.20 | convolution fusion | flops 6442450944 | bytes 16777216 | tf_op jit(solution)/shard_map/dot_general | solution.py:37
  278.9 11.5 %multiply_convert_fusion.1 = (bf16[4,256,1536]{2,1,0:T(8,128)(2,1)}, f32[4,256,1536]{2,1,0:T(8,128)}) fusion(f32[4,256,1536]{2,1,0:T(8,128)} %fusion.11, bf16[4,256,2048]{2,1,0:T(8,128)(2,1)S(1)} %copy-done.6, bf16[2048,3072]{1,0:T(8,128)(2,1)S(1)} %bitcast.177), kind=kOutput, calls=%fused_computation.31 | convolution fusion | flops 6458179584 | bytes 26214400 | tf_op jit(solution)/shard_map/dot_general | solution.py:37
  290.5 10.6 %bitcast_convert_fusion.2 = bf16[1536,2048]{1,0:T(8,128)(2,1)} fusion(bf16[4,256,1536]{2,1,0:T(8,128)(2,1)} %get-tuple-element.225, bf16[4,256,2048]{2,1,0:T(8,128)(2,1)S(1)} %copy-done.39), kind=kOutput, calls=%fused_computation.2 | convolution fusion | flops 6445596672 | bytes 13631488 | tf_op jit(solution)/shard_map/dot_general | solution.py:45
  301.5 9.7 %all-gather.9.cloned.1.call-done = bf16[1536,2048]{1,0:T(8,128)(2,1)} async-done(((bf16[192,2048]{1,0:T(8,128)(2,1)}), bf16[1536,2048]{1,0:T(8,128)(2,1)}) %all-gather.9.cloned.1.call-update) | async-done | bytes 6291472 | tf_op jit(solution)/shard_map/all_gather | solution.py:53
  311.2 17.8 %fusion.9 = (bf16[4,256,1536]{2,1,0:T(8,128)(2,1)S(1)}, bf16[4,256,1536]{2,1,0:T(8,128)(2,1)}) fusion(f32[4,256,1536]{2,1,0:T(8,128)} %fusion.11, f32[4,256,1536]{2,1,0:T(8,128)} %get-tuple-element.226, bf16[4,256,2048]{2,1,0:T(8,128)(2,1)} %get-tuple-element.82, bf16[1536,2048]{1,0:T(8,128)(2,1)} %all-gather.9.cloned.1.call-done), kind=kOutput, calls=%fused_computation.16 | convolution fusion | flops 6480199680 | bytes 29360128 | tf_op jit(solution)/shard_map/dot_general | solution.py:41
  329.0 18.9 %bitcast_convert_fusion = bf16[2048,3072]{1,0:T(8,128)(2,1)} fusion(bf16[4,256,2048]{2,1,0:T(8,128)(2,1)S(1)} %copy-done.7, bf16[4,256,1536]{2,1,0:T(8,128)(2,1)} %get-tuple-element.198, bf16[4,256,1536]{2,1,0:T(8,128)(2,1)S(1)} %get-tuple-element.197), kind=kOutput, calls=%fused_computation | convolution fusion | flops 12903776256 | bytes 23068672 | tf_op jit(solution)/shard_map/dot_general | solution.py:45
  348.1 6.3 pad_maximum_fusion
  354.4 17.7 %convolution_convert_fusion.refs_0_ = bf16[4,256,2048]{2,1,0:T(8,128)(2,1)S(1)} fusion(bf16[4,256,3072]{2,1,0:T(8,128)(2,1)} %pad_maximum_fusion, bf16[2048,3072,1]{1,0,2:T(8,128)(2,1)} %bitcast.176), kind=kOutput, calls=%fused_computation.34 | convolution fusion | flops 12886999040 | bytes 23068672 | tf_op jit(solution)/shard_map/dot_general | solution.py:41
  372.8 74.4 %shard_map.319 = (f32[256,2048]{1,0:T(8,128)S(1)}, bf16[4,256,2048]{2,1,0:T(8,128)(2,1)S(1)}) custom-call(bf16[4,256,2048]{2,1,0:T(8,128)(2,1)S(1)} %convolution_convert_fusion.refs_0_, f32[256,2048]{1,0:T(8,128)S(1)} %get-tuple-element.90.refs_1_, f32[1,2048]{1,0:T(1,128)S(1)} %unstack.12.refs_2_, bf16[256,2048]{1,0:T(8,128)(2,1)S(1)} %bitcast.151, ...), custom_call_target="tpu_custom_call" | custom-call | flops 20971520 | bytes 20000000 | tf_op jit(solution)/shard_map/pallas_call | solution.py:810
  447.2 1.3 copy-done.3
  448.5 2.0 copy-done.8
  450.5 7.2 %bitcast_convert_fusion.3 = bf16[640,2048]{1,0:T(8,128)(2,1)} fusion(bf16[4,256,640]{2,1,0:T(8,128)(2,1)} %bitcast.181, bf16[4,256,2048]{2,1,0:T(8,128)(2,1)} %copy-done.8), kind=kOutput, calls=%fused_computation.33 | convolution fusion | flops 2685665280 | bytes 8126464 | tf_op jit(solution)/shard_map/dot_general | solution.py:45
  458.0 11.3 %fusion.20.part_ref = bf16[4,256,2048]{2,1,0:T(8,128)(2,1)} fusion(bf16[4,256,1536]{2,1,0:T(8,128)(2,1)} %get-tuple-element.225, bf16[1536,2048]{1,0:T(8,128)(2,1)} %all-gather.9.cloned.1.call-done), kind=kOutput, calls=%fused_computation.35 | convolution fusion | flops 6444548096 | bytes 13631488 | tf_op jit(solution)/shard_map/dot_general | solution.py:37
  469.3 5.1 fusion.26
  474.4 64.5 %shard_map.320 = (bf16[4,256,1536]{2,1,0:T(8,128)(2,1)}, f32[768,256]{1,0:T(8,128)}, f32[768,256]{1,0:T(8,128)}, f32[8,768]{1,0:T(8,128)}, f32[256,2048]{1,0:T(8,128)}) custom-call(f32[1024,768]{1,0:T(8,128)} %bitcast.161, f32[4,256,1536]{2,1,0:T(8,128)} %fusion.18.xy_ref, f32[1024,768]{1,0:T(8,128)} %get-tuple-element.95.st_ref, ...), custom_call_target="tpu_custom_call" | custom-call | flops 2415919104 | bytes 40000000 | tf_op jit(solution)/shard_map/pallas_call | solution.py:625
  538.9 11.6 %bitcast_convert_fusion.1 = bf16[2048,1536]{1,0:T(8,128)(2,1)} fusion(bf16[4,256,2048]{2,1,0:T(8,128)(2,1)} %fusion.2, bf16[4,256,1536]{2,1,0:T(8,128)(2,1)} %get-tuple-element.104), kind=kOutput, calls=%fused_computation.1 | convolution fusion | flops 6445596672 | bytes 13631488 | tf_op jit(solution)/shard_map/dot_general | solution.py:45
  551.4 2.6 convert_element_type.141
  554.1 2.4 select_maximum_fusion
  556.5 1.3 add_convert_fusion
  557.8 3.7 reduce-scatter.11.cloned.1.call-done
  561.4 1.9 convert_element_type.142
  563.4 1.4 convert_dynamic-update-slice_fusion
  565.8 3.4 collective-permute-start.1
  569.2 4.3 all-to-all-start
  573.5 9.9 %fusion.16.refs_0_ = bf16[4,256,2048]{2,1,0:T(8,128)(2,1)S(1)} fusion(bf16[4,256,1536]{2,1,0:T(8,128)(2,1)} %get-tuple-element.104, bf16[2048,1536]{1,0:T(8,128)(2,1)} %bitcast.179), kind=kOutput, calls=%fused_computation.26 | convolution fusion | flops 6442450944 | bytes 13631488 | tf_op jit(solution)/shard_map/dot_general | solution.py:41
  583.7 48.2 %shard_map.321 = (f32[256,2048]{1,0:T(8,128)S(1)}, f32[80,640]{1,0:T(8,128)S(1)}) custom-call(bf16[4,256,2048]{2,1,0:T(8,128)(2,1)S(1)} %fusion.16.refs_0_, bf16[256,2048]{1,0:T(8,128)(2,1)S(1)} %bitcast.150, f32[1,2048]{1,0:T(1,128)S(1)} %unstack.13.refs_2_, bf16[8,80,640]{2,1,0:T(8,128)(2,1)S(1)} %bitcast.152), custom_call_target="tpu_custom_call" | custom-call | flops 20971520 | bytes 20000000 | tf_op jit(solution)/shard_map/pallas_call | solution.py:810
  631.9 1.7 add.96
  633.6 1.8 convert_bitcast_fusion
  639.4 3.8 all-to-all-start.1
  645.3 7.9 %all-to-all-done.1 = bf16[4,64,1536]{2,1,0:T(8,128)(2,1)S(1)} async-done(((bf16[4,64,1536]{2,1,0:T(8,128)(2,1)}), bf16[4,64,1536]{2,1,0:T(8,128)(2,1)S(1)}, u32[]{:S(2)}, u32[]{:S(2)}) %all-to-all-start.1) | async-done | bytes 786464 | tf_op jit(solution)/shard_map/all_to_all | solution.py:49
  (160 shorter events, 21.7 us)
Async XLA Ops:
  7.2 19.0 %copy-start.19 = (bf16[64,6144]{1,0:T(8,128)(2,1)S(1)}, bf16[64,6144]{1,0:T(8,128)(2,1)}, u32[]{:S(2)}) copy-start(bf16[64,6144]{1,0:T(8,128)(2,1)} %param.35) | copy-start | bytes 2359300
  7.2 19.0 %copy-start.17 = (bf16[64,6144]{1,0:T(8,128)(2,1)S(1)}, bf16[64,6144]{1,0:T(8,128)(2,1)}, u32[]{:S(2)}) copy-start(bf16[64,6144]{1,0:T(8,128)(2,1)} %param.36) | copy-start | bytes 2359300
  7.2 52.5 %all-gather.5.cloned.1.call-start = ((), (), s32[]{:S(2)}) async-start(), calls=%async_computation.6 | async-start | bytes 2949120 | tf_op jit(solution)/shard_map/all_gather | solution.py:53
  7.9 112.4 %all-gather.7.cloned.1.call-start = ((), (), s32[]{:S(2)}) async-start(), calls=%async_computation.7 | async-start | bytes 7077888 | tf_op jit(solution)/shard_map/all_gather | solution.py:1039
  11.8 14.9 %copy-start.30 = (bf16[80,4]{0,1:T(4,128)(2,1)S(1)}, bf16[80,4]{0,1:T(4,128)(2,1)}, u32[]{:S(2)}) copy-start(bf16[80,4]{0,1:T(4,128)(2,1)} %param.26) | copy-start | bytes 1924
  11.8 14.9 %copy-start.31 = (bf16[80]{0:T(256)(128)(2,1)S(1)}, bf16[80]{0:T(256)(128)(2,1)}, u32[]{:S(2)}) copy-start(bf16[80]{0:T(256)(128)(2,1)} %param.27) | copy-start | bytes 484
  11.8 14.9 %copy-start.32 = (bf16[80]{0:T(256)(128)(2,1)S(1)}, bf16[80]{0:T(256)(128)(2,1)}, u32[]{:S(2)}) copy-start(bf16[80]{0:T(256)(128)(2,1)} %param.29) | copy-start | bytes 484
  11.8 14.9 %copy-start.33 = (bf16[80]{0:T(256)(128)(2,1)S(1)}, bf16[80]{0:T(256)(128)(2,1)}, u32[]{:S(2)}) copy-start(bf16[80]{0:T(256)(128)(2,1)} %param.31) | copy-start | bytes 484
  11.8 14.9 %copy-start.34 = (bf16[80]{0:T(256)(128)(2,1)S(1)}, bf16[80]{0:T(256)(128)(2,1)}, u32[]{:S(2)}) copy-start(bf16[80]{0:T(256)(128)(2,1)} %param.32) | copy-start | bytes 484
  11.8 15.1 %copy-start.27 = (bf16[80,256]{1,0:T(8,128)(2,1)S(1)}, bf16[80,256]{1,0:T(8,128)(2,1)}, u32[]{:S(2)}) copy-start(bf16[80,256]{1,0:T(8,128)(2,1)} %param.30) | copy-start | bytes 122884
  11.8 15.0 %copy-start.28 = (bf16[80,256]{1,0:T(8,128)(2,1)S(1)}, bf16[80,256]{1,0:T(8,128)(2,1)}, u32[]{:S(2)}) copy-start(bf16[80,256]{1,0:T(8,128)(2,1)} %param.28) | copy-start | bytes 122884
  26.1 240.8 %all-gather.11.cloned.1.call-start = ((), (), s32[]{:S(2)}) async-start(), calls=%async_computation.9 | async-start | bytes 14155776 | tf_op jit(solution)/shard_map/all_gather | solution.py:1039
  53.3 6.4 copy-start
  57.9 40.0 %copy-start.25 = (f32[1,4,8,64]{3,2,0,1:T(8,128)}, f32[1,4,8,64]{3,2,0,1:T(8,128)S(1)}, u32[]{:S(2)}) copy-start(f32[1,4,8,64]{3,2,0,1:T(8,128)S(1)} %get-tuple-element.224) | copy-start | bytes 24580
  59.7 36.0 %copy-start.14 = (bf16[640,2048]{1,0:T(8,128)(2,1)S(1)}, bf16[640,2048]{1,0:T(8,128)(2,1)}, u32[]{:S(2)}) copy-start(bf16[640,2048]{1,0:T(8,128)(2,1)} %all-gather.5.cloned.1.call-done) | copy-start | bytes 7864324
  95.8 14.3 %collective-permute-start = (bf16[128,2048]{1,0:T(8,128)(2,1)S(1)}, bf16[128,2048]{1,0:T(8,128)(2,1)S(1)}, u32[]{:S(2)}, u32[]{:S(2)}) collective-permute-start(bf16[128,2048]{1,0:T(8,128)(2,1)S(1)} %slice.161), channel_id=1, source_target_pairs={{8,0},{16,8},{24,16},{9,1},{17,9},{25,17},{10,2},{18,10},{26,18},{... | collective-permute-start | bytes 1572872 | tf_op jit(solution)/shard_map/ppermute | solution.py:21
  120.4 12.7 %copy-start.38 = (f32[8]{0:T(128)S(1)}, f32[8]{0:T(128)}, u32[]{:S(2)}) copy-start(f32[8]{0:T(128)} %param.21) | copy-start | bytes 100
  120.4 13.3 %copy-start.1 = (bf16[1,256,2048]{2,1,0:T(8,128)(2,1)S(1)}, bf16[1,256,2048]{2,1,0:T(8,128)(2,1)}, u32[]{:S(2)}) copy-start(bf16[1,256,2048]{2,1,0:T(8,128)(2,1)} %param.22) | copy-start | bytes 3145732
  120.4 190.8 %all-gather.9.cloned.1.call-start = ((), (), s32[]{:S(2)}) async-start(), calls=%async_computation.8 | async-start | bytes 7077888 | tf_op jit(solution)/shard_map/all_gather | solution.py:53
  132.3 318.2 %reduce-scatter.5.cloned.1.call-start = ((), (), s32[]{:S(2)}) async-start(), calls=%async_computation.10 | async-start | bytes 7077888 | tf_op jit(solution)/shard_map/reduce_scatter | solution.py:57
  135.6 49.5 %copy-start.15 = (bf16[768,2048]{1,0:T(8,128)(2,1)S(1)}, bf16[768,2048]{1,0:T(8,128)(2,1)}, u32[]{:S(2)}) copy-start(bf16[768,2048]{1,0:T(8,128)(2,1)} %fusion.25) | copy-start | bytes 9437188
  264.9 2.0 copy-start.5
  266.9 12.0 %copy-start.6 = (bf16[4,256,2048]{2,1,0:T(8,128)(2,1)S(1)}, bf16[4,256,2048]{2,1,0:T(8,128)(2,1)}, u32[]{:S(2)}) copy-start(bf16[4,256,2048]{2,1,0:T(8,128)(2,1)} %copy-done.5) | copy-start | bytes 12582916
  266.9 12.0 %copy-start.37 = (bf16[4,512,3072]{2,1,0:T(8,128)(2,1)S(1)}, bf16[4,512,3072]{2,1,0:T(8,128)(2,1)}, u32[]{:S(2)}) copy-start(bf16[4,512,3072]{2,1,0:T(8,128)(2,1)} %all-gather.11.cloned.1.call-done) | copy-start | bytes 37748740
  278.9 11.6 %copy-start.39 = (bf16[4,256,2048]{2,1,0:T(8,128)(2,1)S(1)}, bf16[4,256,2048]{2,1,0:T(8,128)(2,1)}, u32[]{:S(2)}) copy-start(bf16[4,256,2048]{2,1,0:T(8,128)(2,1)} %get-tuple-element.82) | copy-start | bytes 12582916
  301.1 237.8 %reduce-scatter.7.cloned.1.call-start = ((), (), s32[]{:S(2)}) async-start(), calls=%async_computation.11 | async-start | bytes 14155776 | tf_op jit(solution)/shard_map/reduce_scatter | solution.py:1042
  311.2 17.8 %copy-start.7 = (bf16[4,256,2048]{2,1,0:T(8,128)(2,1)S(1)}, bf16[4,256,2048]{2,1,0:T(8,128)(2,1)}, u32[]{:S(2)}) copy-start(bf16[4,256,2048]{2,1,0:T(8,128)(2,1)} %copy-done.5) | copy-start | bytes 12582916
  329.0 18.9 %copy-start.21 = (bf16[4,256,1536]{2,1,0:T(8,128)(2,1)}, bf16[4,256,1536]{2,1,0:T(8,128)(2,1)S(1)}, u32[]{:S(2)}) copy-start(bf16[4,256,1536]{2,1,0:T(8,128)(2,1)S(1)} %get-tuple-element.197) | copy-start | bytes 9437188
  347.9 213.5 %reduce-scatter.11.cloned.1.call-start = ((), (), s32[]{:S(2)}) async-start(), calls=%async_computation.13 | async-start | bytes 2949120 | tf_op jit(solution)/shard_map/reduce_scatter | solution.py:57
  354.4 18.4 %copy-start.2 = (bf16[1,256,2048]{2,1,0:T(8,128)(2,1)S(1)}, bf16[1,256,2048]{2,1,0:T(8,128)(2,1)}, u32[]{:S(2)}) copy-start(bf16[1,256,2048]{2,1,0:T(8,128)(2,1)} %param.22) | copy-start | bytes 3145732
  447.2 1.3 copy-start.3
  448.5 2.0 copy-start.8
  457.7 181.7 %reduce-scatter.9.cloned.1.call-start = ((), (), s32[]{:S(2)}) async-start(), calls=%async_computation.12 | async-start | bytes 7077888 | tf_op jit(solution)/shard_map/reduce_scatter | solution.py:1042
  458.0 11.3 %copy-start.9 = (bf16[4,256,2048]{2,1,0:T(8,128)(2,1)S(1)}, bf16[4,256,2048]{2,1,0:T(8,128)(2,1)}, u32[]{:S(2)}) copy-start(bf16[4,256,2048]{2,1,0:T(8,128)(2,1)} %copy-done.8) | copy-start | bytes 12582916
  458.0 11.3 %copy-start.16 = (bf16[768,2048]{1,0:T(8,128)(2,1)S(1)}, bf16[768,2048]{1,0:T(8,128)(2,1)}, u32[]{:S(2)}) copy-start(bf16[768,2048]{1,0:T(8,128)(2,1)} %fusion.25) | copy-start | bytes 9437188
  551.4 5.1 copy-start.22
  565.8 17.7 %collective-permute-start.1 = (bf16[128,640]{1,0:T(8,128)(2,1)S(1)}, bf16[128,640]{1,0:T(8,128)(2,1)S(1)}, u32[]{:S(2)}, u32[]{:S(2)}) collective-permute-start(bf16[128,640]{1,0:T(8,128)(2,1)S(1)} %slice.164), channel_id=1, source_target_pairs={{0,8},{8,16},{16,24},{1,9},{9,17},{17,25},{2,10},{10,18},{18,26},{... | collective-permute-start | bytes 491528 | tf_op jit(solution)/shard_map/ppermute | solution.py:21
  569.2 64.4 %all-to-all-start = ((bf16[4,64,3072]{2,1,0:T(8,128)(2,1)}), bf16[4,64,3072]{2,1,0:T(8,128)(2,1)}, u32[]{:S(2)}, u32[]{:S(2)}) async-start(bf16[4,64,3072]{2,1,0:T(8,128)(2,1)} %reduce-scatter.7.cloned.1.call-done), calls=%async_computation.4 | async-start | bytes 3145728 | tf_op jit(solution)/shard_map/all_to_all | solution.py:49
  573.5 9.9 %copy-start.13 = (bf16[896,640]{1,0:T(8,128)(2,1)S(1)}, bf16[896,640]{1,0:T(8,128)(2,1)}, u32[]{:S(2)}) copy-start(bf16[896,640]{1,0:T(8,128)(2,1)} %copy-done.12) | copy-start | bytes 3440644
  583.4 48.4 %copy-start.4 = (f32[256,2048]{1,0:T(8,128)S(1)}, f32[256,2048]{1,0:T(8,128)}, u32[]{:S(2)}) copy-start(f32[256,2048]{1,0:T(8,128)} %copy-done.3) | copy-start | bytes 6291460
  635.6 1.3 copy-start.18
  635.6 2.1 copy-start.20
  635.8 3.7 copy-start.10
  635.8 2.2 copy-start.35
  637.7 15.8 %copy-start.23 = (bf16[64,2560]{1,0:T(8,128)(2,1)S(1)}, bf16[64,2560]{1,0:T(8,128)(2,1)}, u32[]{:S(2)}) copy-start(bf16[64,2560]{1,0:T(8,128)(2,1)} %param.25) | copy-start | bytes 983044
  639.4 15.1 %copy-start.24 = (bf16[64,2560]{1,0:T(8,128)(2,1)S(1)}, bf16[64,2560]{1,0:T(8,128)(2,1)}, u32[]{:S(2)}) copy-start(bf16[64,2560]{1,0:T(8,128)(2,1)} %param.24) | copy-start | bytes 983044
  639.4 13.8 %all-to-all-start.1 = ((bf16[4,64,1536]{2,1,0:T(8,128)(2,1)}), bf16[4,64,1536]{2,1,0:T(8,128)(2,1)S(1)}, u32[]{:S(2)}, u32[]{:S(2)}) async-start(bf16[4,64,1536]{2,1,0:T(8,128)(2,1)} %reduce-scatter.9.cloned.1.call-done), calls=%async_computation.5 | async-start | bytes 1572864 | tf_op jit(solution)/shard_map/all_to_all | solution.py:49
  645.3 10.2 %copy-start.36 = (bf16[64]{0:T(256)(128)(2,1)S(1)}, bf16[64]{0:T(256)(128)(2,1)}, u32[]{:S(2)}) copy-start(bf16[64]{0:T(256)(128)(2,1)} %param.23) | copy-start | bytes 388
  (4 other events, 3.8 us)
Sparse Core Ops, SparseCore 0:
  9.7 45.4 all-gather.4
  56.7 63.5 all-gather.6
  122.0 117.1 all-gather.10
  240.7 70.4 all-gather.8
  313.3 72.3 reduce-scatter.4
  387.9 133.8 reduce-scatter.6
  524.1 37.2 reduce-scatter.10
  563.7 75.6 reduce-scatter.8
